TPU v7x, 32 devices: a whole 2x2x4 slice. The times are simulated.
32 devices in a mesh: row: 4 (over x, core), col: 8 (over z, y).
Axes of the slice: x: 2, y: 2, z: 4, core: 2. Of those that a mesh axis runs over, the one named last changes fastest.
Arguments:
- vectors: float32 [2048, 2048], P('row', 'col'), may hold values from -6 to 6
- reflectors: float32 [4, 2048, 256], P(None, ('row', 'col')), may hold values from -6 to 6
- owner_list: int32 [16], replicated, may hold values from 0 to 7, as said below
- slot_list: int32 [16], replicated, may hold values from 0 to 1
Outputs:
- result: float32 [2048, 2048], P('row', 'col')
Inputs may be any that keep to these rules, and one draw needn't show every extreme that they name: owner_list * 2 + slot_list takes each value 0 to 15 exactly once.
All inputs are finite; a program needn't handle non-finite values.
Results may differ from a plain program's by a relative error of at most 0.0001.
Values sent between devices are 32-bit elements; how exact they have to be, the bound alone decides.
No kernel may reach another device: no remote copies, remote signals or barrier semaphores. Data moves between devices by JAX's collectives and lax.ppermute only.
A program may use at most 64 MiB of HBM per device.

v0:
```python
import jax
import jax.numpy as jnp
from jax import lax
from jax.sharding import PartitionSpec as P

BW = 128
BLK_DEV = 2
PANELS = 4


def matmul(left, right):
    return jnp.dot(left, right, precision=lax.Precision.HIGHEST, preferred_element_type=jnp.float32)


def upper_inverse(upper):
    order = upper.shape[0]
    if order <= 16:
        diag_vals = jnp.diagonal(upper)
        nilpotent = -(jnp.triu(upper, 1) / diag_vals[:, None])
        accum = jnp.eye(order, dtype=jnp.float32) + nilpotent
        power = nilpotent
        for _ in range(max((order - 1).bit_length() - 1, 0)):
            power = matmul(power, power)
            accum = accum + matmul(accum, power)
        return accum * (1.0 / diag_vals)[None, :]
    half = order // 2
    first_inv = upper_inverse(upper[:half, :half])
    second_inv = upper_inverse(upper[half:, half:])
    corner = -matmul(matmul(first_inv, upper[:half, half:]), second_inv)
    top_part = jnp.concatenate([first_inv, corner], axis=1)
    low_part = jnp.concatenate([jnp.zeros((order - half, half), jnp.float32), second_inv], axis=1)
    return jnp.concatenate([top_part, low_part], axis=0)


def resort(slab_now, owner_list, slot_list):
    spread = lax.all_to_all(slab_now, "col", split_axis=0, concat_axis=1, tiled=True)
    blocks = owner_list.shape[0]
    target = owner_list * BLK_DEV + slot_list
    positions = jnp.arange(blocks, dtype=jnp.int32)
    one_hot = (target[:, None] == positions[None, :]).astype(jnp.float32)
    blocks_view = spread.reshape(spread.shape[0], blocks, BW)
    ordered = jnp.einsum(
        "rbw,bc->rcw",
        blocks_view,
        one_hot,
        precision=lax.Precision.HIGHEST,
        preferred_element_type=jnp.float32,
    )
    ordered = ordered.reshape(spread.shape[0], blocks * BW)
    return lax.all_to_all(ordered, "col", split_axis=1, concat_axis=0, tiled=True)


def update_slab(slab_now, panel_rows, gram_sum, product):
    upper_form = jnp.triu(gram_sum, 1) + jnp.diag(jnp.diagonal(gram_sum) * 0.5)
    coefficients = matmul(upper_inverse(upper_form), product)
    return slab_now - matmul(panel_rows, coefficients)


def on_device(vectors, reflectors, owner_list, slot_list):
    gathered = lax.all_gather(reflectors, "col", axis=1, tiled=True)
    slab_now = vectors
    slab_now = resort(slab_now, owner_list, slot_list)
    for panel_index in reversed(range(PANELS)):
        panel_rows = gathered[panel_index]
        local_product = matmul(panel_rows.T, slab_now)
        local_gram = matmul(panel_rows.T, panel_rows)
        gram_sum, product = lax.psum((local_gram, local_product), "row")
        slab_now = update_slab(slab_now, panel_rows, gram_sum, product)
    return slab_now


def solution(mesh):
    return jax.shard_map(
        on_device,
        mesh=mesh,
        in_specs=(P("row", "col"), P(None, ("row", "col"), None), P(), P()),
        out_specs=P("row", "col"),
        check_vma=False,
    )
```

profile of v0, /device:TPU:0, one launch (start us, length us, event | category | flops | bytes accessed | tf_op | source)
XLA Modules:
  0.0 471.0 jit_solution(6222561898858705004)
XLA Ops:
  7.3 7.3 %all-to-all-start = ((f32[8,64,256]{2,1,0:T(8,128)}), f32[8,64,256]{2,1,0:T(8,128)S(1)}, u32[]{:S(2)}, u32[]{:S(2)}) async-start(f32[8,64,256]{2,1,0:T(8,128)} %bitcast.805), calls=%async_computation | async-start | bytes 1048576 | tf_op jit(solution)/shard_map/all_to_all | solution.py:36
  15.2 20.9 %all-to-all-done = f32[8,64,256]{2,1,0:T(8,128)S(1)} async-done(((f32[8,64,256]{2,1,0:T(8,128)}), f32[8,64,256]{2,1,0:T(8,128)S(1)}, u32[]{:S(2)}, u32[]{:S(2)}) %all-to-all-start) | async-done | bytes 524320 | tf_op jit(solution)/shard_map/all_to_all | solution.py:36
  38.0 3.5 all-to-all-start.1
  41.6 31.0 %all-gather.2.cloned.1.call-done = f32[4,512,256]{2,1,0:T(8,128)} async-done(((f32[4,64,256]{2,1,0:T(8,128)}), f32[4,512,256]{2,1,0:T(8,128)}) %all-gather.2.cloned.1.call-update) | async-done | bytes 2097168 | tf_op jit(solution)/shard_map/all_gather | solution.py:60
  72.5 3.1 fusion.68
  75.6 2.8 convolution_bitcast_fusion.8
  79.2 1.7 fusion.69
  81.0 29.8 %all-reduce.75.cloned.1.call-done = (f32[256,256]{0,1:T(8,128)}, f32[256,256]{1,0:T(8,128)}) async-done(((f32[256,256]{0,1:T(8,128)}, f32[256,256]{1,0:T(8,128)}), (f32[256,256]{0,1:T(8,128)}, f32[256,256]{1,0:T(8,128)})) %all-reduce.75.cloned.1.call-update) | async-done | bytes 524304 | tf_op jit(solution)/shard_map/psum | solution.py:67
  110.8 2.6 gather_fusion
  113.4 1.1 select_add_fusion.3
  115.2 1.0 fusion.519
  171.6 1.1 fusion
  172.7 1.3 convolution_bitcast_fusion.7
  174.2 1.7 fusion.70
  176.0 31.6 %all-reduce.73.cloned.1.call-done = (f32[256,256]{0,1:T(8,128)}, f32[256,256]{1,0:T(8,128)}) async-done(((f32[256,256]{0,1:T(8,128)}, f32[256,256]{1,0:T(8,128)}), (f32[256,256]{0,1:T(8,128)}, f32[256,256]{1,0:T(8,128)})) %all-reduce.73.cloned.1.call-update) | async-done | bytes 524304 | tf_op jit(solution)/shard_map/psum | solution.py:67
  207.5 2.6 gather_fusion.17
  210.1 1.1 select_add_fusion.2
  211.9 1.0 fusion.535
  268.4 1.1 fusion.1
  269.4 1.3 convolution_bitcast_fusion.6
  271.0 1.7 fusion.71
  272.8 31.5 %all-reduce.71.cloned.1.call-done = (f32[256,256]{0,1:T(8,128)}, f32[256,256]{1,0:T(8,128)}) async-done(((f32[256,256]{0,1:T(8,128)}, f32[256,256]{1,0:T(8,128)}), (f32[256,256]{0,1:T(8,128)}, f32[256,256]{1,0:T(8,128)})) %all-reduce.71.cloned.1.call-update) | async-done | bytes 524304 | tf_op jit(solution)/shard_map/psum | solution.py:67
  304.3 2.6 gather_fusion.34
  306.8 1.1 select_add_fusion.1
  308.7 1.0 fusion.551
  365.1 1.1 fusion.2
  366.2 1.3 convolution_bitcast_fusion.5
  367.5 33.5 %all-reduce.69.cloned.1.call-done = (f32[256,256]{0,1:T(8,128)}, f32[256,256]{1,0:T(8,128)}) async-done(((f32[256,256]{0,1:T(8,128)}, f32[256,256]{1,0:T(8,128)}), (f32[256,256]{0,1:T(8,128)}, f32[256,256]{1,0:T(8,128)})) %all-reduce.69.cloned.1.call-update) | async-done | bytes 524304 | tf_op jit(solution)/shard_map/psum | solution.py:67
  401.0 2.6 gather_fusion.51
  403.6 1.1 select_add_fusion
  462.1 1.1 fusion.3
  463.2 1.0 copy.19
  (743 shorter events, 229.7 us)
Async XLA Ops:
  6.5 66.0 %all-gather.2.cloned.1.call-start = ((), (), s32[]{:S(2)}) async-start(), calls=%async_computation.2 | async-start | bytes 2359296 | tf_op jit(solution)/shard_map/all_gather | solution.py:60
  7.3 28.9 %all-to-all-start = ((f32[8,64,256]{2,1,0:T(8,128)}), f32[8,64,256]{2,1,0:T(8,128)S(1)}, u32[]{:S(2)}, u32[]{:S(2)}) async-start(f32[8,64,256]{2,1,0:T(8,128)} %bitcast.805), calls=%async_computation | async-start | bytes 1048576 | tf_op jit(solution)/shard_map/all_to_all | solution.py:36
  38.0 37.6 %all-to-all-start.1 = ((f32[64,8,256]{2,0,1:T(8,128)}), f32[64,8,256]{2,0,1:T(8,128)S(1)}, u32[]{:S(2)}, u32[]{:S(2)}) async-start(f32[64,8,256]{2,0,1:T(8,128)} %copy.13), calls=%async_computation.1 | async-start | bytes 1048576 | tf_op jit(solution)/shard_map/all_to_all | solution.py:50
  41.5 69.3 %all-reduce.75.cloned.1.call-start = ((), (), s32[]{:S(2)}) async-start(), calls=%async_computation.6 | async-start | bytes 1048576 | tf_op jit(solution)/shard_map/psum | solution.py:67
  72.5 6.7 %copy-start = (f32[4,512,256]{2,1,0:T(8,128)S(1)}, f32[4,512,256]{2,1,0:T(8,128)}, u32[]{:S(2)}) copy-start(f32[4,512,256]{2,1,0:T(8,128)} %all-gather.2.cloned.1.call-done) | copy-start | bytes 6291460
  78.4 129.1 %all-reduce.73.cloned.1.call-start = ((), (), s32[]{:S(2)}) async-start(), calls=%async_computation.5 | async-start | bytes 1048576 | tf_op jit(solution)/shard_map/psum | solution.py:67
  114.4 0.8 copy-start.3
  141.6 16.7 %copy-start.4 = (f32[256,256]{1,0:T(8,128)S(1)}, f32[256,256]{1,0:T(8,128)}, u32[]{:S(2)}) copy-start(f32[256,256]{1,0:T(8,128)} %copy-done.3) | copy-start | bytes 786436
  155.1 16.1 %copy-start.9 = (f32[256,256]{0,1:T(8,128)S(1)}, f32[256,256]{0,1:T(8,128)}, u32[]{:S(2)}) copy-start(f32[256,256]{0,1:T(8,128)} %get-tuple-element.11) | copy-start | bytes 786436
  174.0 130.2 %all-reduce.71.cloned.1.call-start = ((), (), s32[]{:S(2)}) async-start(), calls=%async_computation.4 | async-start | bytes 1048576 | tf_op jit(solution)/shard_map/psum | solution.py:67
  211.2 0.8 copy-start.5
  238.3 16.7 %copy-start.6 = (f32[256,256]{1,0:T(8,128)S(1)}, f32[256,256]{1,0:T(8,128)}, u32[]{:S(2)}) copy-start(f32[256,256]{1,0:T(8,128)} %copy-done.5) | copy-start | bytes 786436
  251.8 16.1 %copy-start.10 = (f32[256,256]{0,1:T(8,128)S(1)}, f32[256,256]{0,1:T(8,128)}, u32[]{:S(2)}) copy-start(f32[256,256]{0,1:T(8,128)} %get-tuple-element.9) | copy-start | bytes 786436
  270.8 130.3 %all-reduce.69.cloned.1.call-start = ((), (), s32[]{:S(2)}) async-start(), calls=%async_computation.3 | async-start | bytes 1048576 | tf_op jit(solution)/shard_map/psum | solution.py:67
  307.9 0.8 copy-start.7
  335.1 16.7 %copy-start.8 = (f32[256,256]{1,0:T(8,128)S(1)}, f32[256,256]{1,0:T(8,128)}, u32[]{:S(2)}) copy-start(f32[256,256]{1,0:T(8,128)} %copy-done.7) | copy-start | bytes 786436
  348.6 16.1 %copy-start.11 = (f32[256,256]{0,1:T(8,128)S(1)}, f32[256,256]{0,1:T(8,128)}, u32[]{:S(2)}) copy-start(f32[256,256]{0,1:T(8,128)} %get-tuple-element.7) | copy-start | bytes 786436
  404.7 0.8 copy-start.1
  432.0 16.7 %copy-start.2 = (f32[256,256]{1,0:T(8,128)S(1)}, f32[256,256]{1,0:T(8,128)}, u32[]{:S(2)}) copy-start(f32[256,256]{1,0:T(8,128)} %copy-done.1) | copy-start | bytes 786436
  445.6 16.1 %copy-start.12 = (f32[256,256]{0,1:T(8,128)S(1)}, f32[256,256]{0,1:T(8,128)}, u32[]{:S(2)}) copy-start(f32[256,256]{0,1:T(8,128)} %get-tuple-element.5) | copy-start | bytes 786436
Sparse Core Ops, SparseCore 0:
  9.5 62.9 all-gather.1
  78.6 32.1 all-reduce.74
  174.1 33.3 all-reduce.72
  270.9 33.3 all-reduce.70
  367.6 33.3 all-reduce.68
where the time goes:
time: 480 us; the launch traced here: 471 us
  matrix products  199 us (41%)
  waiting for transfers between devices  179 us (37%)
  local copies, waits for them, and re-layouts  59 us (12%)
  between operations  14.5 us (3%)
  starting transfers between devices  11.9 us (2%)
  other arithmetic  7.52 us (2%)
    dot_general x520, matrix products, matmul(): jnp.dot(left, right, precision=lax.Precision.HIGHEST, preferred_element_t...  199 us
    psum x4, waiting for transfers between devices, on_device(): gram_sum, product = lax.psum((local_gram, local_product), 'row')  126 us
    gather x64, local copies, waits for them, and re-layouts, upper_inverse(): diag_vals = jnp.diagonal(upper)  43.3 us
    all_gather x1, waiting for transfers between devices, on_device(): gathered = lax.all_gather(reflectors, 'col', axis=1, tiled=True)  31 us
    all_to_all x1, waiting for transfers between devices, resort(): lax.all_to_all(slab_now, 'col', split_axis=0, concat_axis=1, tiled=True)  20.9 us
    gather x4, local copies, waits for them, and re-layouts, update_slab(): upper_form = jnp.triu(gram_sum, 1) + jnp.diag(jnp.diagonal(gram_sum) * 0.5)  10.3 us
  transfers between devices with their start and end apart: 7, of which 6 were waited for; matrix products, arithmetic and copies ran while one was open for 2% of the time, Pallas kernels for 0%

commit v1 on v0

v1 whole, which is shorter than its diff:
```python
import functools

import jax
import jax.numpy as jnp
from jax import lax
from jax.experimental import pallas as pl
from jax.experimental.pallas import tpu as pltpu
from jax.sharding import PartitionSpec as P

BW = 128
BLK_DEV = 2
LOW = 8
F32, BF16 = jnp.float32, jnp.bfloat16
PARAMS = pltpu.CompilerParams(vmem_limit_bytes=48 * 1024 * 1024)


def vmem(count):
    return [pl.BlockSpec(memory_space=pltpu.VMEM)] * count


def smem(count):
    return [pl.BlockSpec(memory_space=pltpu.SMEM)] * count


def halves(value):
    high = value.astype(BF16)
    return high, (value - high.astype(F32)).astype(BF16)


def dot(left, right):
    return jnp.dot(left, right, preferred_element_type=F32)


def dot3(left, right):
    return dot(left[0], right[0]) + (dot(left[0], right[1]) + dot(left[1], right[0]))


def pairs_of(panels):
    return [(p, q) for p in range(panels) for q in range(p + 1, panels)]


def reorder_kernel(half, owner, slot, spread, ordered):
    def move(block, carry):
        place = slot[block] * half + owner[block]
        parity = block % BLK_DEV

        @pl.when(parity == 0)
        def _():
            ordered[place] = spread[block // BLK_DEV, :, :BW]

        @pl.when(parity == 1)
        def _():
            ordered[place] = spread[block // BLK_DEV, :, BW:]

        return carry

    lax.fori_loop(0, ordered.shape[0], move, 0)


def reorder(spread, owner_list, slot_list):
    cols, rows, _ = spread.shape
    return pl.pallas_call(
        functools.partial(reorder_kernel, cols),
        out_shape=jax.ShapeDtypeStruct((cols * BLK_DEV, rows, BW), F32),
        in_specs=smem(2) + vmem(1),
        out_specs=vmem(1)[0],
        compiler_params=PARAMS,
        name="reorder",
    )(owner_list, slot_list, spread)


def gram_kernel(count, has_before, *refs):
    pieces, refs = refs[:count], refs[count:]
    if has_before:
        (diag_before, corner_before), refs = refs[:2], refs[2:]
    high, low, high_t, low_t, diag, corner = refs
    panels, rows, width = pieces[0].shape
    for at, piece in enumerate(pieces):
        for p in range(panels):
            top, rest = halves(piece[p])
            high[at * rows:(at + 1) * rows, p * width:(p + 1) * width] = top
            low[at * rows:(at + 1) * rows, p * width:(p + 1) * width] = rest
    for p in range(panels):
        cut = slice(p * width, (p + 1) * width)
        high_t[cut, :] = high[:, cut].T
        low_t[cut, :] = low[:, cut].T

    def product(p, q):
        left, right = slice(p * width, (p + 1) * width), slice(q * width, (q + 1) * width)
        return dot3((high_t[left, :], low_t[left, :]), (high[:, right], low[:, right]))

    for p in range(panels):
        value = product(p, p)
        diag[p] = value + diag_before[p] if has_before else value
    for at, (p, q) in enumerate(pairs_of(panels)):
        value = product(p, q)
        corner[at] = value + corner_before[at] if has_before else value


def gram(pieces, before):
    panels, rows, width = pieces[0].shape
    count, full = len(pieces), panels * width
    total = count * rows
    corners = len(pairs_of(panels))
    inputs = list(pieces) + list(before or ())
    return pl.pallas_call(
        functools.partial(gram_kernel, count, before is not None),
        out_shape=(
            jax.ShapeDtypeStruct((total, full), BF16),
            jax.ShapeDtypeStruct((total, full), BF16),
            jax.ShapeDtypeStruct((full, total), BF16),
            jax.ShapeDtypeStruct((full, total), BF16),
            jax.ShapeDtypeStruct((panels, width, width), F32),
            jax.ShapeDtypeStruct((corners, width, width), F32),
        ),
        in_specs=vmem(len(inputs)),
        out_specs=tuple(vmem(6)),
        compiler_params=PARAMS,
        cost_estimate=pl.CostEstimate(
            flops=6 * (panels + corners) * width * width * total, bytes_accessed=16 * total * full, transcendentals=0
        ),
        name="gram",
    )(*inputs)


def invert_kernel(own, other, inverse):
    panels, order, _ = own.shape
    row = lax.broadcasted_iota(jnp.int32, (order, order), 0)
    col = lax.broadcasted_iota(jnp.int32, (order, order), 1)
    on_diag, upper = row == col, row < col
    identity = jnp.where(on_diag, 1.0, 0.0).astype(F32)
    strict, scale = [], []
    for p in range(panels):
        gram_sum = own[p] + other[p]
        half = jnp.where(on_diag, 0.5 * gram_sum, 0.0)
        by_row = 1.0 / jnp.sum(half, axis=1, keepdims=True)
        by_col = 1.0 / jnp.sum(half, axis=0, keepdims=True)
        strict.append(jnp.where(upper, gram_sum * by_row, 0.0))
        scale.append(by_col)

    def multiply(left, right):
        return dot3(halves(left), halves(right))

    size = 16
    same = (row // size) == (col // size)
    power = [jnp.where(same, -value, 0.0) for value in strict]
    accum = [identity + value for value in power]
    for _ in range(3):
        power = [multiply(value, value) for value in power]
        accum = [value + multiply(value, extra) for value, extra in zip(accum, power)]
    while size < order:
        wider = (row // (2 * size)) == (col // (2 * size))
        mask = jnp.logical_and(wider, jnp.logical_not((row // size) == (col // size)))
        part = [multiply(value, jnp.where(mask, edge, 0.0)) for value, edge in zip(accum, strict)]
        accum = [value - multiply(edge, value) for value, edge in zip(accum, part)]
        size *= 2
    for p in range(panels):
        inverse[p] = accum[p] * scale[p]


def invert(own, other):
    return pl.pallas_call(
        invert_kernel,
        out_shape=jax.ShapeDtypeStruct(own.shape, F32),
        in_specs=vmem(2),
        out_specs=vmem(1)[0],
        compiler_params=PARAMS,
        cost_estimate=pl.CostEstimate(flops=10**10, bytes_accessed=own.size * 12, transcendentals=0),
        name="invert",
    )(own, other)


def place_of(at, inner):
    row, col = lax.axis_index("row"), lax.axis_index("col")
    group, z = at // 4, at % 4
    outer, low = row // inner, col % LOW
    odd = (row % inner) % 2
    first, second = group & 1, group >> 1
    by_y = jnp.where(odd == 0, first, second)
    by_x = jnp.where(odd == 0, second, first)
    return jnp.bitwise_xor(outer, by_x), jnp.bitwise_xor(low, z * 2 + by_y), by_x


def project_kernel(inner, high_a, low_a, high_b, low_b, slab, product, slab_high, slab_low):
    rows = slab.shape[1]
    for at in range(2 * LOW):
        outer, low, _ = place_of(at, inner)
        high, rest = halves(slab[outer * LOW + low])
        cut = slice(at * rows, (at + 1) * rows)
        slab_high[cut, :BW] = high
        slab_high[cut, BW:] = rest
        slab_low[cut, :] = high
    middle = LOW * rows
    wide = dot(high_a[...], slab_high[:middle, :]) + dot(high_b[...], slab_high[middle:, :])
    narrow = dot(low_a[...], slab_low[:middle, :]) + dot(low_b[...], slab_low[middle:, :])
    product[...] = wide[:, :BW] + (wide[:, BW:] + narrow)


def project(inner, transposed, slab):
    full = transposed[0].shape[0]
    total = slab.shape[0] * slab.shape[1]
    return pl.pallas_call(
        functools.partial(project_kernel, inner),
        out_shape=jax.ShapeDtypeStruct((full, BW), F32),
        in_specs=vmem(5),
        out_specs=vmem(1)[0],
        scratch_shapes=[pltpu.VMEM((total, 2 * BW), BF16), pltpu.VMEM((total, BW), BF16)],
        compiler_params=PARAMS,
        cost_estimate=pl.CostEstimate(flops=8 * full * total * BW, bytes_accessed=4 * total * full, transcendentals=0),
        name="project",
    )(*transposed, slab)


def update_kernel(inner, own, other, inverse, corner_own, corner_other, high_a, low_a, high_b, low_b, slab, result, solved_wide, solved_high):
    panels, width, _ = inverse.shape
    rows = slab.shape[1]
    pairs = pairs_of(panels)
    solved = [None] * panels
    for p in reversed(range(panels)):
        cut = slice(p * width, (p + 1) * width)
        value = own[cut, :] + other[cut, :]
        for at, (i, q) in enumerate(pairs):
            if i == p:
                value = value - dot3(halves(corner_own[at] + corner_other[at]), solved[q])
        value = dot3(halves(inverse[p]), halves(value))
        solved[p] = halves(value)
        solved_wide[cut, :BW] = solved[p][0]
        solved_wide[cut, BW:] = solved[p][1]
        solved_high[cut, :] = solved[p][0]
    for part, (high, low) in enumerate(((high_a, low_a), (high_b, low_b))):
        wide = dot(high[...], solved_wide[...])
        change = wide[:, :BW] + (wide[:, BW:] + dot(low[...], solved_high[...]))
        for at in range(LOW):
            outer, low_at, away = place_of(part * LOW + at, inner)
            result[away, low_at] = slab[outer * LOW + low_at] - change[at * rows:(at + 1) * rows, :]


def update(inner, own, other, inverse, corner_own, corner_other, straight, slab):
    full = own.shape[0]
    return pl.pallas_call(
        functools.partial(update_kernel, inner),
        out_shape=jax.ShapeDtypeStruct((2, LOW) + slab.shape[1:], F32),
        in_specs=vmem(10),
        out_specs=vmem(1)[0],
        scratch_shapes=[pltpu.VMEM((full, 2 * BW), BF16), pltpu.VMEM((full, BW), BF16)],
        compiler_params=PARAMS,
        name="update",
    )(own, other, inverse, corner_own, corner_other, *straight, slab)


def on_device(rows, cols, vectors, reflectors, owner_list, slot_list):
    inner = rows // 2
    extra = cols // LOW
    local_rows = vectors.shape[0] // cols

    def at(row, col):
        return row * cols + col

    def send(value, change):
        perm = [(at(r, c), at(*change(r, c))) for r in range(rows) for c in range(cols)]
        return lax.ppermute(value, ("row", "col"), perm)

    def by_z(step):
        return lambda r, c: (r, c ^ (2 * step))

    def by_first(r, c):
        return (r, c ^ 1) if (r % inner) % 2 == 0 else ((r + inner) % rows, c)

    def by_second(r, c):
        return (r, c ^ 1) if (r % inner) % 2 == 1 else ((r + inner) % rows, c)

    own = reflectors
    if extra > 1:
        groups = [[e * LOW + low for e in range(extra)] for low in range(LOW)]
        own = lax.all_gather(own, "col", axis=1, tiled=True, axis_index_groups=groups)
    start = [own] + [send(own, by_z(step)) for step in (1, 2, 3)]
    spread = lax.all_to_all(vectors.reshape(cols, local_rows, -1), "col", split_axis=0, concat_axis=0, tiled=True)
    first = [send(piece, by_first) for piece in start]
    second = [send(piece, by_second) for piece in start + first]

    ordered = reorder(spread, owner_list, slot_list)
    groups = [[at(o * inner + i, c) for o in range(2) for c in range(cols)] for i in range(inner)]
    slab = lax.all_to_all(ordered, ("row", "col"), split_axis=0, concat_axis=0, tiled=True, axis_index_groups=groups)
    slab = slab.reshape(2, extra, LOW, local_rows, BW).transpose(0, 2, 1, 3, 4)
    slab = slab.reshape(2 * LOW, extra * local_rows, BW)

    high_a, low_a, high_at, low_at, diag, corner = gram(start + first, None)
    high_b, low_b, high_bt, low_bt, diag, corner = gram(second, (diag, corner))
    product = project(inner, (high_at, low_at, high_bt, low_bt), slab)

    def over_inner(value, bit):
        return send(value, lambda r, c: (r ^ bit, c))

    bit = 1
    while 2 * bit < inner:
        diag, corner, product = (value + over_inner(value, bit) for value in (diag, corner, product))
        bit *= 2
    inverse = invert(diag, over_inner(diag, bit))
    result = update(
        inner, product, over_inner(product, bit), inverse, corner, over_inner(corner, bit), (high_a, low_a, high_b, low_b), slab
    )

    keep, away = result[0], result[1]
    back = send(away, lambda r, c: ((r + inner) % rows, c))
    outer = lax.axis_index("row") // inner

    def natural(value):
        return value.reshape(LOW, extra, local_rows, BW).transpose(1, 0, 2, 3).reshape(vectors.shape[0], BW)

    keep, back = natural(keep), natural(back)
    is_first = outer == 0
    return jnp.concatenate([jnp.where(is_first, keep, back), jnp.where(is_first, back, keep)], axis=1)


def solution(mesh):
    return jax.shard_map(
        functools.partial(on_device, mesh.shape["row"], mesh.shape["col"]),
        mesh=mesh,
        in_specs=(P("row", "col"), P(None, ("row", "col"), None), P(), P()),
        out_specs=P("row", "col"),
        check_vma=False,
    )
```

time: 480 us -> 115 us (0.24); the launches traced: 471 us -> 114 us
  matrix products: 199 us -> 0 us
  waiting for transfers between devices: 179 us -> 39.9 us
  local copies, waits for them, and re-layouts: 59 us -> 13.2 us
  Pallas kernels: 0 us -> 27.2 us
  starting transfers between devices: 11.9 us -> 32.8 us
  between operations: 14.5 us -> 0.17 us
  other arithmetic: 7.52 us -> 0.87 us
    dot_general x521 -> x0, matrix products: 199 us -> none  [the longest x520 199 us: matmul(): jnp.dot(left, right, precision=lax.Precision.HIGHEST, preferred_element_t...]
    psum x4 -> x0, waiting for transfers between devices: 126 us -> none  [on_device(): gram_sum, product = lax.psum((local_gram, local_product), 'row')]
    gather x68 -> x0, local copies, waits for them, and re-layouts: 53.6 us -> none  [the longest x64 43.3 us: upper_inverse(): diag_vals = jnp.diagonal(upper)]
    ppermute x0 -> x19, waiting for transfers between devices: none -> 38.9 us  [send(): return lax.ppermute(value, ('row', 'col'), perm)]
    all_gather x1 -> x0, waiting for transfers between devices: 31 us -> none  [on_device(): gathered = lax.all_gather(reflectors, 'col', axis=1, tiled=True)]
    pallas_call x0 -> x6, Pallas kernels: none -> 27.2 us  [the longest x2 10.6 us: gram(): pl.pallas_call(functools.partial(gram_kernel, count, before is not None),...]
    ppermute x0 -> x19, starting transfers between devices: none -> 21.8 us  [send(): return lax.ppermute(value, ('row', 'col'), perm)]
    all_to_all x2, waiting for transfers between devices: 20.9 us -> 1.07 us  [the longest x1 1.06 us: on_device(): lax.all_to_all(ordered, ('row', 'col'), split_axis=0, concat_axis=0, tile...]
  transfers between devices with their start and end apart: 7 -> 21, of which waited for: 6 -> 6; matrix products, arithmetic and copies ran while one was open for 2% -> 0% of each run, Pallas kernels for 0% -> 19%
where the time goes in v1:
time: 115 us; the launch traced here: 114 us
  waiting for transfers between devices  39.9 us (35%)
  starting transfers between devices  32.8 us (29%)
  Pallas kernels  27.2 us (24%)
  local copies, waits for them, and re-layouts  13.2 us (11%)
    ppermute x19, waiting for transfers between devices, send(): return lax.ppermute(value, ('row', 'col'), perm)  38.9 us
    ppermute x19, starting transfers between devices, send(): return lax.ppermute(value, ('row', 'col'), perm)  21.8 us
    unnamed x32, local copies, waits for them, and re-layouts  13.2 us
    pallas_call x2, Pallas kernels, gram(): pl.pallas_call(functools.partial(gram_kernel, count, before is not None),...  10.6 us
    pallas_call x1, Pallas kernels, invert(): pl.pallas_call(invert_kernel, out_shape=jax.ShapeDtypeStruct(own.shape, F...  7.47 us
    all_to_all x1, starting transfers between devices, on_device(): lax.all_to_all(vectors.reshape(cols, local_rows, -1), 'col', split_axis=0...  7.28 us
    pallas_call x1, Pallas kernels, update(): pl.pallas_call(functools.partial(update_kernel, inner), out_shape=jax.Sha...  5.99 us
    all_to_all x1, starting transfers between devices, on_device(): lax.all_to_all(ordered, ('row', 'col'), split_axis=0, concat_axis=0, tile...  3.75 us
  transfers between devices with their start and end apart: 21, of which 6 were waited for; matrix products, arithmetic and copies ran while one was open for 0% of the time, Pallas kernels for 19%

profile of v1, /device:TPU:0, one launch (start us, length us, event | category | flops | bytes accessed | tf_op | source)
XLA Modules:
  0.0 114.2 jit_solution(13740659190508903543)
XLA Ops:
  0.0 7.3 %all-to-all-start = ((f32[8,64,256]{2,1,0:T(8,128)}), f32[8,64,256]{2,1,0:T(8,128)S(1)}, u32[]{:S(2)}, u32[]{:S(2)}) async-start(f32[8,64,256]{2,1,0:T(8,128)} %bitcast.9), calls=%async_computation | async-start | bytes 1048576 | tf_op jit(solution)/shard_map/all_to_all | solution.py:277
  7.3 2.0 %collective-permute-start = (f32[4,64,256]{2,1,0:T(8,128)}, f32[4,64,256]{2,1,0:T(8,128)S(1)}, u32[]{:S(2)}, u32[]{:S(2)}) collective-permute-start(f32[4,64,256]{2,1,0:T(8,128)} %refs_0_.1), channel_id=1, source_target_pairs={{0,2},{1,3},{2,0},{3,1},{4,6},{5,7},{6,4},{7,5},{8,10},{9,11},{10,... | collective-permute-start | bytes 786440 | tf_op jit(solution)/shard_map/ppermute | solution.py:261
  9.3 2.4 %collective-permute-start.1 = (f32[4,64,256]{2,1,0:T(8,128)}, f32[4,64,256]{2,1,0:T(8,128)S(1)}, u32[]{:S(2)}, u32[]{:S(2)}) collective-permute-start(f32[4,64,256]{2,1,0:T(8,128)} %refs_0_.1), channel_id=1, source_target_pairs={{0,4},{1,5},{2,6},{3,7},{4,0},{5,1},{6,2},{7,3},{8,12},{9,13},{10,... | collective-permute-start | bytes 786440 | tf_op jit(solution)/shard_map/ppermute | solution.py:261
  11.8 1.9 %collective-permute-start.3 = (f32[4,64,256]{2,1,0:T(8,128)}, f32[4,64,256]{2,1,0:T(8,128)S(1)}, u32[]{:S(2)}, u32[]{:S(2)}) collective-permute-start(f32[4,64,256]{2,1,0:T(8,128)} %refs_0_.1), channel_id=1, source_target_pairs={{0,1},{1,0},{2,3},{3,2},{4,5},{5,4},{6,7},{7,6},{8,24},{9,25},{10,... | collective-permute-start | bytes 786440 | tf_op jit(solution)/shard_map/ppermute | solution.py:261
  13.7 1.5 %collective-permute-start.7 = (f32[4,64,256]{2,1,0:T(8,128)}, f32[4,64,256]{2,1,0:T(8,128)S(1)}, u32[]{:S(2)}, u32[]{:S(2)}) collective-permute-start(f32[4,64,256]{2,1,0:T(8,128)} %refs_0_.1), channel_id=1, source_target_pairs={{0,16},{1,17},{2,18},{3,19},{4,20},{5,21},{6,22},{7,23},{8,9},{9,8... | collective-permute-start | bytes 786440 | tf_op jit(solution)/shard_map/ppermute | solution.py:261
  15.2 12.3 %collective-permute-done.refs_1_ = f32[4,64,256]{2,1,0:T(8,128)S(1)} collective-permute-done((f32[4,64,256]{2,1,0:T(8,128)}, f32[4,64,256]{2,1,0:T(8,128)S(1)}, u32[]{:S(2)}, u32[]{:S(2)}) %collective-permute-start) | collective-permute-done | bytes 262176 | tf_op jit(solution)/shard_map/ppermute | solution.py:261
  27.5 1.6 %collective-permute-start.4 = (f32[4,64,256]{2,1,0:T(8,128)S(1)}, f32[4,64,256]{2,1,0:T(8,128)}, u32[]{:S(2)}, u32[]{:S(2)}) collective-permute-start(f32[4,64,256]{2,1,0:T(8,128)S(1)} %collective-permute-done.refs_1_), channel_id=1, source_target_pairs={{0,1},{1,0},{2,3},{3,2},{4,5},{5,4},{6,7},{7,6},{8,24},{9,25},{10,... | collective-permute-start | bytes 786440 | tf_op jit(solution)/shard_map/ppermute | solution.py:261
  29.1 11.0 %collective-permute-done.1.refs_2_ = f32[4,64,256]{2,1,0:T(8,128)S(1)} collective-permute-done((f32[4,64,256]{2,1,0:T(8,128)}, f32[4,64,256]{2,1,0:T(8,128)S(1)}, u32[]{:S(2)}, u32[]{:S(2)}) %collective-permute-start.1) | collective-permute-done | bytes 262176 | tf_op jit(solution)/shard_map/ppermute | solution.py:261
  40.1 1.1 collective-permute-start.5
  42.1 1.5 %collective-permute-start.10 = (f32[4,64,256]{2,1,0:T(8,128)S(1)}, f32[4,64,256]{2,1,0:T(8,128)S(1)}, u32[]{:S(2)}, u32[]{:S(2)}) collective-permute-start(f32[4,64,256]{2,1,0:T(8,128)S(1)} %collective-permute-done.2.refs_3_), channel_id=1, source_target_pairs={{0,16},{1,17},{2,18},{3,19},{4,20},{5,21},{6,22},{7,23},{8,9},{9,8... | collective-permute-start | bytes 786440 | tf_op jit(solution)/shard_map/ppermute | solution.py:261
  44.2 1.5 %collective-permute-start.9 = (f32[4,64,256]{2,1,0:T(8,128)S(1)}, f32[4,64,256]{2,1,0:T(8,128)}, u32[]{:S(2)}, u32[]{:S(2)}) collective-permute-start(f32[4,64,256]{2,1,0:T(8,128)S(1)} %collective-permute-done.1.refs_2_), channel_id=1, source_target_pairs={{0,16},{1,17},{2,18},{3,19},{4,20},{5,21},{6,22},{7,23},{8,9},{9,8... | collective-permute-start | bytes 786440 | tf_op jit(solution)/shard_map/ppermute | solution.py:261
  45.6 3.8 %collective-permute-done.5.refs_6_ = f32[4,64,256]{2,1,0:T(8,128)} collective-permute-done((f32[4,64,256]{2,1,0:T(8,128)S(1)}, f32[4,64,256]{2,1,0:T(8,128)}, u32[]{:S(2)}, u32[]{:S(2)}) %collective-permute-start.5) | collective-permute-done | bytes 262176 | tf_op jit(solution)/shard_map/ppermute | solution.py:261
  49.4 1.5 %collective-permute-start.11 = (f32[4,64,256]{2,1,0:T(8,128)S(1)}, f32[4,64,256]{2,1,0:T(8,128)}, u32[]{:S(2)}, u32[]{:S(2)}) collective-permute-start(f32[4,64,256]{2,1,0:T(8,128)S(1)} %collective-permute-done.3.refs_4_), channel_id=1, source_target_pairs={{0,16},{1,17},{2,18},{3,19},{4,20},{5,21},{6,22},{7,23},{8,9},{9,8... | collective-permute-start | bytes 786440 | tf_op jit(solution)/shard_map/ppermute | solution.py:261
  50.9 4.1 %collective-permute-done.6.refs_7_ = f32[4,64,256]{2,1,0:T(8,128)} collective-permute-done((f32[4,64,256]{2,1,0:T(8,128)S(1)}, f32[4,64,256]{2,1,0:T(8,128)}, u32[]{:S(2)}, u32[]{:S(2)}) %collective-permute-start.6) | collective-permute-done | bytes 262176 | tf_op jit(solution)/shard_map/ppermute | solution.py:261
  55.1 1.5 %collective-permute-start.12 = (f32[4,64,256]{2,1,0:T(8,128)}, f32[4,64,256]{2,1,0:T(8,128)}, u32[]{:S(2)}, u32[]{:S(2)}) collective-permute-start(f32[4,64,256]{2,1,0:T(8,128)} %collective-permute-done.4.refs_5_), channel_id=1, source_target_pairs={{0,16},{1,17},{2,18},{3,19},{4,20},{5,21},{6,22},{7,23},{8,9},{9,8... | collective-permute-start | bytes 786440 | tf_op jit(solution)/shard_map/ppermute | solution.py:261
  58.5 1.5 %collective-permute-start.14 = (f32[4,64,256]{2,1,0:T(8,128)}, f32[4,64,256]{2,1,0:T(8,128)}, u32[]{:S(2)}, u32[]{:S(2)}) collective-permute-start(f32[4,64,256]{2,1,0:T(8,128)} %collective-permute-done.6.refs_7_), channel_id=1, source_target_pairs={{0,16},{1,17},{2,18},{3,19},{4,20},{5,21},{6,22},{7,23},{8,9},{9,8... | collective-permute-start | bytes 786440 | tf_op jit(solution)/shard_map/ppermute | solution.py:261
  60.9 4.8 %gram.2 = (bf16[512,1024]{1,0:T(8,128)(2,1)S(1)}, bf16[512,1024]{1,0:T(8,128)(2,1)S(1)}, bf16[1024,512]{1,0:T(8,128)(2,1)S(1)}, bf16[1024,512]{1,0:T(8,128)(2,1)...) custom-call(f32[4,64,256]{2,1,0:T(8,128)S(1)} %copy-done.11, f32[4,64,256]{2,1,0:T(8,128)S(1)} %collective-permute-done.refs_1_, ...), custom_call_target="tpu_custom_call" | custom-call | flops 2013265920 | bytes 8388608 | tf_op jit(solution)/shard_map/gram/pallas_call | solution.py:106
  65.7 1.0 copy-done
  66.8 1.8 %reorder.1 = f32[16,64,128]{2,1,0:T(8,128)} custom-call(s32[16]{0:T(128)S(1)} %copy-done.8, s32[16]{0:T(128)S(1)} %copy-done.9, f32[8,64,256]{2,1,0:T(8,128)S(1)} %all-to-all-done.spread), custom_call_target="tpu_custom_call" | custom-call | tf_op jit(solution)/shard_map/reorder/pallas_call | solution.py:62
  68.5 3.8 %all-to-all-start.1 = ((f32[16,64,128]{2,1,0:T(8,128)}), f32[16,64,128]{2,1,0:T(8,128)S(1)}, u32[]{:S(2)}, u32[]{:S(2)}) async-start(f32[16,64,128]{2,1,0:T(8,128)} %reorder.1), calls=%async_computation.1 | async-start | bytes 1048576 | tf_op jit(solution)/shard_map/all_to_all | solution.py:283
  74.2 5.8 %gram.3 = (bf16[512,1024]{1,0:T(8,128)(2,1)S(1)}, bf16[512,1024]{1,0:T(8,128)(2,1)S(1)}, bf16[1024,512]{1,0:T(8,128)(2,1)S(1)}, bf16[1024,512]{1,0:T(8,128)(2,1)...) custom-call(f32[4,64,256]{2,1,0:T(8,128)S(1)} %collective-permute-done.7.refs_0_, f32[4,64,256]{2,1,0:T(8,128)S(1)} %copy-done.15, ...), custom_call_target="tpu_custom_call" | custom-call | flops 2013265920 | bytes 8388608 | tf_op jit(solution)/shard_map/gram/pallas_call | solution.py:106
  80.0 1.1 copy-done.3
  83.6 1.1 all-to-all-done.1.slab
  84.7 1.2 %copy-done.1 = bf16[1024,512]{1,0:T(8,128)(2,1)S(1)} copy-done((bf16[1024,512]{1,0:T(8,128)(2,1)S(1)}, bf16[1024,512]{1,0:T(8,128)(2,1)}, u32[]{:S(2)}) %copy-start.1) | copy-done | bytes 1048600
  85.9 1.2 %copy-done.2 = bf16[1024,512]{1,0:T(8,128)(2,1)S(1)} copy-done((bf16[1024,512]{1,0:T(8,128)(2,1)S(1)}, bf16[1024,512]{1,0:T(8,128)(2,1)}, u32[]{:S(2)}) %copy-start.2) | copy-done | bytes 1048600
  87.1 1.2 %copy-done.6 = bf16[1024,512]{1,0:T(8,128)(2,1)S(1)} copy-done((bf16[1024,512]{1,0:T(8,128)(2,1)S(1)}, bf16[1024,512]{1,0:T(8,128)(2,1)}, u32[]{:S(2)}) %copy-start.6) | copy-done | bytes 1048600
  88.3 1.2 %copy-done.7 = bf16[1024,512]{1,0:T(8,128)(2,1)S(1)} copy-done((bf16[1024,512]{1,0:T(8,128)(2,1)S(1)}, bf16[1024,512]{1,0:T(8,128)(2,1)}, u32[]{:S(2)}) %copy-start.7) | copy-done | bytes 1048600
  89.6 1.4 %project.1.own = f32[1024,128]{1,0:T(8,128)S(1)} custom-call(bf16[1024,512]{1,0:T(8,128)(2,1)S(1)} %copy-done.1, bf16[1024,512]{1,0:T(8,128)(2,1)S(1)} %copy-done.2, bf16[1024,512]{1,0:T(8,128)(2,1)S(1)} %copy-done.6, bf16[1024,512]{1,0:T(8,128)(2,1)S(1)} %copy-done.7, f32[16,64,128]{2,1,0:T(8,128)S(1)} %all-to-all-done.1.slab), custom_call_target="tpu_custom_call" | custom-call | flops 1073741824 | bytes 4194304 | tf_op jit(solution)/shard_map/project/pallas_call | solution.py:202
  91.0 7.5 %invert.1.inverse = f32[4,256,256]{2,1,0:T(8,128)S(1)} custom-call(f32[4,256,256]{2,1,0:T(8,128)S(1)} %copy-done.10, f32[4,256,256]{2,1,0:T(8,128)} %collective-permute-done.16.other), custom_call_target="tpu_custom_call" | custom-call | flops 10000000000 | bytes 3145728 | tf_op jit(solution)/shard_map/invert/pallas_call | solution.py:162
  98.5 6.0 %update.1 = f32[2,8,64,128]{3,2,1,0:T(8,128)S(1)} custom-call(f32[1024,128]{1,0:T(8,128)S(1)} %project.1.own, f32[1024,128]{1,0:T(8,128)S(1)} %collective-permute-done.15.other, f32[4,256,256]{2,1,0:T(8,128)S(1)} %invert.1.inverse, f32[6,256,256]{2,1,0:T(8,128)} %get-tuple-element.24.corner_own, f32[6,256,256]{2,1,0:T(8,128)} %collective-permute-done.17.corner_other, ...), custom_call_target="tpu_custom_call" | custom-call | tf_op jit(solution)/shard_map/update/pallas_call | solution.py:240
  104.5 1.2 %collective-permute-start.18 = (f32[8,64,128]{2,1,0:T(8,128)S(1)}, f32[8,64,128]{2,1,0:T(8,128)S(1)}, u32[]{:S(2)}, u32[]{:S(2)}) collective-permute-start(f32[8,64,128]{2,1,0:T(8,128)S(1)} %get-tuple-element.32), channel_id=1, source_target_pairs={{0,16},{1,17},{2,18},{3,19},{4,20},{5,21},{6,22},{7,23},{8,24},{9,... | collective-permute-start | bytes 786440 | tf_op jit(solution)/shard_map/ppermute | solution.py:261
  105.7 7.6 %collective-permute-done.18 = f32[8,64,128]{2,1,0:T(8,128)S(1)} collective-permute-done((f32[8,64,128]{2,1,0:T(8,128)S(1)}, f32[8,64,128]{2,1,0:T(8,128)S(1)}, u32[]{:S(2)}, u32[]{:S(2)}) %collective-permute-start.18) | collective-permute-done | bytes 262176 | tf_op jit(solution)/shard_map/ppermute | solution.py:261
  (51 shorter events, 9.9 us)
Async XLA Ops:
  0.0 66.7 %all-to-all-start = ((f32[8,64,256]{2,1,0:T(8,128)}), f32[8,64,256]{2,1,0:T(8,128)S(1)}, u32[]{:S(2)}, u32[]{:S(2)}) async-start(f32[8,64,256]{2,1,0:T(8,128)} %bitcast.9), calls=%async_computation | async-start | bytes 1048576 | tf_op jit(solution)/shard_map/all_to_all | solution.py:277
  7.3 59.5 %copy-start.8 = (s32[16]{0:T(128)S(1)}, s32[16]{0:T(128)}, u32[]{:S(2)}) copy-start(s32[16]{0:T(128)} %owner.1) | copy-start | bytes 196
  7.3 59.5 %copy-start.9 = (s32[16]{0:T(128)S(1)}, s32[16]{0:T(128)}, u32[]{:S(2)}) copy-start(s32[16]{0:T(128)} %slot.1) | copy-start | bytes 196
  7.3 20.2 %collective-permute-start = (f32[4,64,256]{2,1,0:T(8,128)}, f32[4,64,256]{2,1,0:T(8,128)S(1)}, u32[]{:S(2)}, u32[]{:S(2)}) collective-permute-start(f32[4,64,256]{2,1,0:T(8,128)} %refs_0_.1), channel_id=1, source_target_pairs={{0,2},{1,3},{2,0},{3,1},{4,6},{5,7},{6,4},{7,5},{8,10},{9,11},{10,... | collective-permute-start | bytes 786440 | tf_op jit(solution)/shard_map/ppermute | solution.py:261
  9.3 30.8 %collective-permute-start.1 = (f32[4,64,256]{2,1,0:T(8,128)}, f32[4,64,256]{2,1,0:T(8,128)S(1)}, u32[]{:S(2)}, u32[]{:S(2)}) collective-permute-start(f32[4,64,256]{2,1,0:T(8,128)} %refs_0_.1), channel_id=1, source_target_pairs={{0,4},{1,5},{2,6},{3,7},{4,0},{5,1},{6,2},{7,3},{8,12},{9,13},{10,... | collective-permute-start | bytes 786440 | tf_op jit(solution)/shard_map/ppermute | solution.py:261
  11.7 29.5 %collective-permute-start.2 = (f32[4,64,256]{2,1,0:T(8,128)}, f32[4,64,256]{2,1,0:T(8,128)S(1)}, u32[]{:S(2)}, u32[]{:S(2)}) collective-permute-start(f32[4,64,256]{2,1,0:T(8,128)} %refs_0_.1), channel_id=1, source_target_pairs={{0,6},{1,7},{2,4},{3,5},{4,2},{5,3},{6,0},{7,1},{8,14},{9,15},{10,... | collective-permute-start | bytes 786440 | tf_op jit(solution)/shard_map/ppermute | solution.py:261
  11.8 30.4 %collective-permute-start.3 = (f32[4,64,256]{2,1,0:T(8,128)}, f32[4,64,256]{2,1,0:T(8,128)S(1)}, u32[]{:S(2)}, u32[]{:S(2)}) collective-permute-start(f32[4,64,256]{2,1,0:T(8,128)} %refs_0_.1), channel_id=1, source_target_pairs={{0,1},{1,0},{2,3},{3,2},{4,5},{5,4},{6,7},{7,6},{8,24},{9,25},{10,... | collective-permute-start | bytes 786440 | tf_op jit(solution)/shard_map/ppermute | solution.py:261
  13.7 29.9 %collective-permute-start.7 = (f32[4,64,256]{2,1,0:T(8,128)}, f32[4,64,256]{2,1,0:T(8,128)S(1)}, u32[]{:S(2)}, u32[]{:S(2)}) collective-permute-start(f32[4,64,256]{2,1,0:T(8,128)} %refs_0_.1), channel_id=1, source_target_pairs={{0,16},{1,17},{2,18},{3,19},{4,20},{5,21},{6,22},{7,23},{8,9},{9,8... | collective-permute-start | bytes 786440 | tf_op jit(solution)/shard_map/ppermute | solution.py:261
  27.5 16.6 %collective-permute-start.4 = (f32[4,64,256]{2,1,0:T(8,128)S(1)}, f32[4,64,256]{2,1,0:T(8,128)}, u32[]{:S(2)}, u32[]{:S(2)}) collective-permute-start(f32[4,64,256]{2,1,0:T(8,128)S(1)} %collective-permute-done.refs_1_), channel_id=1, source_target_pairs={{0,1},{1,0},{2,3},{3,2},{4,5},{5,4},{6,7},{7,6},{8,24},{9,25},{10,... | collective-permute-start | bytes 786440 | tf_op jit(solution)/shard_map/ppermute | solution.py:261
  40.1 9.3 %collective-permute-start.5 = (f32[4,64,256]{2,1,0:T(8,128)S(1)}, f32[4,64,256]{2,1,0:T(8,128)}, u32[]{:S(2)}, u32[]{:S(2)}) collective-permute-start(f32[4,64,256]{2,1,0:T(8,128)S(1)} %collective-permute-done.1.refs_2_), channel_id=1, source_target_pairs={{0,1},{1,0},{2,3},{3,2},{4,5},{5,4},{6,7},{7,6},{8,24},{9,25},{10,... | collective-permute-start | bytes 786440 | tf_op jit(solution)/shard_map/ppermute | solution.py:261
  41.1 13.9 %collective-permute-start.6 = (f32[4,64,256]{2,1,0:T(8,128)S(1)}, f32[4,64,256]{2,1,0:T(8,128)}, u32[]{:S(2)}, u32[]{:S(2)}) collective-permute-start(f32[4,64,256]{2,1,0:T(8,128)S(1)} %collective-permute-done.2.refs_3_), channel_id=1, source_target_pairs={{0,1},{1,0},{2,3},{3,2},{4,5},{5,4},{6,7},{7,6},{8,24},{9,25},{10,... | collective-permute-start | bytes 786440 | tf_op jit(solution)/shard_map/ppermute | solution.py:261
  42.1 14.4 %collective-permute-start.10 = (f32[4,64,256]{2,1,0:T(8,128)S(1)}, f32[4,64,256]{2,1,0:T(8,128)S(1)}, u32[]{:S(2)}, u32[]{:S(2)}) collective-permute-start(f32[4,64,256]{2,1,0:T(8,128)S(1)} %collective-permute-done.2.refs_3_), channel_id=1, source_target_pairs={{0,16},{1,17},{2,18},{3,19},{4,20},{5,21},{6,22},{7,23},{8,9},{9,8... | collective-permute-start | bytes 786440 | tf_op jit(solution)/shard_map/ppermute | solution.py:261
  43.6 14.2 %collective-permute-start.8 = (f32[4,64,256]{2,1,0:T(8,128)S(1)}, f32[4,64,256]{2,1,0:T(8,128)S(1)}, u32[]{:S(2)}, u32[]{:S(2)}) collective-permute-start(f32[4,64,256]{2,1,0:T(8,128)S(1)} %collective-permute-done.refs_1_), channel_id=1, source_target_pairs={{0,16},{1,17},{2,18},{3,19},{4,20},{5,21},{6,22},{7,23},{8,9},{9,8... | collective-permute-start | bytes 786440 | tf_op jit(solution)/shard_map/ppermute | solution.py:261
  44.2 28.1 %collective-permute-start.9 = (f32[4,64,256]{2,1,0:T(8,128)S(1)}, f32[4,64,256]{2,1,0:T(8,128)}, u32[]{:S(2)}, u32[]{:S(2)}) collective-permute-start(f32[4,64,256]{2,1,0:T(8,128)S(1)} %collective-permute-done.1.refs_2_), channel_id=1, source_target_pairs={{0,16},{1,17},{2,18},{3,19},{4,20},{5,21},{6,22},{7,23},{8,9},{9,8... | collective-permute-start | bytes 786440 | tf_op jit(solution)/shard_map/ppermute | solution.py:261
  49.4 22.9 %collective-permute-start.11 = (f32[4,64,256]{2,1,0:T(8,128)S(1)}, f32[4,64,256]{2,1,0:T(8,128)}, u32[]{:S(2)}, u32[]{:S(2)}) collective-permute-start(f32[4,64,256]{2,1,0:T(8,128)S(1)} %collective-permute-done.3.refs_4_), channel_id=1, source_target_pairs={{0,16},{1,17},{2,18},{3,19},{4,20},{5,21},{6,22},{7,23},{8,9},{9,8... | collective-permute-start | bytes 786440 | tf_op jit(solution)/shard_map/ppermute | solution.py:261
  55.1 17.3 %collective-permute-start.12 = (f32[4,64,256]{2,1,0:T(8,128)}, f32[4,64,256]{2,1,0:T(8,128)}, u32[]{:S(2)}, u32[]{:S(2)}) collective-permute-start(f32[4,64,256]{2,1,0:T(8,128)} %collective-permute-done.4.refs_5_), channel_id=1, source_target_pairs={{0,16},{1,17},{2,18},{3,19},{4,20},{5,21},{6,22},{7,23},{8,9},{9,8... | collective-permute-start | bytes 786440 | tf_op jit(solution)/shard_map/ppermute | solution.py:261
  57.3 15.1 %collective-permute-start.13 = (f32[4,64,256]{2,1,0:T(8,128)}, f32[4,64,256]{2,1,0:T(8,128)}, u32[]{:S(2)}, u32[]{:S(2)}) collective-permute-start(f32[4,64,256]{2,1,0:T(8,128)} %collective-permute-done.5.refs_6_), channel_id=1, source_target_pairs={{0,16},{1,17},{2,18},{3,19},{4,20},{5,21},{6,22},{7,23},{8,9},{9,8... | collective-permute-start | bytes 786440 | tf_op jit(solution)/shard_map/ppermute | solution.py:261
  58.5 13.8 %collective-permute-start.14 = (f32[4,64,256]{2,1,0:T(8,128)}, f32[4,64,256]{2,1,0:T(8,128)}, u32[]{:S(2)}, u32[]{:S(2)}) collective-permute-start(f32[4,64,256]{2,1,0:T(8,128)} %collective-permute-done.6.refs_7_), channel_id=1, source_target_pairs={{0,16},{1,17},{2,18},{3,19},{4,20},{5,21},{6,22},{7,23},{8,9},{9,8... | collective-permute-start | bytes 786440 | tf_op jit(solution)/shard_map/ppermute | solution.py:261
  65.7 1.0 copy-start
  68.5 16.1 %all-to-all-start.1 = ((f32[16,64,128]{2,1,0:T(8,128)}), f32[16,64,128]{2,1,0:T(8,128)S(1)}, u32[]{:S(2)}, u32[]{:S(2)}) async-start(f32[16,64,128]{2,1,0:T(8,128)} %reorder.1), calls=%async_computation.1 | async-start | bytes 1048576 | tf_op jit(solution)/shard_map/all_to_all | solution.py:283
  80.0 1.1 copy-start.3
  81.1 1.0 copy-start.4
  82.1 1.0 copy-start.5
  83.1 7.9 %collective-permute-start.16 = (f32[4,256,256]{2,1,0:T(8,128)}, f32[4,256,256]{2,1,0:T(8,128)}, u32[]{:S(2)}, u32[]{:S(2)}) collective-permute-start(f32[4,256,256]{2,1,0:T(8,128)} %get-tuple-element.23.own), channel_id=1, source_target_pairs={{0,8},{1,9},{2,10},{3,11},{4,12},{5,13},{6,14},{7,15},{8,0},{9,1},... | collective-permute-start | bytes 3145736 | tf_op jit(solution)/shard_map/ppermute | solution.py:261
  83.1 15.4 %collective-permute-start.17 = (f32[6,256,256]{2,1,0:T(8,128)}, f32[6,256,256]{2,1,0:T(8,128)}, u32[]{:S(2)}, u32[]{:S(2)}) collective-permute-start(f32[6,256,256]{2,1,0:T(8,128)} %get-tuple-element.24.corner_own), channel_id=1, source_target_pairs={{0,8},{1,9},{2,10},{3,11},{4,12},{5,13},{6,14},{7,15},{8,0},{9,1},... | collective-permute-start | bytes 4718600 | tf_op jit(solution)/shard_map/ppermute | solution.py:261
  84.6 1.2 %copy-start.1 = (bf16[1024,512]{1,0:T(8,128)(2,1)S(1)}, bf16[1024,512]{1,0:T(8,128)(2,1)}, u32[]{:S(2)}) copy-start(bf16[1024,512]{1,0:T(8,128)(2,1)} %copy-done) | copy-start | bytes 3145732
  85.9 1.2 %copy-start.2 = (bf16[1024,512]{1,0:T(8,128)(2,1)S(1)}, bf16[1024,512]{1,0:T(8,128)(2,1)}, u32[]{:S(2)}) copy-start(bf16[1024,512]{1,0:T(8,128)(2,1)} %get-tuple-element.18.low_a) | copy-start | bytes 3145732
  87.1 1.2 %copy-start.6 = (bf16[1024,512]{1,0:T(8,128)(2,1)S(1)}, bf16[1024,512]{1,0:T(8,128)(2,1)}, u32[]{:S(2)}) copy-start(bf16[1024,512]{1,0:T(8,128)(2,1)} %copy-done.5) | copy-start | bytes 3145732
  88.3 1.2 %copy-start.7 = (bf16[1024,512]{1,0:T(8,128)(2,1)S(1)}, bf16[1024,512]{1,0:T(8,128)(2,1)}, u32[]{:S(2)}) copy-start(bf16[1024,512]{1,0:T(8,128)(2,1)} %get-tuple-element.22.low_b) | copy-start | bytes 3145732
  89.5 1.5 %copy-start.10 = (f32[4,256,256]{2,1,0:T(8,128)S(1)}, f32[4,256,256]{2,1,0:T(8,128)}, u32[]{:S(2)}) copy-start(f32[4,256,256]{2,1,0:T(8,128)} %get-tuple-element.23.own) | copy-start | bytes 3145732
  90.9 7.6 %collective-permute-start.15 = (f32[1024,128]{1,0:T(8,128)S(1)}, f32[1024,128]{1,0:T(8,128)S(1)}, u32[]{:S(2)}, u32[]{:S(2)}) collective-permute-start(f32[1024,128]{1,0:T(8,128)S(1)} %project.1.own), channel_id=1, source_target_pairs={{0,8},{1,9},{2,10},{3,11},{4,12},{5,13},{6,14},{7,15},{8,0},{9,1},... | collective-permute-start | bytes 1572872 | tf_op jit(solution)/shard_map/ppermute | solution.py:261
  104.5 8.8 %collective-permute-start.18 = (f32[8,64,128]{2,1,0:T(8,128)S(1)}, f32[8,64,128]{2,1,0:T(8,128)S(1)}, u32[]{:S(2)}, u32[]{:S(2)}) collective-permute-start(f32[8,64,128]{2,1,0:T(8,128)S(1)} %get-tuple-element.32), channel_id=1, source_target_pairs={{0,16},{1,17},{2,18},{3,19},{4,20},{5,21},{6,22},{7,23},{8,24},{9,... | collective-permute-start | bytes 786440 | tf_op jit(solution)/shard_map/ppermute | solution.py:261
  (5 other events, 4.3 us)

commit v2 on v1

v2 whole, which is shorter than its diff:
```python
import functools

import jax
import jax.numpy as jnp
from jax import lax
from jax.experimental import pallas as pl
from jax.experimental.pallas import tpu as pltpu
from jax.sharding import PartitionSpec as P

BW = 128
BLK_DEV = 2
LOW = 8
CHUNKS = 4
F32, BF16 = jnp.float32, jnp.bfloat16


def vmem(count):
    return [pl.BlockSpec(memory_space=pltpu.VMEM)] * count


def smem(count):
    return [pl.BlockSpec(memory_space=pltpu.SMEM)] * count


def shape(dims, kind=F32):
    return jax.ShapeDtypeStruct(tuple(dims), kind)


def call(body, name, outs, inputs, scratch=(), scalars=0, far=0, far_outs=0, copies=0, aliases=None, flops=0, mib=16, near_pinned=False):
    near = len(inputs) - scalars - far
    any_space = pl.BlockSpec(memory_space=pl.ANY)
    return pl.pallas_call(
        body,
        out_shape=tuple(pltpu.VMEM(out.shape, out.dtype) if near_pinned else out for out in outs[:len(outs) - far_outs]) + tuple(pltpu.HBM(out.shape, out.dtype) for out in outs[len(outs) - far_outs:]),
        in_specs=smem(scalars) + vmem(near) + [any_space] * far,
        out_specs=tuple(vmem(len(outs) - far_outs) + [any_space] * far_outs),
        scratch_shapes=list(scratch) + ([pltpu.SemaphoreType.DMA((copies,))] if copies else []),
        input_output_aliases=aliases or {},
        compiler_params=pltpu.CompilerParams(vmem_limit_bytes=mib * 1024 * 1024),
        cost_estimate=pl.CostEstimate(flops=flops, bytes_accessed=4 * 1024 * 1024, transcendentals=0),
        name=name,
    )(*inputs)


def pinned(arrays):
    return [pltpu.with_memory_space_constraint(array, pltpu.HBM) for array in arrays]


def start_copies(pairs, sems, base=0):
    copies = [pltpu.make_async_copy(src, dst, sems.at[base + at]) for at, (src, dst) in enumerate(pairs)]
    for copy in copies:
        copy.start()
    return copies


def halves(value):
    high = value.astype(BF16)
    return high, (value - high.astype(F32)).astype(BF16)


def dot(left, right):
    return jnp.dot(left, right, preferred_element_type=F32)


def dot3(left, right):
    return dot(left[0], right[0]) + (dot(left[0], right[1]) + dot(left[1], right[0]))


def pairs_of(panels):
    return [(p, q) for p in range(panels) for q in range(p + 1, panels)]


def reorder_kernel(half, owner_list, slot_list, spread, ordered, owner, slot, held, sems):
    copies = start_copies([(owner_list, owner), (slot_list, slot), (spread, held)], sems)
    for copy in copies:
        copy.wait()

    def move(block, carry):
        place = slot[block] * half + owner[block]
        parity = block % BLK_DEV

        @pl.when(parity == 0)
        def _():
            ordered[place] = held[block // BLK_DEV, :, :BW]

        @pl.when(parity == 1)
        def _():
            ordered[place] = held[block // BLK_DEV, :, BW:]

        return carry

    lax.fori_loop(0, ordered.shape[0], move, 0)


def reorder(spread, owner_list, slot_list):
    cols, rows, _ = spread.shape
    outs = [shape((cols * BLK_DEV, rows, BW))]
    scratch = [pltpu.SMEM(owner_list.shape, jnp.int32), pltpu.SMEM(slot_list.shape, jnp.int32), pltpu.VMEM(spread.shape, F32)]
    return call(
        functools.partial(reorder_kernel, cols), "reorder", outs, (owner_list, slot_list, spread), far=3, copies=3, scratch=scratch
    )[0]


def is_odd(inner):
    return (lax.axis_index("row") % inner) % 2


def gram_kernel(inner, count, before, *refs):
    pieces, refs = refs[:4 * count], refs[4 * count:]
    diag, corner, high_out, low_out, staged, high, low, high_t, low_t, sems = refs
    panels, rows, width = pieces[0].shape
    odd = is_odd(inner)
    places = (0, jnp.where(odd == 0, 1, 2), jnp.where(odd == 0, 2, 1), 3)
    arriving = start_copies([(piece, staged.at[at]) for at, piece in enumerate(pieces)], sems)
    for at, copy in enumerate(arriving):
        copy.wait()
        cut = pl.ds(pl.multiple_of((at // 4 * 4 + places[at % 4]) * rows, rows), rows)
        for p in range(panels):
            top, rest = halves(staged[at, p])
            high[cut, p * width:(p + 1) * width] = top
            low[cut, p * width:(p + 1) * width] = rest
    leaving = start_copies([(high, high_out), (low, low_out)], sems, 4 * count)
    cuts = [slice(p * width, (p + 1) * width) for p in range(panels)]
    for p, cut in enumerate(cuts):
        high_t[cut, :] = high[:, cut].T
        low_t[cut, :] = low[:, cut].T
        value = dot3((high_t[cut, :], low_t[cut, :]), (high[:, cut], low[:, cut]))
        diag[p] = value + before[0][p] if before else value
    for at, (p, q) in enumerate(pairs_of(panels)):
        value = dot3((high_t[cuts[p], :], low_t[cuts[p], :]), (high[:, cuts[q]], low[:, cuts[q]]))
        corner[at] = value + before[1][at] if before else value
    for copy in leaving:
        copy.wait()


def gram(inner, pieces, before, after):
    panels, rows, width = pieces[0].shape
    count = len(pieces) // 4
    total, full = len(pieces) * rows, panels * width
    corners = len(pairs_of(panels))
    outs = [shape((panels, width, width)), shape((corners, width, width)), shape((total, full), BF16), shape((total, full), BF16)]
    near = [pltpu.with_memory_space_constraint(array, pltpu.VMEM) for array in before or ()]
    far = list(pieces) + ([] if after is None else [after])

    def body(*refs):
        if near:
            gram_kernel(inner, count, refs[:2], *refs[2:])
        else:
            gram_kernel(inner, count, (), *refs)

    if after is not None and not near:
        body_first = body
        body = lambda *refs: body_first(*refs[:4 * count], *refs[4 * count + 1:])
    return call(
        body, "gram", outs, (*near, *far), far=len(far), far_outs=2, copies=4 * count + 2, aliases={0: 0, 1: 1} if near else None,
        scratch=[
            pltpu.VMEM((len(pieces), panels, rows, width), F32), pltpu.VMEM((total, full), BF16), pltpu.VMEM((total, full), BF16),
            pltpu.VMEM((full, total), BF16), pltpu.VMEM((full, total), BF16),
        ],
        flops=6 * (panels + corners) * width * width * total, mib=32, near_pinned=True,
    )


def invert_kernel(own, other, inverse):
    panels, order, _ = own.shape
    row = lax.broadcasted_iota(jnp.int32, (order, order), 0)
    col = lax.broadcasted_iota(jnp.int32, (order, order), 1)
    on_diag, upper = row == col, row < col
    identity = jnp.where(on_diag, 1.0, 0.0).astype(F32)
    strict, scale = [], []
    for p in range(panels):
        gram_sum = own[p] + other[p]
        half = jnp.where(on_diag, 0.5 * gram_sum, 0.0)
        by_row = 1.0 / jnp.sum(half, axis=1, keepdims=True)
        by_col = 1.0 / jnp.sum(half, axis=0, keepdims=True)
        strict.append(jnp.where(upper, gram_sum * by_row, 0.0))
        scale.append(by_col)

    def multiply(left, right):
        return dot3(halves(left), halves(right))

    size = 16
    same = (row // size) == (col // size)
    power = [jnp.where(same, -value, 0.0) for value in strict]
    accum = [identity + value for value in power]
    for _ in range(3):
        power = [multiply(value, value) for value in power]
        accum = [value + multiply(value, extra) for value, extra in zip(accum, power)]
    while size < order:
        wider = (row // (2 * size)) == (col // (2 * size))
        mask = jnp.logical_and(wider, jnp.logical_not((row // size) == (col // size)))
        uppers = [jnp.concatenate([v[k:k + size] for k in range(0, order, 2 * size)], axis=0) for v in accum]
        part = [multiply(value, jnp.where(mask, edge, 0.0)) for value, edge in zip(uppers, strict)]
        uppers = [u - multiply(edge, value) for u, edge, value in zip(uppers, part, accum)]
        accum = [
            jnp.concatenate(
                [x for k in range(order // (2 * size)) for x in (u[k * size:(k + 1) * size], v[(2 * k + 1) * size:(2 * k + 2) * size])],
                axis=0,
            )
            for u, v in zip(uppers, accum)
        ]
        size *= 2
    for p in range(panels):
        inverse[p] = accum[p] * scale[p]


def invert(own, other):
    own, other = (pltpu.with_memory_space_constraint(value, pltpu.VMEM) for value in (own, other))
    return call(invert_kernel, "invert", [shape(own.shape)], (own, other), flops=5 * 10**9, near_pinned=True)[0]


def place_of(inner, chunk, by_x, by_y):
    row, col = lax.axis_index("row"), lax.axis_index("col")
    return jnp.bitwise_xor(row // inner, by_x), jnp.bitwise_xor(col % LOW, chunk * 2 + by_y)


def project_kernel(inner, parts, *refs):
    arrays, (slab, product, left, held, held_slab, sems) = refs[:len(parts) * 2], refs[len(parts) * 2:]
    rows = slab.shape[1]
    chunk_rows = 4 * rows
    pairs, at = [(slab, held_slab)], 0
    for part, chunks in enumerate(parts):
        for chunk in range(chunks):
            cut = slice(chunk * chunk_rows, (chunk + 1) * chunk_rows)
            pairs += [(arrays[2 * part + k].at[cut, :], held.at[k, at]) for k in range(2)]
            at += 1
    copies = start_copies(pairs, sems)
    copies[0].wait()
    total = None
    for chunk in range(CHUNKS):
        for at in range(4):
            outer, low = place_of(inner, chunk, at // 2, at % 2)
            left[:, at * rows:(at + 1) * rows] = held_slab[outer * LOW + low].T
        high, rest = halves(left[...])
        copies[1 + 2 * chunk].wait()
        copies[2 + 2 * chunk].wait()
        value = dot(high, held[0, chunk]) + (dot(high, held[1, chunk]) + dot(rest, held[0, chunk]))
        total = value if total is None else total + value
    product[...] = total


def project(inner, arrays, slab):
    full = arrays[0].shape[1]
    parts = [array.shape[0] // (4 * slab.shape[1]) for array in arrays[::2]]
    total = 4 * slab.shape[1]
    return call(
        functools.partial(project_kernel, inner, parts), "project", [shape((BW, full))], (*pinned(arrays), slab), far=len(arrays) + 1,
        scratch=[pltpu.VMEM((BW, total), F32), pltpu.VMEM((2, CHUNKS, total, full), BF16), pltpu.VMEM(slab.shape, F32)],
        copies=2 * CHUNKS + 1, flops=6 * full * total * CHUNKS * BW,
    )[0]


def copies_of_half(by_x, parts, arrays, rows, held):
    pairs, at = [], 0
    for part, chunks in enumerate(parts):
        for chunk in range(chunks):
            cut = slice((4 * chunk + 2 * by_x) * rows, (4 * chunk + 2 * by_x + 2) * rows)
            pairs += [(arrays[2 * part + k].at[cut, :], held.at[k, at]) for k in range(2)]
            at += 1
    return pairs


def change(inner, by_x, chunk, held, wide, slab, result):
    rows = slab.shape[1]
    main = dot(held[0, chunk], wide[...])
    delta = main[:, :BW] + (main[:, BW:] + dot(held[1, chunk], wide[:, :BW]))
    for by_y in range(2):
        outer, low_at = place_of(inner, chunk, by_x, by_y)
        result[low_at] = slab[outer * LOW + low_at] - delta[by_y * rows:(by_y + 1) * rows, :]


def solve_kernel(inner, parts, own, other, inverse, *refs):
    (corner_own, corner_other), refs = refs[:2], refs[2:]
    arrays, (slab, away, wide, held_own, held_other, held, held_slab, sems) = refs[:len(parts) * 2], refs[len(parts) * 2:]
    panels, width, _ = inverse.shape
    pairs = pairs_of(panels)
    copies = start_copies(
        [(corner_own, held_own), (corner_other, held_other), (slab, held_slab)] + copies_of_half(1, parts, arrays, slab.shape[1], held), sems
    )
    solved = [None] * panels
    for p in reversed(range(panels)):
        cut = slice(p * width, (p + 1) * width)
        value = (own[:, cut] + other[:, cut]).T
        if p == panels - 2:
            copies[0].wait()
            copies[1].wait()
        for at, (i, q) in enumerate(pairs):
            if i == p:
                value = value - dot3(halves(held_own[at] + held_other[at]), solved[q])
        value = dot3(halves(inverse[p]), halves(value))
        solved[p] = halves(value)
        wide[cut, :BW] = solved[p][0]
        wide[cut, BW:] = solved[p][1]
    copies[2].wait()
    for chunk in range(CHUNKS):
        copies[3 + 2 * chunk].wait()
        copies[4 + 2 * chunk].wait()
        change(inner, 1, chunk, held, wide, held_slab, away)


def keep_kernel(inner, parts, wide, *refs):
    arrays, (slab, keep, held, held_slab, sems) = refs[:len(parts) * 2], refs[len(parts) * 2:]
    copies = start_copies([(slab, held_slab)] + copies_of_half(0, parts, arrays, slab.shape[1], held), sems)
    copies[0].wait()
    for chunk in range(CHUNKS):
        copies[1 + 2 * chunk].wait()
        copies[2 + 2 * chunk].wait()
        change(inner, 0, chunk, held, wide, held_slab, keep)


def on_device(rows, cols, vectors, reflectors, owner_list, slot_list):
    inner = rows // 2
    extra = cols // LOW
    local_rows = vectors.shape[0] // cols
    panels = reflectors.shape[0]

    def at(row, col):
        return row * cols + col

    def send(value, change_of):
        perm = [(at(r, c), at(*change_of(r, c))) for r in range(rows) for c in range(cols)]
        return lax.ppermute(value, ("row", "col"), perm)

    def by_z(step):
        return lambda r, c: (r, c ^ (2 * step))

    def by_first(r, c):
        return (r, c ^ 1) if (r % inner) % 2 == 0 else ((r + inner) % rows, c)

    def by_second(r, c):
        return (r, c ^ 1) if (r % inner) % 2 == 1 else ((r + inner) % rows, c)

    own = reflectors
    if extra > 1:
        groups = [[e * LOW + low for e in range(extra)] for low in range(LOW)]
        own = lax.all_gather(own, "col", axis=1, tiled=True, axis_index_groups=groups)
    def after(value, *others):
        return lax.optimization_barrier((value, *others))[0]

    start = [own, send(own, by_z(1)), send(own, by_z(2))]
    start.append(send(start[2], by_z(1)))
    first, second, both = [], [], []
    first.append(send(start[0], by_first))
    second.append(send(start[0], by_second))
    both.append(send(first[0], by_second))
    first.append(send(start[1], by_first))
    second.append(send(start[1], by_second))
    both.append(send(first[1], by_second))
    vectors = after(vectors, start[1], start[2], first[0], second[0])
    spread = lax.all_to_all(vectors.reshape(cols, local_rows, -1), "col", split_axis=0, concat_axis=0, tiled=True)
    ordered = reorder(spread, owner_list, slot_list)
    first.append(send(start[2], by_first))
    second.append(send(start[2], by_second))
    both.append(send(first[2], by_second))
    first.append(send(start[3], by_first))
    second.append(send(start[3], by_second))
    both.append(send(first[3], by_second))
    groups = [[at(o * inner + i, c) for o in range(2) for c in range(cols)] for i in range(inner)]
    slab = lax.all_to_all(ordered, ("row", "col"), split_axis=0, concat_axis=0, tiled=True, axis_index_groups=groups)
    slab = slab.reshape(2, extra, LOW, local_rows, BW).transpose(0, 2, 1, 3, 4)
    slab = slab.reshape(2 * LOW, extra * local_rows, BW)

    pieces = [(start[chunk], first[chunk], second[chunk], both[chunk]) for chunk in range(CHUNKS)]
    parts = (3, 1)
    arrays, sums = (), None
    *sums, high, low = gram(inner, sum(pieces[0:3], ()), None, ordered)
    arrays += (high, low)
    *sums, high, low = gram(inner, sum(pieces[3:4], ()), sums, None)
    arrays += (high, low)
    diag, corner = sums

    def over_inner(value, bit):
        return send(value, lambda r, c: (r ^ bit, c))

    bits = [1 << k for k in range(inner.bit_length() - 1)]
    for bit in bits[:-1]:
        diag, corner = (value + over_inner(value, bit) for value in (diag, corner))
    bit = bits[-1]
    diag_other = over_inner(diag, bit)
    inverse = invert(diag, diag_other)
    product = project(inner, arrays, slab)
    for step in bits[:-1]:
        product = product + over_inner(product, step)
    full, half_rows, block = product.shape[1], 2 * slab.shape[1], shape((LOW,) + slab.shape[1:])
    half_held = [pltpu.VMEM((2, CHUNKS, half_rows, full), BF16), pltpu.VMEM(slab.shape, F32)]
    away, wide = call(
        functools.partial(solve_kernel, inner, parts), "solve", [block, shape((full, 2 * BW), BF16)],
        (product, over_inner(product, bit), inverse, corner, over_inner(corner, bit), *pinned(arrays), slab),
        far=len(arrays) + 3, copies=2 * CHUNKS + 3, scratch=[pltpu.VMEM(corner.shape, F32)] * 2 + half_held, flops=3 * 10**9,
    )
    back = send(away, lambda r, c: ((r + inner) % rows, c))
    keep, = call(
        functools.partial(keep_kernel, inner, parts), "keep", [block], (wide, *pinned(arrays), slab),
        far=len(arrays) + 1, copies=2 * CHUNKS + 1, scratch=half_held, flops=10**9,
    )
    outer = lax.axis_index("row") // inner

    def natural(value):
        return value.reshape(LOW, extra, local_rows, BW).transpose(1, 0, 2, 3).reshape(vectors.shape[0], BW)

    keep, back = natural(keep), natural(back)
    is_first = outer == 0
    return jnp.concatenate([jnp.where(is_first, keep, back), jnp.where(is_first, back, keep)], axis=1)


def solution(mesh):
    return jax.shard_map(
        functools.partial(on_device, mesh.shape["row"], mesh.shape["col"]),
        mesh=mesh,
        in_specs=(P("row", "col"), P(None, ("row", "col"), None), P(), P()),
        out_specs=P("row", "col"),
        check_vma=False,
    )
```

time: 115 us -> 94.6 us (0.82)
  local copies, waits for them, and re-layouts: 13.2 us -> 1.31 us
  waiting for transfers between devices: 39.9 us -> 33.6 us
  starting transfers between devices: 32.8 us -> 29.7 us
  Pallas kernels: 27.2 us -> 28.6 us
    unnamed x32 -> x6, local copies, waits for them, and re-layouts: 13.2 us -> 1.31 us
    ppermute x19, waiting for transfers between devices: 38.9 us -> 33.6 us  [send(): return lax.ppermute(value, ('row', 'col'), perm)]
    all_to_all x1, starting transfers between devices: 7.28 us -> 3.86 us  [on_device(): lax.all_to_all(vectors.reshape(cols, local_rows, -1), 'col', split_axis=0...]
    pallas_call x6 -> x7, Pallas kernels: 27.2 us -> 28.6 us  [call(): pl.pallas_call(body, out_shape=tuple((pltpu.VMEM(out.shape, out.dtype) if...]
  transfers between devices with their start and end apart: 21 -> 21, of which waited for: 6 -> 10; matrix products, arithmetic and copies ran while one was open for 0% -> 0% of each run, Pallas kernels for 19% -> 25%
where the time goes in v2:
time: 94.6 us; the launch traced here: 94.1 us
  waiting for transfers between devices  33.6 us (36%)
  starting transfers between devices  29.7 us (31%)
  Pallas kernels  28.6 us (30%)
  local copies, waits for them, and re-layouts  1.31 us (1%)
    ppermute x19, waiting for transfers between devices, send(): return lax.ppermute(value, ('row', 'col'), perm)  33.6 us
    pallas_call x7, Pallas kernels, call(): pl.pallas_call(body, out_shape=tuple((pltpu.VMEM(out.shape, out.dtype) if...  28.6 us
    ppermute x19, starting transfers between devices, send(): return lax.ppermute(value, ('row', 'col'), perm)  21.7 us
    all_to_all x1, starting transfers between devices, on_device(): lax.all_to_all(ordered, ('row', 'col'), split_axis=0, concat_axis=0, tile...  4.08 us
    all_to_all x1, starting transfers between devices, on_device(): lax.all_to_all(vectors.reshape(cols, local_rows, -1), 'col', split_axis=0...  3.86 us
  transfers between devices with their start and end apart: 21, of which 10 were waited for; matrix products, arithmetic and copies ran while one was open for 0% of the time, Pallas kernels for 25%

profile of v2, /device:TPU:0, one launch (start us, length us, event | category | flops | bytes accessed | tf_op | source)
XLA Modules:
  0.0 94.1 jit_solution(5551478075943526698)
XLA Ops:
  0.0 3.0 %collective-permute-start = (f32[4,64,256]{2,1,0:T(8,128)}, f32[4,64,256]{2,1,0:T(8,128)S(1)}, u32[]{:S(2)}, u32[]{:S(2)}) collective-permute-start(f32[4,64,256]{2,1,0:T(8,128)} %refs_0_.1), channel_id=1, source_target_pairs={{0,1},{1,0},{2,3},{3,2},{4,5},{5,4},{6,7},{7,6},{8,24},{9,25},{10,... | collective-permute-start | bytes 786440 | tf_op jit(solution)/shard_map/ppermute | solution.py:322
  3.0 1.5 %collective-permute-start.1 = (f32[4,64,256]{2,1,0:T(8,128)}, f32[4,64,256]{2,1,0:T(8,128)S(1)}, u32[]{:S(2)}, u32[]{:S(2)}) collective-permute-start(f32[4,64,256]{2,1,0:T(8,128)} %refs_0_.1), channel_id=1, source_target_pairs={{0,16},{1,17},{2,18},{3,19},{4,20},{5,21},{6,22},{7,23},{8,9},{9,8... | collective-permute-start | bytes 786440 | tf_op jit(solution)/shard_map/ppermute | solution.py:322
  4.5 1.6 %collective-permute-start.3 = (f32[4,64,256]{2,1,0:T(8,128)}, f32[4,64,256]{2,1,0:T(8,128)S(1)}, u32[]{:S(2)}, u32[]{:S(2)}) collective-permute-start(f32[4,64,256]{2,1,0:T(8,128)} %refs_0_.1), channel_id=1, source_target_pairs={{0,2},{1,3},{2,0},{3,1},{4,6},{5,7},{6,4},{7,5},{8,10},{9,11},{10,... | collective-permute-start | bytes 786440 | tf_op jit(solution)/shard_map/ppermute | solution.py:322
  6.0 2.6 %collective-permute-start.7 = (f32[4,64,256]{2,1,0:T(8,128)}, f32[4,64,256]{2,1,0:T(8,128)S(1)}, u32[]{:S(2)}, u32[]{:S(2)}) collective-permute-start(f32[4,64,256]{2,1,0:T(8,128)} %refs_0_.1), channel_id=1, source_target_pairs={{0,4},{1,5},{2,6},{3,7},{4,0},{5,1},{6,2},{7,3},{8,12},{9,13},{10,... | collective-permute-start | bytes 786440 | tf_op jit(solution)/shard_map/ppermute | solution.py:322
  8.6 1.3 %collective-permute-done.refs_1_ = f32[4,64,256]{2,1,0:T(8,128)S(1)} collective-permute-done((f32[4,64,256]{2,1,0:T(8,128)}, f32[4,64,256]{2,1,0:T(8,128)S(1)}, u32[]{:S(2)}, u32[]{:S(2)}) %collective-permute-start) | collective-permute-done | bytes 262176 | tf_op jit(solution)/shard_map/ppermute | solution.py:322
  9.9 7.7 %collective-permute-done.3.refs_4_ = f32[4,64,256]{2,1,0:T(8,128)S(1)} collective-permute-done((f32[4,64,256]{2,1,0:T(8,128)}, f32[4,64,256]{2,1,0:T(8,128)S(1)}, u32[]{:S(2)}, u32[]{:S(2)}) %collective-permute-start.3) | collective-permute-done | bytes 262176 | tf_op jit(solution)/shard_map/ppermute | solution.py:322
  17.6 2.4 %collective-permute-done.7.refs_8_ = f32[4,64,256]{2,1,0:T(8,128)S(1)} collective-permute-done((f32[4,64,256]{2,1,0:T(8,128)}, f32[4,64,256]{2,1,0:T(8,128)S(1)}, u32[]{:S(2)}, u32[]{:S(2)}) %collective-permute-start.7) | collective-permute-done | bytes 262176 | tf_op jit(solution)/shard_map/ppermute | solution.py:322
  20.0 3.9 %all-to-all-start = ((f32[8,64,256]{2,1,0:T(8,128)}), f32[8,64,256]{2,1,0:T(8,128)S(1)}, u32[]{:S(2)}, u32[]{:S(2)}) async-start(f32[8,64,256]{2,1,0:T(8,128)} %bitcast.5), calls=%async_computation | async-start | bytes 1048576 | tf_op jit(solution)/shard_map/all_to_all | solution.py:350
  24.4 2.0 %collective-permute-start.11 = (f32[4,64,256]{2,1,0:T(8,128)S(1)}, f32[4,64,256]{2,1,0:T(8,128)S(1)}, u32[]{:S(2)}, u32[]{:S(2)}) collective-permute-start(f32[4,64,256]{2,1,0:T(8,128)S(1)} %collective-permute-done.7.refs_8_), channel_id=1, source_target_pairs={{0,2},{1,3},{2,0},{3,1},{4,6},{5,7},{6,4},{7,5},{8,10},{9,11},{10,... | collective-permute-start | bytes 786440 | tf_op jit(solution)/shard_map/ppermute | solution.py:322
  26.5 1.5 %collective-permute-start.4 = (f32[4,64,256]{2,1,0:T(8,128)S(1)}, f32[4,64,256]{2,1,0:T(8,128)S(1)}, u32[]{:S(2)}, u32[]{:S(2)}) collective-permute-start(f32[4,64,256]{2,1,0:T(8,128)S(1)} %collective-permute-done.3.refs_4_), channel_id=1, source_target_pairs={{0,1},{1,0},{2,3},{3,2},{4,5},{5,4},{6,7},{7,6},{8,24},{9,25},{10,... | collective-permute-start | bytes 786440 | tf_op jit(solution)/shard_map/ppermute | solution.py:322
  28.5 1.5 %collective-permute-start.5 = (f32[4,64,256]{2,1,0:T(8,128)S(1)}, f32[4,64,256]{2,1,0:T(8,128)S(1)}, u32[]{:S(2)}, u32[]{:S(2)}) collective-permute-start(f32[4,64,256]{2,1,0:T(8,128)S(1)} %collective-permute-done.3.refs_4_), channel_id=1, source_target_pairs={{0,16},{1,17},{2,18},{3,19},{4,20},{5,21},{6,22},{7,23},{8,9},{9,8... | collective-permute-start | bytes 786440 | tf_op jit(solution)/shard_map/ppermute | solution.py:322
  30.0 3.2 %collective-permute-done.2.refs_3_ = f32[4,64,256]{2,1,0:T(8,128)S(1)} collective-permute-done((f32[4,64,256]{2,1,0:T(8,128)S(1)}, f32[4,64,256]{2,1,0:T(8,128)S(1)}, u32[]{:S(2)}, u32[]{:S(2)}) %collective-permute-start.2) | collective-permute-done | bytes 262176 | tf_op jit(solution)/shard_map/ppermute | solution.py:322
  33.7 3.7 %collective-permute-done.11.refs_2_ = f32[4,64,256]{2,1,0:T(8,128)S(1)} collective-permute-done((f32[4,64,256]{2,1,0:T(8,128)S(1)}, f32[4,64,256]{2,1,0:T(8,128)S(1)}, u32[]{:S(2)}, u32[]{:S(2)}) %collective-permute-start.11) | collective-permute-done | bytes 262176 | tf_op jit(solution)/shard_map/ppermute | solution.py:322
  37.4 1.1 %collective-permute-start.12 = (f32[4,64,256]{2,1,0:T(8,128)S(1)}, f32[4,64,256]{2,1,0:T(8,128)S(1)}, u32[]{:S(2)}, u32[]{:S(2)}) collective-permute-start(f32[4,64,256]{2,1,0:T(8,128)S(1)} %collective-permute-done.11.refs_2_), channel_id=1, source_target_pairs={{0,1},{1,0},{2,3},{3,2},{4,5},{5,4},{6,7},{7,6},{8,24},{9,25},{10,... | collective-permute-start | bytes 786440 | tf_op jit(solution)/shard_map/ppermute | solution.py:322
  39.0 4.4 %collective-permute-done.8.refs_9_ = f32[4,64,256]{2,1,0:T(8,128)S(1)} collective-permute-done((f32[4,64,256]{2,1,0:T(8,128)S(1)}, f32[4,64,256]{2,1,0:T(8,128)S(1)}, u32[]{:S(2)}, u32[]{:S(2)}) %collective-permute-start.8) | collective-permute-done | bytes 262176 | tf_op jit(solution)/shard_map/ppermute | solution.py:322
  43.4 1.1 %collective-permute-start.10 = (f32[4,64,256]{2,1,0:T(8,128)S(1)}, f32[4,64,256]{2,1,0:T(8,128)}, u32[]{:S(2)}, u32[]{:S(2)}) collective-permute-start(f32[4,64,256]{2,1,0:T(8,128)S(1)} %collective-permute-done.8.refs_9_), channel_id=1, source_target_pairs={{0,16},{1,17},{2,18},{3,19},{4,20},{5,21},{6,22},{7,23},{8,9},{9,8... | collective-permute-start | bytes 786440 | tf_op jit(solution)/shard_map/ppermute | solution.py:322
  44.6 0.7 copy-done
  45.2 0.7 copy-done.1
  45.9 1.8 %reorder.1.refs_12_ = f32[16,64,128]{2,1,0:T(8,128)} custom-call(s32[16]{0:T(128)S(1)} %copy-done, s32[16]{0:T(128)S(1)} %copy-done.1, f32[8,64,256]{2,1,0:T(8,128)S(1)} %all-to-all-done.spread), custom_call_target="tpu_custom_call" | custom-call | bytes 4194304 | tf_op jit(solution)/shard_map/reorder/pallas_call | solution.py:32
  47.7 4.1 %all-to-all-start.1 = ((f32[16,64,128]{2,1,0:T(8,128)}), f32[16,64,128]{2,1,0:T(8,128)S(1)}, u32[]{:S(2)}, u32[]{:S(2)}) async-start(f32[16,64,128]{2,1,0:T(8,128)} %reorder.1.refs_12_), calls=%async_computation.1 | async-start | bytes 1048576 | tf_op jit(solution)/shard_map/all_to_all | solution.py:359
  51.8 2.0 %collective-permute-start.13 = (f32[4,64,256]{2,1,0:T(8,128)S(1)}, f32[4,64,256]{2,1,0:T(8,128)S(1)}, u32[]{:S(2)}, u32[]{:S(2)}) collective-permute-start(f32[4,64,256]{2,1,0:T(8,128)S(1)} %collective-permute-done.11.refs_2_), channel_id=1, source_target_pairs={{0,16},{1,17},{2,18},{3,19},{4,20},{5,21},{6,22},{7,23},{8,9},{9,8... | collective-permute-start | bytes 786440 | tf_op jit(solution)/shard_map/ppermute | solution.py:322
  53.9 6.2 %gram.2 = (f32[4,256,256]{2,1,0:T(8,128)}, f32[6,256,256]{2,1,0:T(8,128)}, bf16[768,1024]{1,0:T(8,128)(2,1)}, bf16[768,1024]{1,0:T(8,128)(2,1)}) custom-call(f32[4,64,256]{2,1,0:T(8,128)S(1)} %copy-done.2, f32[4,64,256]{2,1,0:T(8,128)S(1)} %collective-permute-done.refs_1_, f32[4,64,256]{2,1,0:T(8,128)S(1)} %collective-permute-done.1.refs_2_, ...), custom_call_target="tpu_custom_call" | custom-call | flops 3019898880 | bytes 4194304 | tf_op jit(solution)/shard_map/gram/pallas_call | solution.py:32
  60.6 3.3 %collective-permute-done.14.refs_5_ = f32[4,64,256]{2,1,0:T(8,128)S(1)} collective-permute-done((f32[4,64,256]{2,1,0:T(8,128)S(1)}, f32[4,64,256]{2,1,0:T(8,128)S(1)}, u32[]{:S(2)}, u32[]{:S(2)}) %collective-permute-start.14) | collective-permute-done | bytes 262176 | tf_op jit(solution)/shard_map/ppermute | solution.py:322
  63.9 4.7 %gram.3 = (f32[4,256,256]{2,1,0:T(8,128)}, f32[6,256,256]{2,1,0:T(8,128)}, bf16[256,1024]{1,0:T(8,128)(2,1)}, bf16[256,1024]{1,0:T(8,128)(2,1)}) custom-call(f32[4,256,256]{2,1,0:T(8,128)} %get-tuple-element.19.refs_0_, f32[6,256,256]{2,1,0:T(8,128)} %get-tuple-element.20.refs_1_, ...), custom_call_target="tpu_custom_call", output_to_operand_aliasing={{0}: (0, {}), {1}: (1, {})} | custom-call | flops 1006632960 | bytes 4194304 | tf_op jit(solution)/shard_map/gram/pallas_call | solution.py:32
  69.2 2.6 %project.1.own = f32[128,1024]{1,0:T(8,128)S(1)} custom-call(bf16[768,1024]{1,0:T(8,128)(2,1)} %get-tuple-element.17.refs_0_.refs_2_, bf16[768,1024]{1,0:T(8,128)(2,1)} %get-tuple-element.18.refs_1_.refs_3_, bf16[256,1024]{1,0:T(8,128)(2,1)} %get-tuple-element.21.refs_2_.refs_4_, bf16[256,1024]{1,0:T(8,128)(2,1)} %get-tuple-element.22.refs_3_.refs_5_, ...), custom_call_target="tpu_custom_call" | custom-call | flops 805306368 | bytes 4194304 | tf_op jit(solution)/shard_map/project/pallas_call | solution.py:32
  72.0 2.0 %collective-permute-done.16.other = f32[4,256,256]{2,1,0:T(8,128)} collective-permute-done((f32[4,256,256]{2,1,0:T(8,128)}, f32[4,256,256]{2,1,0:T(8,128)}, u32[]{:S(2)}, u32[]{:S(2)}) %collective-permute-start.16) | collective-permute-done | bytes 1048608 | tf_op jit(solution)/shard_map/ppermute | solution.py:322
  74.0 6.2 %invert.1.inverse = f32[4,256,256]{2,1,0:T(8,128)S(1)} custom-call(f32[4,256,256]{2,1,0:T(8,128)} %get-tuple-element.23.own, f32[4,256,256]{2,1,0:T(8,128)} %collective-permute-done.16.other), custom_call_target="tpu_custom_call" | custom-call | flops 5000000000 | bytes 4194304 | tf_op jit(solution)/shard_map/invert/pallas_call | solution.py:32
  80.2 4.7 %solve.1 = (f32[8,64,128]{2,1,0:T(8,128)S(1)}, bf16[1024,256]{1,0:T(8,128)(2,1)S(1)}) custom-call(f32[128,1024]{1,0:T(8,128)S(1)} %project.1.own, f32[128,1024]{1,0:T(8,128)S(1)} %collective-permute-done.15.other, f32[4,256,256]{2,1,0:T(8,128)S(1)} %invert.1.inverse, f32[6,256,256]{2,1,0:T(8,128)} %get-tuple-element.24.refs_0_, ...), custom_call_target="tpu_custom_call" | custom-call | flops 3000000000 | bytes 4194304 | tf_op jit(solution)/shard_map/solve/pallas_call | solution.py:32
  84.8 0.9 collective-permute-start.18
  85.7 2.4 %keep.1 = f32[8,64,128]{2,1,0:T(8,128)S(1)} custom-call(bf16[1024,256]{1,0:T(8,128)(2,1)S(1)} %get-tuple-element.25.wide, bf16[768,1024]{1,0:T(8,128)(2,1)} %get-tuple-element.17.refs_0_.refs_2_, bf16[768,1024]{1,0:T(8,128)(2,1)} %get-tuple-element.18.refs_1_.refs_3_, bf16[256,1024]{1,0:T(8,128)(2,1)} %get-tuple-element.21.refs_2_.refs_4_, ...), custom_call_target="tpu_custom_call" | custom-call | flops 1000000000 | bytes 4194304 | tf_op jit(solution)/shard_map/keep/pallas_call | solution.py:32
  88.1 5.1 %collective-permute-done.18 = f32[8,64,128]{2,1,0:T(8,128)S(1)} collective-permute-done((f32[8,64,128]{2,1,0:T(8,128)S(1)}, f32[8,64,128]{2,1,0:T(8,128)S(1)}, u32[]{:S(2)}, u32[]{:S(2)}) %collective-permute-start.18) | collective-permute-done | bytes 262176 | tf_op jit(solution)/shard_map/ppermute | solution.py:322
  93.3 0.8 pad_maximum_fusion
  (25 shorter events, 3.5 us)
Async XLA Ops:
  0.0 9.9 %collective-permute-start = (f32[4,64,256]{2,1,0:T(8,128)}, f32[4,64,256]{2,1,0:T(8,128)S(1)}, u32[]{:S(2)}, u32[]{:S(2)}) collective-permute-start(f32[4,64,256]{2,1,0:T(8,128)} %refs_0_.1), channel_id=1, source_target_pairs={{0,1},{1,0},{2,3},{3,2},{4,5},{5,4},{6,7},{7,6},{8,24},{9,25},{10,... | collective-permute-start | bytes 786440 | tf_op jit(solution)/shard_map/ppermute | solution.py:322
  3.0 6.9 %collective-permute-start.1 = (f32[4,64,256]{2,1,0:T(8,128)}, f32[4,64,256]{2,1,0:T(8,128)S(1)}, u32[]{:S(2)}, u32[]{:S(2)}) collective-permute-start(f32[4,64,256]{2,1,0:T(8,128)} %refs_0_.1), channel_id=1, source_target_pairs={{0,16},{1,17},{2,18},{3,19},{4,20},{5,21},{6,22},{7,23},{8,9},{9,8... | collective-permute-start | bytes 786440 | tf_op jit(solution)/shard_map/ppermute | solution.py:322
  4.5 13.2 %collective-permute-start.3 = (f32[4,64,256]{2,1,0:T(8,128)}, f32[4,64,256]{2,1,0:T(8,128)S(1)}, u32[]{:S(2)}, u32[]{:S(2)}) collective-permute-start(f32[4,64,256]{2,1,0:T(8,128)} %refs_0_.1), channel_id=1, source_target_pairs={{0,2},{1,3},{2,0},{3,1},{4,6},{5,7},{6,4},{7,5},{8,10},{9,11},{10,... | collective-permute-start | bytes 786440 | tf_op jit(solution)/shard_map/ppermute | solution.py:322
  6.0 14.0 %collective-permute-start.7 = (f32[4,64,256]{2,1,0:T(8,128)}, f32[4,64,256]{2,1,0:T(8,128)S(1)}, u32[]{:S(2)}, u32[]{:S(2)}) collective-permute-start(f32[4,64,256]{2,1,0:T(8,128)} %refs_0_.1), channel_id=1, source_target_pairs={{0,4},{1,5},{2,6},{3,7},{4,0},{5,1},{6,2},{7,3},{8,12},{9,13},{10,... | collective-permute-start | bytes 786440 | tf_op jit(solution)/shard_map/ppermute | solution.py:322
  20.0 33.9 %copy-start.2 = (f32[4,64,256]{2,1,0:T(8,128)S(1)}, f32[4,64,256]{2,1,0:T(8,128)}, u32[]{:S(2)}) copy-start(f32[4,64,256]{2,1,0:T(8,128)} %refs_0_.1) | copy-start | bytes 786436
  20.0 24.5 %all-to-all-start = ((f32[8,64,256]{2,1,0:T(8,128)}), f32[8,64,256]{2,1,0:T(8,128)S(1)}, u32[]{:S(2)}, u32[]{:S(2)}) async-start(f32[8,64,256]{2,1,0:T(8,128)} %bitcast.5), calls=%async_computation | async-start | bytes 1048576 | tf_op jit(solution)/shard_map/all_to_all | solution.py:350
  23.9 9.2 %collective-permute-start.2 = (f32[4,64,256]{2,1,0:T(8,128)S(1)}, f32[4,64,256]{2,1,0:T(8,128)S(1)}, u32[]{:S(2)}, u32[]{:S(2)}) collective-permute-start(f32[4,64,256]{2,1,0:T(8,128)S(1)} %collective-permute-done.refs_1_), channel_id=1, source_target_pairs={{0,16},{1,17},{2,18},{3,19},{4,20},{5,21},{6,22},{7,23},{8,9},{9,8... | collective-permute-start | bytes 786440 | tf_op jit(solution)/shard_map/ppermute | solution.py:322
  24.4 13.0 %collective-permute-start.11 = (f32[4,64,256]{2,1,0:T(8,128)S(1)}, f32[4,64,256]{2,1,0:T(8,128)S(1)}, u32[]{:S(2)}, u32[]{:S(2)}) collective-permute-start(f32[4,64,256]{2,1,0:T(8,128)S(1)} %collective-permute-done.7.refs_8_), channel_id=1, source_target_pairs={{0,2},{1,3},{2,0},{3,1},{4,6},{5,7},{6,4},{7,5},{8,10},{9,11},{10,... | collective-permute-start | bytes 786440 | tf_op jit(solution)/shard_map/ppermute | solution.py:322
  26.5 12.1 %collective-permute-start.4 = (f32[4,64,256]{2,1,0:T(8,128)S(1)}, f32[4,64,256]{2,1,0:T(8,128)S(1)}, u32[]{:S(2)}, u32[]{:S(2)}) collective-permute-start(f32[4,64,256]{2,1,0:T(8,128)S(1)} %collective-permute-done.3.refs_4_), channel_id=1, source_target_pairs={{0,1},{1,0},{2,3},{3,2},{4,5},{5,4},{6,7},{7,6},{8,24},{9,25},{10,... | collective-permute-start | bytes 786440 | tf_op jit(solution)/shard_map/ppermute | solution.py:322
  27.9 15.5 %collective-permute-start.8 = (f32[4,64,256]{2,1,0:T(8,128)S(1)}, f32[4,64,256]{2,1,0:T(8,128)S(1)}, u32[]{:S(2)}, u32[]{:S(2)}) collective-permute-start(f32[4,64,256]{2,1,0:T(8,128)S(1)} %collective-permute-done.7.refs_8_), channel_id=1, source_target_pairs={{0,1},{1,0},{2,3},{3,2},{4,5},{5,4},{6,7},{7,6},{8,24},{9,25},{10,... | collective-permute-start | bytes 786440 | tf_op jit(solution)/shard_map/ppermute | solution.py:322
  28.5 23.3 %collective-permute-start.5 = (f32[4,64,256]{2,1,0:T(8,128)S(1)}, f32[4,64,256]{2,1,0:T(8,128)S(1)}, u32[]{:S(2)}, u32[]{:S(2)}) collective-permute-start(f32[4,64,256]{2,1,0:T(8,128)S(1)} %collective-permute-done.3.refs_4_), channel_id=1, source_target_pairs={{0,16},{1,17},{2,18},{3,19},{4,20},{5,21},{6,22},{7,23},{8,9},{9,8... | collective-permute-start | bytes 786440 | tf_op jit(solution)/shard_map/ppermute | solution.py:322
  33.1 20.8 %collective-permute-start.9 = (f32[4,64,256]{2,1,0:T(8,128)S(1)}, f32[4,64,256]{2,1,0:T(8,128)}, u32[]{:S(2)}, u32[]{:S(2)}) collective-permute-start(f32[4,64,256]{2,1,0:T(8,128)S(1)} %collective-permute-done.7.refs_8_), channel_id=1, source_target_pairs={{0,16},{1,17},{2,18},{3,19},{4,20},{5,21},{6,22},{7,23},{8,9},{9,8... | collective-permute-start | bytes 786440 | tf_op jit(solution)/shard_map/ppermute | solution.py:322
  37.4 16.4 %collective-permute-start.12 = (f32[4,64,256]{2,1,0:T(8,128)S(1)}, f32[4,64,256]{2,1,0:T(8,128)S(1)}, u32[]{:S(2)}, u32[]{:S(2)}) collective-permute-start(f32[4,64,256]{2,1,0:T(8,128)S(1)} %collective-permute-done.11.refs_2_), channel_id=1, source_target_pairs={{0,1},{1,0},{2,3},{3,2},{4,5},{5,4},{6,7},{7,6},{8,24},{9,25},{10,... | collective-permute-start | bytes 786440 | tf_op jit(solution)/shard_map/ppermute | solution.py:322
  38.5 15.4 %collective-permute-start.6 = (f32[4,64,256]{2,1,0:T(8,128)S(1)}, f32[4,64,256]{2,1,0:T(8,128)}, u32[]{:S(2)}, u32[]{:S(2)}) collective-permute-start(f32[4,64,256]{2,1,0:T(8,128)S(1)} %collective-permute-done.4.refs_5_), channel_id=1, source_target_pairs={{0,16},{1,17},{2,18},{3,19},{4,20},{5,21},{6,22},{7,23},{8,9},{9,8... | collective-permute-start | bytes 786440 | tf_op jit(solution)/shard_map/ppermute | solution.py:322
  43.4 10.5 %collective-permute-start.10 = (f32[4,64,256]{2,1,0:T(8,128)S(1)}, f32[4,64,256]{2,1,0:T(8,128)}, u32[]{:S(2)}, u32[]{:S(2)}) collective-permute-start(f32[4,64,256]{2,1,0:T(8,128)S(1)} %collective-permute-done.8.refs_9_), channel_id=1, source_target_pairs={{0,16},{1,17},{2,18},{3,19},{4,20},{5,21},{6,22},{7,23},{8,9},{9,8... | collective-permute-start | bytes 786440 | tf_op jit(solution)/shard_map/ppermute | solution.py:322
  44.6 0.7 copy-start
  45.2 0.7 copy-start.1
  47.7 21.5 %all-to-all-start.1 = ((f32[16,64,128]{2,1,0:T(8,128)}), f32[16,64,128]{2,1,0:T(8,128)S(1)}, u32[]{:S(2)}, u32[]{:S(2)}) async-start(f32[16,64,128]{2,1,0:T(8,128)} %reorder.1.refs_12_), calls=%async_computation.1 | async-start | bytes 1048576 | tf_op jit(solution)/shard_map/all_to_all | solution.py:359
  51.8 8.8 %collective-permute-start.13 = (f32[4,64,256]{2,1,0:T(8,128)S(1)}, f32[4,64,256]{2,1,0:T(8,128)S(1)}, u32[]{:S(2)}, u32[]{:S(2)}) collective-permute-start(f32[4,64,256]{2,1,0:T(8,128)S(1)} %collective-permute-done.11.refs_2_), channel_id=1, source_target_pairs={{0,16},{1,17},{2,18},{3,19},{4,20},{5,21},{6,22},{7,23},{8,9},{9,8... | collective-permute-start | bytes 786440 | tf_op jit(solution)/shard_map/ppermute | solution.py:322
  53.8 10.1 %collective-permute-start.14 = (f32[4,64,256]{2,1,0:T(8,128)S(1)}, f32[4,64,256]{2,1,0:T(8,128)S(1)}, u32[]{:S(2)}, u32[]{:S(2)}) collective-permute-start(f32[4,64,256]{2,1,0:T(8,128)S(1)} %collective-permute-done.12.refs_3_), channel_id=1, source_target_pairs={{0,16},{1,17},{2,18},{3,19},{4,20},{5,21},{6,22},{7,23},{8,9},{9,8... | collective-permute-start | bytes 786440 | tf_op jit(solution)/shard_map/ppermute | solution.py:322
  68.6 11.5 %collective-permute-start.17 = (f32[6,256,256]{2,1,0:T(8,128)}, f32[6,256,256]{2,1,0:T(8,128)S(1)}, u32[]{:S(2)}, u32[]{:S(2)}) collective-permute-start(f32[6,256,256]{2,1,0:T(8,128)} %get-tuple-element.24.refs_0_), channel_id=1, source_target_pairs={{0,8},{1,9},{2,10},{3,11},{4,12},{5,13},{6,14},{7,15},{8,0},{9,1},... | collective-permute-start | bytes 4718600 | tf_op jit(solution)/shard_map/ppermute | solution.py:322
  68.7 5.3 %collective-permute-start.16 = (f32[4,256,256]{2,1,0:T(8,128)}, f32[4,256,256]{2,1,0:T(8,128)}, u32[]{:S(2)}, u32[]{:S(2)}) collective-permute-start(f32[4,256,256]{2,1,0:T(8,128)} %get-tuple-element.23.own), channel_id=1, source_target_pairs={{0,8},{1,9},{2,10},{3,11},{4,12},{5,13},{6,14},{7,15},{8,0},{9,1},... | collective-permute-start | bytes 3145736 | tf_op jit(solution)/shard_map/ppermute | solution.py:322
  71.9 8.3 %collective-permute-start.15 = (f32[128,1024]{1,0:T(8,128)S(1)}, f32[128,1024]{1,0:T(8,128)S(1)}, u32[]{:S(2)}, u32[]{:S(2)}) collective-permute-start(f32[128,1024]{1,0:T(8,128)S(1)} %project.1.own), channel_id=1, source_target_pairs={{0,8},{1,9},{2,10},{3,11},{4,12},{5,13},{6,14},{7,15},{8,0},{9,1},... | collective-permute-start | bytes 1572872 | tf_op jit(solution)/shard_map/ppermute | solution.py:322
  84.8 8.4 %collective-permute-start.18 = (f32[8,64,128]{2,1,0:T(8,128)S(1)}, f32[8,64,128]{2,1,0:T(8,128)S(1)}, u32[]{:S(2)}, u32[]{:S(2)}) collective-permute-start(f32[8,64,128]{2,1,0:T(8,128)S(1)} %get-tuple-element.26), channel_id=1, source_target_pairs={{0,16},{1,17},{2,18},{3,19},{4,20},{5,21},{6,22},{7,23},{8,24},{9,... | collective-permute-start | bytes 786440 | tf_op jit(solution)/shard_map/ppermute | solution.py:322

commit v3 on v2

v3 whole, which is shorter than its diff:
```python
import functools

import jax
import jax.numpy as jnp
from jax import lax
from jax.experimental import pallas as pl
from jax.experimental.pallas import tpu as pltpu
from jax.sharding import PartitionSpec as P

BW = 128
BLK_DEV = 2
LOW = 8
CHUNKS = 4
F32, BF16 = jnp.float32, jnp.bfloat16


def vmem(count):
    return [pl.BlockSpec(memory_space=pltpu.VMEM)] * count


def smem(count):
    return [pl.BlockSpec(memory_space=pltpu.SMEM)] * count


def shape(dims, kind=F32):
    return jax.ShapeDtypeStruct(tuple(dims), kind)


def call(body, name, outs, inputs, scratch=(), scalars=0, far=0, far_outs=0, copies=0, aliases=None, flops=0, mib=16):
    near = len(inputs) - scalars - far
    any_space = pl.BlockSpec(memory_space=pl.ANY)
    return pl.pallas_call(
        body,
        out_shape=tuple(outs[:len(outs) - far_outs]) + tuple(pltpu.HBM(out.shape, out.dtype) for out in outs[len(outs) - far_outs:]),
        in_specs=smem(scalars) + vmem(near) + [any_space] * far,
        out_specs=tuple(vmem(len(outs) - far_outs) + [any_space] * far_outs),
        scratch_shapes=list(scratch) + ([pltpu.SemaphoreType.DMA((copies,))] if copies else []),
        input_output_aliases=aliases or {},
        compiler_params=pltpu.CompilerParams(vmem_limit_bytes=mib * 1024 * 1024),
        cost_estimate=pl.CostEstimate(flops=flops, bytes_accessed=4 * 1024 * 1024, transcendentals=0),
        name=name,
    )(*inputs)


def pinned(arrays):
    return [pltpu.with_memory_space_constraint(array, pltpu.HBM) for array in arrays]


def start_copies(pairs, sems, base=0):
    copies = [pltpu.make_async_copy(src, dst, sems.at[base + at]) for at, (src, dst) in enumerate(pairs)]
    for copy in copies:
        copy.start()
    return copies


def halves(value):
    high = value.astype(BF16)
    return high, (value - high.astype(F32)).astype(BF16)


def dot(left, right):
    return jnp.dot(left, right, preferred_element_type=F32)


def dot3(left, right):
    rows = left[0].shape[0]
    both = dot(jnp.concatenate(left, axis=0), right[0])
    return both[:rows] + (both[rows:] + dot(left[0], right[1]))


def dot3_wide(left, wide):
    rows = left.shape[0] // 2
    full = dot(left, wide)
    return full[:rows, :BW] + (full[:rows, BW:] + full[rows:, :BW])


def pairs_of(panels):
    return [(p, q) for p in range(panels) for q in range(p + 1, panels)]


def reorder_kernel(half, owner_list, slot_list, spread, ordered, owner, slot, held, sems):
    copies = start_copies([(owner_list, owner), (slot_list, slot), (spread, held)], sems)
    for copy in copies:
        copy.wait()

    def move(block, carry):
        place = slot[block] * half + owner[block]
        parity = block % BLK_DEV

        @pl.when(parity == 0)
        def _():
            ordered[place] = held[block // BLK_DEV, :, :BW]

        @pl.when(parity == 1)
        def _():
            ordered[place] = held[block // BLK_DEV, :, BW:]

        return carry

    lax.fori_loop(0, ordered.shape[0], move, 0)


def reorder(spread, owner_list, slot_list):
    cols, rows, _ = spread.shape
    outs = [shape((cols * BLK_DEV, rows, BW))]
    scratch = [pltpu.SMEM(owner_list.shape, jnp.int32), pltpu.SMEM(slot_list.shape, jnp.int32), pltpu.VMEM(spread.shape, F32)]
    return call(
        functools.partial(reorder_kernel, cols), "reorder", outs, (*pinned((owner_list, slot_list)), spread), far=3, copies=3, scratch=scratch
    )[0]


def is_odd(inner):
    return (lax.axis_index("row") % inner) % 2


def gram_kernel(inner, count, summed, wanted, *refs):
    pieces, refs = refs[:4 * count], refs[4 * count:]
    before, refs = (refs[:len(wanted)], refs[len(wanted):]) if summed else ((), refs)
    outs, (high_out, low_out, staged, high, low, high_t, low_t, *held, sems) = refs[:len(wanted)], refs[len(wanted):]
    panels, rows, width = pieces[0].shape
    odd = is_odd(inner)
    places = (0, jnp.where(odd == 0, 1, 2), jnp.where(odd == 0, 2, 1), 3)
    arriving = start_copies([(piece, staged.at[at]) for at, piece in enumerate(pieces)], sems)
    base = 4 * count
    sums = start_copies(list(zip(before, held)), sems, base)
    for at, copy in enumerate(arriving):
        copy.wait()
        cut = pl.ds(pl.multiple_of((at // 4 * 4 + places[at % 4]) * rows, rows), rows)
        for p in range(panels):
            top, rest = halves(staged[at, p])
            high[cut, p * width:(p + 1) * width] = top
            low[cut, p * width:(p + 1) * width] = rest
    leaving = start_copies([(high, high_out), (low, low_out)], sems, base + 2)
    for copy in sums:
        copy.wait()
    cuts = [slice(p * width, (p + 1) * width) for p in range(panels)]
    for cut in cuts:
        high_t[cut, :] = high[:, cut].T
        low_t[cut, :] = low[:, cut].T
    base += 4
    for kind, blocks in enumerate(wanted):
        for at, (p, q) in enumerate(blocks):
            value = dot3((high_t[cuts[p], :], low_t[cuts[p], :]), (high[:, cuts[q]], low[:, cuts[q]]))
            held[kind][at] = value + held[kind][at] if summed else value
            leaving += start_copies([(held[kind].at[at], outs[kind].at[at])], sems, base)
            base += 1
    for copy in leaving:
        copy.wait()


def diag_pairs(panels):
    return [(p, p) for p in range(panels)]


def gram(inner, pieces, before, wanted, after=None):
    panels, rows, width = pieces[0].shape
    count = len(pieces) // 4
    total, full = len(pieces) * rows, panels * width
    blocks = [shape((len(pairs), width, width)) for pairs in wanted]
    outs = blocks + [shape((total, full), BF16), shape((total, full), BF16)]
    far = list(pieces) + pinned(before or ())
    used = len(far)
    if after is not None:
        far.append(after)

    def body(*refs):
        gram_kernel(inner, count, before is not None, wanted, *refs[:used], *refs[len(far):])

    number = sum(len(pairs) for pairs in wanted)
    return call(
        body, "gram", outs, far, far=len(far), far_outs=len(outs), copies=4 * count + 4 + number,
        scratch=[
            pltpu.VMEM((len(pieces), panels, rows, width), F32), pltpu.VMEM((total, full), BF16), pltpu.VMEM((total, full), BF16),
            pltpu.VMEM((full, total), BF16), pltpu.VMEM((full, total), BF16), *(pltpu.VMEM(block.shape, F32) for block in blocks),
        ],
        flops=6 * number * width * width * total, mib=32,
    )


def corner_kernel(panels, high_in, low_in, before, corner, high, low, held, sems):
    width = high.shape[1] // panels
    copies = start_copies([(high_in, high), (low_in, low), (before, held)], sems)
    for copy in copies[:2]:
        copy.wait()
    cuts = [slice(p * width, (p + 1) * width) for p in range(panels)]
    left = [(high[:, cut].T, low[:, cut].T) for cut in cuts[:-1]]
    copies[2].wait()
    leaving = []
    for at, (p, q) in enumerate(pairs_of(panels)):
        held[at] += dot3(left[p], (high[:, cuts[q]], low[:, cuts[q]]))
        leaving += start_copies([(held.at[at], corner.at[at])], sems, 3 + at)
    for copy in leaving:
        copy.wait()


def corners(panels, parts, before):
    total, full = parts[0].shape
    count, width, _ = before.shape
    return call(
        functools.partial(corner_kernel, panels), "corner", [shape(before.shape)], pinned((*parts, before)), far=3, far_outs=1,
        copies=3 + count, scratch=[pltpu.VMEM((total, full), BF16), pltpu.VMEM((total, full), BF16), pltpu.VMEM(before.shape, F32)],
        flops=6 * count * width * width * total,
    )[0]


def inverses(own, other, copies):
    panels, order, _ = own.shape
    row = lax.broadcasted_iota(jnp.int32, (order, order), 0)
    col = lax.broadcasted_iota(jnp.int32, (order, order), 1)
    apart = jnp.bitwise_xor(row, col)
    strict, edges, scale = [], [], []
    for p in range(panels):
        copies[2 * p].wait()
        copies[2 * p + 1].wait()
        gram_sum = own[p] + other[p]
        half = jnp.where(apart == 0, 0.5 * gram_sum, 0.0)
        by_row = 1.0 / jnp.sum(half, axis=1, keepdims=True)
        by_col = 1.0 / jnp.sum(half, axis=0, keepdims=True)
        strict.append(jnp.where(row < col, gram_sum * by_row, 0.0))
        edges.append(halves(strict[-1]))
        scale.append(by_col)

    def stacked(value):
        high, rest = halves(value)
        return jnp.concatenate([high.astype(F32), rest.astype(F32)], axis=0).astype(BF16)

    def multiply(left, right):
        rows = left.shape[0]
        if rows >= 16:
            return dot3(halves(left), right)
        both = stacked(left)
        full = dot(both, right[0])
        return full[:rows] + (full[rows:] + dot(both, right[1])[:rows])

    def inside(size):
        return jnp.where(apart < size, 1.0, 0.0)

    def widen(value):
        size = value.shape[0]
        if size < 16:
            return halves(jnp.concatenate([value] * (order // size), axis=0) * inside(size))
        mask = inside(size).astype(BF16)
        return tuple(jnp.concatenate([part] * (order // size), axis=0) * mask for part in halves(value))

    size = 8
    mask = inside(size)
    small_row = lax.broadcasted_iota(jnp.int32, (size, order), 0)
    small_col = lax.broadcasted_iota(jnp.int32, (size, order), 1)
    identity = jnp.where(small_row == small_col % size, 1.0, 0.0)
    full = [value * -mask for value in strict]
    power = [sum(value[k:k + size] for k in range(0, order, size)) for value in full]
    accum = [identity + value for value in power]
    power = [multiply(value, halves(wide)) for value, wide in zip(power, full)]
    both = [multiply(jnp.concatenate([value, extra], axis=0), widen(extra)) for value, extra in zip(accum, power)]
    accum = [value + extra[:size] for value, extra in zip(accum, both)]
    accum = [value + multiply(value, widen(extra[size:])) for value, extra in zip(accum, both)]
    while size < order:
        between = (inside(2 * size) - inside(size)).astype(BF16)
        lane = lax.broadcasted_iota(jnp.int32, (size, order), 1)
        even = (lane // size) % 2 == 0
        uppers = [jnp.where(even, value, 0.0) for value in accum]
        part = [multiply(value, (edge[0] * between, edge[1] * between)) for value, edge in zip(uppers, edges)]
        part = [multiply(edge, widen(value)) for edge, value in zip(part, accum)]
        accum = [
            jnp.concatenate([upper - edge, jnp.where(even, 0.0, value)], axis=0) for upper, edge, value in zip(uppers, part, accum)
        ]
        size *= 2
    return [jnp.concatenate(halves(value * by_col), axis=0) for value, by_col in zip(accum, scale)]


def place_of(inner, chunk, by_x, by_y):
    row, col = lax.axis_index("row"), lax.axis_index("col")
    return jnp.bitwise_xor(row // inner, by_x), jnp.bitwise_xor(col % LOW, chunk * 2 + by_y)


def copies_of_rows(parts, arrays, first, count, stride, held):
    pairs = []
    for k in range(2):
        at = k * CHUNKS * count
        for part, chunks in enumerate(parts):
            for chunk in range(chunks):
                pairs.append((arrays[2 * part + k].at[chunk * stride + first:chunk * stride + first + count, :], held.at[at:at + count, :]))
                at += count
    return pairs


def project_kernel(inner, parts, *refs):
    arrays, (slab, product, left, held, held_slab, sems) = refs[:len(parts) * 2], refs[len(parts) * 2:]
    rows = slab.shape[1]
    total = CHUNKS * 4 * rows
    copies = start_copies([(slab, held_slab)] + copies_of_rows(parts, arrays, 0, 4 * rows, 4 * rows, held), sems)
    copies[0].wait()
    for chunk in range(CHUNKS):
        for at in range(4):
            outer, low = place_of(inner, chunk, at // 2, at % 2)
            start = (4 * chunk + at) * rows
            left[:, start:start + rows] = held_slab[outer * LOW + low].T
    high, rest = halves(left[...])
    for copy in copies[1:]:
        copy.wait()
    both = dot(jnp.concatenate([high, rest], axis=0), held[:total, :])
    product[...] = both[:BW] + (both[BW:] + dot(high, held[total:, :]))


def project(inner, arrays, slab):
    full = arrays[0].shape[1]
    parts = [array.shape[0] // (4 * slab.shape[1]) for array in arrays[::2]]
    total = CHUNKS * 4 * slab.shape[1]
    return call(
        functools.partial(project_kernel, inner, parts), "project", [shape((BW, full))], pinned((*arrays, slab)), far=len(arrays) + 1,
        scratch=[pltpu.VMEM((BW, total), F32), pltpu.VMEM((2 * total, full), BF16), pltpu.VMEM(slab.shape, F32)],
        copies=2 * CHUNKS + 1, flops=6 * full * total * BW,
    )[0]


def change(inner, by_x, held, wide, slab, result):
    rows = slab.shape[1]
    delta = dot3_wide(held[...], wide[...])
    for chunk in range(CHUNKS):
        for by_y in range(2):
            outer, low_at = place_of(inner, chunk, by_x, by_y)
            start = (2 * chunk + by_y) * rows
            result[low_at] = slab[outer * LOW + low_at] - delta[start:start + rows, :]


def solve_kernel(inner, parts, own, other, diag_own, diag_other, corner_own, corner_other, *refs):
    arrays, refs = refs[:len(parts) * 2], refs[len(parts) * 2:]
    slab, away, wide, held_diag_own, held_diag_other, held_own, held_other, held, held_slab, sems = refs
    panels, width, _ = diag_own.shape
    pairs = pairs_of(panels)
    rows = slab.shape[1]
    diags = start_copies(
        [(far.at[p], near.at[p]) for p in range(panels) for far, near in ((diag_own, held_diag_own), (diag_other, held_diag_other))], sems
    )
    copies = start_copies(
        [(corner_own, held_own), (corner_other, held_other), (slab, held_slab)]
        + copies_of_rows(parts, arrays, 2 * rows, 2 * rows, 4 * rows, held), sems, 2 * panels
    )
    values = [(own[:, p * width:(p + 1) * width] + other[:, p * width:(p + 1) * width]).T for p in range(panels)]
    scaled = inverses(held_diag_own, held_diag_other, diags)
    for p in reversed(range(panels)):
        cut = slice(p * width, (p + 1) * width)
        solved = jnp.concatenate(halves(dot3_wide(scaled[p], jnp.concatenate(halves(values[p]), axis=1))), axis=1)
        wide[cut, :] = solved
        if p == panels - 1:
            copies[0].wait()
            copies[1].wait()
        for at, (i, q) in enumerate(pairs):
            if q == p:
                values[i] = values[i] - dot3_wide(jnp.concatenate(halves(held_own[at] + held_other[at]), axis=0), solved)
    for copy in copies[2:]:
        copy.wait()
    change(inner, 1, held, wide, held_slab, away)


def column_of(outer):
    return pl.ds(pl.multiple_of(outer * BW, BW), BW)


def copies_to_result(extra, half, column, result):
    rows = half.shape[1] // extra
    return [
        (half.at[low, e * rows:(e + 1) * rows, :], result.at[(e * LOW + low) * rows:(e * LOW + low + 1) * rows, column])
        for low in range(LOW) for e in range(extra)
    ]


def keep_kernel(inner, parts, extra, wide, *refs):
    arrays, (slab, result, keep, held, held_slab, sems) = refs[:len(parts) * 2], refs[len(parts) * 2:]
    rows = slab.shape[1]
    copies = start_copies([(slab, held_slab)] + copies_of_rows(parts, arrays, 0, 2 * rows, 4 * rows, held), sems)
    for copy in copies:
        copy.wait()
    change(inner, 0, held, wide, held_slab, keep)
    outer = lax.axis_index("row") // inner
    for copy in start_copies(copies_to_result(extra, keep, column_of(outer), result), sems, len(copies)):
        copy.wait()


def place_kernel(inner, extra, begun, back, result, sems):
    outer = lax.axis_index("row") // inner
    for copy in start_copies(copies_to_result(extra, back, column_of(1 - outer), result), sems):
        copy.wait()


def on_device(rows, cols, vectors, reflectors, owner_list, slot_list):
    inner = rows // 2
    extra = cols // LOW
    local_rows = vectors.shape[0] // cols
    panels = reflectors.shape[0]

    def at(row, col):
        return row * cols + col

    def send(value, change_of):
        perm = [(at(r, c), at(*change_of(r, c))) for r in range(rows) for c in range(cols)]
        return lax.ppermute(value, ("row", "col"), perm)

    def by_z(step):
        return lambda r, c: (r, c ^ (2 * step))

    def by_first(r, c):
        return (r, c ^ 1) if (r % inner) % 2 == 0 else ((r + inner) % rows, c)

    def by_second(r, c):
        return (r, c ^ 1) if (r % inner) % 2 == 1 else ((r + inner) % rows, c)

    def after(value, *others):
        return lax.optimization_barrier((value, *others))[0]

    own = reflectors
    if extra > 1:
        groups = [[e * LOW + low for e in range(extra)] for low in range(LOW)]
        own = lax.all_gather(own, "col", axis=1, tiled=True, axis_index_groups=groups)
    start = [own, send(own, by_z(1)), send(own, by_z(2))]
    start.append(send(start[2], by_z(1)))
    first = [send(piece, by_first) for piece in start]
    second = [send(piece, by_second) for piece in start]
    both = [send(piece, by_second) for piece in first]

    vectors = after(vectors, start[1], start[2], first[0], second[0])
    spread = lax.all_to_all(vectors.reshape(cols, local_rows, -1), "col", split_axis=0, concat_axis=0, tiled=True)
    ordered = reorder(spread, owner_list, slot_list)
    groups = [[at(o * inner + i, c) for o in range(2) for c in range(cols)] for i in range(inner)]
    slab = lax.all_to_all(ordered, ("row", "col"), split_axis=0, concat_axis=0, tiled=True, axis_index_groups=groups)
    slab = slab.reshape(2, extra, LOW, local_rows, BW).transpose(0, 2, 1, 3, 4)
    slab = slab.reshape(2 * LOW, extra * local_rows, BW)

    pieces = [(start[chunk], first[chunk], second[chunk], both[chunk]) for chunk in range(CHUNKS)]
    diag_blocks, corner_blocks = diag_pairs(panels), pairs_of(panels)
    diag, corner, high_a, low_a = gram(inner, sum(pieces[:-1], ()), None, (diag_blocks, corner_blocks), ordered)
    diag, corner, high_b, low_b = gram(inner, pieces[-1], (diag, corner), (diag_blocks, corner_blocks))
    arrays, parts = (high_a, low_a, high_b, low_b), (CHUNKS - 1, 1)
    def over_inner(value, bit):
        return send(value, lambda r, c: (r ^ bit, c))

    bits = [1 << k for k in range(inner.bit_length() - 1)]
    for bit in bits[:-1]:
        diag, corner = (value + over_inner(value, bit) for value in (diag, corner))
    diag_other = over_inner(diag, bits[-1])
    product = project(inner, arrays, slab)
    for bit in bits[:-1]:
        product = product + over_inner(product, bit)
    full, half_rows, block = product.shape[1], 2 * slab.shape[1], shape((LOW,) + slab.shape[1:])
    half_held = [pltpu.VMEM((2 * CHUNKS * half_rows, full), BF16), pltpu.VMEM(slab.shape, F32)]
    away, wide = call(
        functools.partial(solve_kernel, inner, parts), "solve", [block, shape((full, 2 * BW), BF16)],
        (product, over_inner(product, bits[-1]), *pinned((diag, diag_other, corner, over_inner(corner, bits[-1]))), *pinned((*arrays, slab))),
        far=len(arrays) + 5, copies=2 * panels + 2 * CHUNKS + 3,
        scratch=[pltpu.VMEM(diag.shape, F32)] * 2 + [pltpu.VMEM(corner.shape, F32)] * 2 + half_held, flops=8 * 10**9, mib=32,
    )
    back = send(away, lambda r, c: ((r + inner) % rows, c))
    begun, = call(
        functools.partial(keep_kernel, inner, parts, extra), "keep", [shape(vectors.shape)], (wide, *pinned((*arrays, slab))),
        far=len(arrays) + 1, far_outs=1, copies=2 * CHUNKS + 1 + LOW * extra, scratch=[pltpu.VMEM(block.shape, F32)] + half_held,
        flops=10**9,
    )
    result, = call(
        functools.partial(place_kernel, inner, extra), "place", [shape(vectors.shape)], (*pinned((begun,)), back), far=2, far_outs=1,
        copies=LOW * extra, aliases={0: 0},
    )
    return result


def solution(mesh):
    return jax.shard_map(
        functools.partial(on_device, mesh.shape["row"], mesh.shape["col"]),
        mesh=mesh,
        in_specs=(P("row", "col"), P(None, ("row", "col"), None), P(), P()),
        out_specs=P("row", "col"),
        check_vma=False,
    )
```

time: 94.6 us -> 91.5 us (0.967)
  Pallas kernels: 28.6 us -> 25.9 us
    pallas_call x7, Pallas kernels: 28.6 us -> 25.9 us  [call(): pl.pallas_call(body, out_shape=tuple(outs[:len(outs) - far_outs]) + tuple...]
  transfers between devices with their start and end apart: 21 -> 21, of which waited for: 10 -> 11; matrix products, arithmetic and copies ran while one was open for 0% -> 0% of each run, Pallas kernels for 25% -> 20%
where the time goes in v3:
time: 91.5 us; the launch traced here: 91.1 us
  waiting for transfers between devices  34.4 us (38%)
  starting transfers between devices  29.9 us (33%)
  Pallas kernels  25.9 us (28%)
    ppermute x19, waiting for transfers between devices, send(): return lax.ppermute(value, ('row', 'col'), perm)  34.4 us
    pallas_call x7, Pallas kernels, call(): pl.pallas_call(body, out_shape=tuple(outs[:len(outs) - far_outs]) + tuple...  25.9 us
    ppermute x19, starting transfers between devices, send(): return lax.ppermute(value, ('row', 'col'), perm)  21.3 us
    all_to_all x1, starting transfers between devices, on_device(): lax.all_to_all(ordered, ('row', 'col'), split_axis=0, concat_axis=0, tile...  4.68 us
    all_to_all x1, starting transfers between devices, on_device(): lax.all_to_all(vectors.reshape(cols, local_rows, -1), 'col', split_axis=0...  3.87 us
  transfers between devices with their start and end apart: 21, of which 11 were waited for; matrix products, arithmetic and copies ran while one was open for 0% of the time, Pallas kernels for 20%

profile of v3, /device:TPU:0, one launch (start us, length us, event | category | flops | bytes accessed | tf_op | source)
XLA Modules:
  0.0 91.1 jit_solution(10353081802646431318)
XLA Ops:
  0.0 3.0 %collective-permute-start.3 = (f32[4,64,256]{2,1,0:T(8,128)}, f32[4,64,256]{2,1,0:T(8,128)S(1)}, u32[]{:S(2)}, u32[]{:S(2)}) collective-permute-start(f32[4,64,256]{2,1,0:T(8,128)} %refs_0_.1), channel_id=1, source_target_pairs={{0,2},{1,3},{2,0},{3,1},{4,6},{5,7},{6,4},{7,5},{8,10},{9,11},{10,... | collective-permute-start | bytes 786440 | tf_op jit(solution)/shard_map/ppermute | solution.py:397
  3.0 1.5 %collective-permute-start.1 = (f32[4,64,256]{2,1,0:T(8,128)}, f32[4,64,256]{2,1,0:T(8,128)S(1)}, u32[]{:S(2)}, u32[]{:S(2)}) collective-permute-start(f32[4,64,256]{2,1,0:T(8,128)} %refs_0_.1), channel_id=1, source_target_pairs={{0,16},{1,17},{2,18},{3,19},{4,20},{5,21},{6,22},{7,23},{8,9},{9,8... | collective-permute-start | bytes 786440 | tf_op jit(solution)/shard_map/ppermute | solution.py:397
  4.5 1.5 %collective-permute-start = (f32[4,64,256]{2,1,0:T(8,128)}, f32[4,64,256]{2,1,0:T(8,128)S(1)}, u32[]{:S(2)}, u32[]{:S(2)}) collective-permute-start(f32[4,64,256]{2,1,0:T(8,128)} %refs_0_.1), channel_id=1, source_target_pairs={{0,1},{1,0},{2,3},{3,2},{4,5},{5,4},{6,7},{7,6},{8,24},{9,25},{10,... | collective-permute-start | bytes 786440 | tf_op jit(solution)/shard_map/ppermute | solution.py:397
  6.0 2.6 %collective-permute-start.7 = (f32[4,64,256]{2,1,0:T(8,128)}, f32[4,64,256]{2,1,0:T(8,128)S(1)}, u32[]{:S(2)}, u32[]{:S(2)}) collective-permute-start(f32[4,64,256]{2,1,0:T(8,128)} %refs_0_.1), channel_id=1, source_target_pairs={{0,4},{1,5},{2,6},{3,7},{4,0},{5,1},{6,2},{7,3},{8,12},{9,13},{10,... | collective-permute-start | bytes 786440 | tf_op jit(solution)/shard_map/ppermute | solution.py:397
  8.6 3.4 %collective-permute-done.3.refs_4_ = f32[4,64,256]{2,1,0:T(8,128)S(1)} collective-permute-done((f32[4,64,256]{2,1,0:T(8,128)}, f32[4,64,256]{2,1,0:T(8,128)S(1)}, u32[]{:S(2)}, u32[]{:S(2)}) %collective-permute-start.3) | collective-permute-done | bytes 262176 | tf_op jit(solution)/shard_map/ppermute | solution.py:397
  12.2 7.8 %collective-permute-done.7.refs_8_ = f32[4,64,256]{2,1,0:T(8,128)S(1)} collective-permute-done((f32[4,64,256]{2,1,0:T(8,128)}, f32[4,64,256]{2,1,0:T(8,128)S(1)}, u32[]{:S(2)}, u32[]{:S(2)}) %collective-permute-start.7) | collective-permute-done | bytes 262176 | tf_op jit(solution)/shard_map/ppermute | solution.py:397
  20.0 3.9 %all-to-all-start = ((f32[8,64,256]{2,1,0:T(8,128)}), f32[8,64,256]{2,1,0:T(8,128)S(1)}, u32[]{:S(2)}, u32[]{:S(2)}) async-start(f32[8,64,256]{2,1,0:T(8,128)} %bitcast.1), calls=%async_computation | async-start | bytes 1048576 | tf_op jit(solution)/shard_map/all_to_all | solution.py:422
  23.9 0.5 collective-permute-start.5
  24.4 2.0 %collective-permute-start.11 = (f32[4,64,256]{2,1,0:T(8,128)S(1)}, f32[4,64,256]{2,1,0:T(8,128)S(1)}, u32[]{:S(2)}, u32[]{:S(2)}) collective-permute-start(f32[4,64,256]{2,1,0:T(8,128)S(1)} %collective-permute-done.7.refs_8_), channel_id=1, source_target_pairs={{0,2},{1,3},{2,0},{3,1},{4,6},{5,7},{6,4},{7,5},{8,10},{9,11},{10,... | collective-permute-start | bytes 786440 | tf_op jit(solution)/shard_map/ppermute | solution.py:397
  26.5 1.5 %collective-permute-start.4 = (f32[4,64,256]{2,1,0:T(8,128)S(1)}, f32[4,64,256]{2,1,0:T(8,128)S(1)}, u32[]{:S(2)}, u32[]{:S(2)}) collective-permute-start(f32[4,64,256]{2,1,0:T(8,128)S(1)} %collective-permute-done.3.refs_4_), channel_id=1, source_target_pairs={{0,1},{1,0},{2,3},{3,2},{4,5},{5,4},{6,7},{7,6},{8,24},{9,25},{10,... | collective-permute-start | bytes 786440 | tf_op jit(solution)/shard_map/ppermute | solution.py:397
  27.9 0.6 collective-permute-start.8
  28.5 1.5 %collective-permute-start.2 = (f32[4,64,256]{2,1,0:T(8,128)S(1)}, f32[4,64,256]{2,1,0:T(8,128)S(1)}, u32[]{:S(2)}, u32[]{:S(2)}) collective-permute-start(f32[4,64,256]{2,1,0:T(8,128)S(1)} %collective-permute-done.refs_1_), channel_id=1, source_target_pairs={{0,16},{1,17},{2,18},{3,19},{4,20},{5,21},{6,22},{7,23},{8,9},{9,8... | collective-permute-start | bytes 786440 | tf_op jit(solution)/shard_map/ppermute | solution.py:397
  30.0 3.1 %collective-permute-done.5.refs_6_ = f32[4,64,256]{2,1,0:T(8,128)S(1)} collective-permute-done((f32[4,64,256]{2,1,0:T(8,128)S(1)}, f32[4,64,256]{2,1,0:T(8,128)S(1)}, u32[]{:S(2)}, u32[]{:S(2)}) %collective-permute-start.5) | collective-permute-done | bytes 262176 | tf_op jit(solution)/shard_map/ppermute | solution.py:397
  33.6 5.4 %collective-permute-done.11.refs_0_ = f32[4,64,256]{2,1,0:T(8,128)S(1)} collective-permute-done((f32[4,64,256]{2,1,0:T(8,128)S(1)}, f32[4,64,256]{2,1,0:T(8,128)S(1)}, u32[]{:S(2)}, u32[]{:S(2)}) %collective-permute-start.11) | collective-permute-done | bytes 262176 | tf_op jit(solution)/shard_map/ppermute | solution.py:397
  39.0 1.5 %collective-permute-start.12 = (f32[4,64,256]{2,1,0:T(8,128)S(1)}, f32[4,64,256]{2,1,0:T(8,128)S(1)}, u32[]{:S(2)}, u32[]{:S(2)}) collective-permute-start(f32[4,64,256]{2,1,0:T(8,128)S(1)} %collective-permute-done.11.refs_0_), channel_id=1, source_target_pairs={{0,1},{1,0},{2,3},{3,2},{4,5},{5,4},{6,7},{7,6},{8,24},{9,25},{10,... | collective-permute-start | bytes 786440 | tf_op jit(solution)/shard_map/ppermute | solution.py:397
  40.8 3.3 %collective-permute-done.8.refs_9_ = f32[4,64,256]{2,1,0:T(8,128)S(1)} collective-permute-done((f32[4,64,256]{2,1,0:T(8,128)S(1)}, f32[4,64,256]{2,1,0:T(8,128)S(1)}, u32[]{:S(2)}, u32[]{:S(2)}) %collective-permute-start.8) | collective-permute-done | bytes 262176 | tf_op jit(solution)/shard_map/ppermute | solution.py:397
  44.1 0.7 collective-permute-start.10
  44.8 1.9 %reorder.1.refs_12_ = f32[16,64,128]{2,1,0:T(8,128)} custom-call(s32[16]{0:T(128)} %owner_list.1, s32[16]{0:T(128)} %slot_list.1, f32[8,64,256]{2,1,0:T(8,128)S(1)} %all-to-all-done.spread), custom_call_target="tpu_custom_call" | custom-call | bytes 4194304 | tf_op jit(solution)/shard_map/reorder/pallas_call | solution.py:32
  46.8 4.7 %all-to-all-start.1 = ((f32[16,64,128]{2,1,0:T(8,128)}), f32[16,64,128]{2,1,0:T(8,128)S(1)}, u32[]{:S(2)}, u32[]{:S(2)}) async-start(f32[16,64,128]{2,1,0:T(8,128)} %reorder.1.refs_12_), calls=%async_computation.1 | async-start | bytes 1048576 | tf_op jit(solution)/shard_map/all_to_all | solution.py:425
  51.5 2.0 %collective-permute-start.13 = (f32[4,64,256]{2,1,0:T(8,128)S(1)}, f32[4,64,256]{2,1,0:T(8,128)S(1)}, u32[]{:S(2)}, u32[]{:S(2)}) collective-permute-start(f32[4,64,256]{2,1,0:T(8,128)S(1)} %collective-permute-done.11.refs_0_), channel_id=1, source_target_pairs={{0,16},{1,17},{2,18},{3,19},{4,20},{5,21},{6,22},{7,23},{8,9},{9,8... | collective-permute-start | bytes 786440 | tf_op jit(solution)/shard_map/ppermute | solution.py:397
  53.6 5.6 %gram.2 = (f32[4,256,256]{2,1,0:T(8,128)}, f32[6,256,256]{2,1,0:T(8,128)}, bf16[768,1024]{1,0:T(8,128)(2,1)}, bf16[768,1024]{1,0:T(8,128)(2,1)}) custom-call(f32[4,64,256]{2,1,0:T(8,128)S(1)} %copy-done, f32[4,64,256]{2,1,0:T(8,128)S(1)} %collective-permute-done.refs_1_, f32[4,64,256]{2,1,0:T(8,128)S(1)} %collective-permute-done.1.refs_2_, ...), custom_call_target="tpu_custom_call" | custom-call | flops 3019898880 | bytes 4194304 | tf_op jit(solution)/shard_map/gram/pallas_call | solution.py:32
  59.2 1.4 %collective-permute-done.13.refs_2_ = f32[4,64,256]{2,1,0:T(8,128)S(1)} collective-permute-done((f32[4,64,256]{2,1,0:T(8,128)S(1)}, f32[4,64,256]{2,1,0:T(8,128)S(1)}, u32[]{:S(2)}, u32[]{:S(2)}) %collective-permute-start.13) | collective-permute-done | bytes 262176 | tf_op jit(solution)/shard_map/ppermute | solution.py:397
  60.5 3.5 %collective-permute-done.14.refs_3_ = f32[4,64,256]{2,1,0:T(8,128)S(1)} collective-permute-done((f32[4,64,256]{2,1,0:T(8,128)S(1)}, f32[4,64,256]{2,1,0:T(8,128)S(1)}, u32[]{:S(2)}, u32[]{:S(2)}) %collective-permute-start.14) | collective-permute-done | bytes 262176 | tf_op jit(solution)/shard_map/ppermute | solution.py:397
  64.1 4.4 %gram.3 = (f32[4,256,256]{2,1,0:T(8,128)}, f32[6,256,256]{2,1,0:T(8,128)}, bf16[256,1024]{1,0:T(8,128)(2,1)}, bf16[256,1024]{1,0:T(8,128)(2,1)}) custom-call(f32[4,64,256]{2,1,0:T(8,128)S(1)} %collective-permute-done.11.refs_0_, f32[4,64,256]{2,1,0:T(8,128)S(1)} %collective-permute-done.12.refs_1_, f32[4,64,256]{2,1,0:T(8,128)S(1)} %collective-permute-done.13.refs_2_, ...), custom_call_target="tpu_custom_call" | custom-call | flops 1006632960 | bytes 4194304 | tf_op jit(solution)/shard_map/gram/pallas_call | solution.py:32
  69.0 0.8 copy-done.1
  69.8 3.4 %project.1.own = f32[128,1024]{1,0:T(8,128)S(1)} custom-call(bf16[768,1024]{1,0:T(8,128)(2,1)} %get-tuple-element.17.refs_0_, bf16[768,1024]{1,0:T(8,128)(2,1)} %get-tuple-element.18.refs_1_, bf16[256,1024]{1,0:T(8,128)(2,1)} %get-tuple-element.21.refs_2_, bf16[256,1024]{1,0:T(8,128)(2,1)} %get-tuple-element.22.refs_3_, f32[16,64,128]{2,1,0:T(8,128)} %copy-done.1), custom_call_target="tpu_custom_call" | custom-call | flops 805306368 | bytes 4194304 | tf_op jit(solution)/shard_map/project/pallas_call | solution.py:32
  73.6 1.5 %collective-permute-done.15.other = f32[128,1024]{1,0:T(8,128)S(1)} collective-permute-done((f32[128,1024]{1,0:T(8,128)S(1)}, f32[128,1024]{1,0:T(8,128)S(1)}, u32[]{:S(2)}, u32[]{:S(2)}) %collective-permute-start.15) | collective-permute-done | bytes 524320 | tf_op jit(solution)/shard_map/ppermute | solution.py:397
  75.2 6.7 %solve.1 = (f32[8,64,128]{2,1,0:T(8,128)S(1)}, bf16[1024,256]{1,0:T(8,128)(2,1)S(1)}) custom-call(f32[128,1024]{1,0:T(8,128)S(1)} %project.1.own, f32[128,1024]{1,0:T(8,128)S(1)} %collective-permute-done.15.other, f32[4,256,256]{2,1,0:T(8,128)} %get-tuple-element.23.diag_own, f32[4,256,256]{2,1,0:T(8,128)} %copy-done.2, ...), custom_call_target="tpu_custom_call" | custom-call | flops 8000000000 | bytes 4194304 | tf_op jit(solution)/shard_map/solve/pallas_call | solution.py:32
  81.9 0.8 collective-permute-start.18
  82.7 3.2 %keep.1.begun = f32[512,256]{1,0:T(8,128)} custom-call(bf16[1024,256]{1,0:T(8,128)(2,1)S(1)} %get-tuple-element.25.wide, bf16[768,1024]{1,0:T(8,128)(2,1)} %get-tuple-element.17.refs_0_, bf16[768,1024]{1,0:T(8,128)(2,1)} %get-tuple-element.18.refs_1_, bf16[256,1024]{1,0:T(8,128)(2,1)} %get-tuple-element.21.refs_2_, ...), custom_call_target="tpu_custom_call" | custom-call | flops 1000000000 | bytes 4194304 | tf_op jit(solution)/shard_map/keep/pallas_call | solution.py:32
  85.9 4.4 %collective-permute-done.18.back = f32[8,64,128]{2,1,0:T(8,128)S(1)} collective-permute-done((f32[8,64,128]{2,1,0:T(8,128)S(1)}, f32[8,64,128]{2,1,0:T(8,128)S(1)}, u32[]{:S(2)}, u32[]{:S(2)}) %collective-permute-start.18) | collective-permute-done | bytes 262176 | tf_op jit(solution)/shard_map/ppermute | solution.py:397
  90.3 0.8 place.1
  (23 shorter events, 2.1 us)
Async XLA Ops:
  0.0 12.1 %collective-permute-start.3 = (f32[4,64,256]{2,1,0:T(8,128)}, f32[4,64,256]{2,1,0:T(8,128)S(1)}, u32[]{:S(2)}, u32[]{:S(2)}) collective-permute-start(f32[4,64,256]{2,1,0:T(8,128)} %refs_0_.1), channel_id=1, source_target_pairs={{0,2},{1,3},{2,0},{3,1},{4,6},{5,7},{6,4},{7,5},{8,10},{9,11},{10,... | collective-permute-start | bytes 786440 | tf_op jit(solution)/shard_map/ppermute | solution.py:397
  3.0 9.2 %collective-permute-start.1 = (f32[4,64,256]{2,1,0:T(8,128)}, f32[4,64,256]{2,1,0:T(8,128)S(1)}, u32[]{:S(2)}, u32[]{:S(2)}) collective-permute-start(f32[4,64,256]{2,1,0:T(8,128)} %refs_0_.1), channel_id=1, source_target_pairs={{0,16},{1,17},{2,18},{3,19},{4,20},{5,21},{6,22},{7,23},{8,9},{9,8... | collective-permute-start | bytes 786440 | tf_op jit(solution)/shard_map/ppermute | solution.py:397
  4.5 7.7 %collective-permute-start = (f32[4,64,256]{2,1,0:T(8,128)}, f32[4,64,256]{2,1,0:T(8,128)S(1)}, u32[]{:S(2)}, u32[]{:S(2)}) collective-permute-start(f32[4,64,256]{2,1,0:T(8,128)} %refs_0_.1), channel_id=1, source_target_pairs={{0,1},{1,0},{2,3},{3,2},{4,5},{5,4},{6,7},{7,6},{8,24},{9,25},{10,... | collective-permute-start | bytes 786440 | tf_op jit(solution)/shard_map/ppermute | solution.py:397
  6.0 14.0 %collective-permute-start.7 = (f32[4,64,256]{2,1,0:T(8,128)}, f32[4,64,256]{2,1,0:T(8,128)S(1)}, u32[]{:S(2)}, u32[]{:S(2)}) collective-permute-start(f32[4,64,256]{2,1,0:T(8,128)} %refs_0_.1), channel_id=1, source_target_pairs={{0,4},{1,5},{2,6},{3,7},{4,0},{5,1},{6,2},{7,3},{8,12},{9,13},{10,... | collective-permute-start | bytes 786440 | tf_op jit(solution)/shard_map/ppermute | solution.py:397
  20.0 33.5 %copy-start = (f32[4,64,256]{2,1,0:T(8,128)S(1)}, f32[4,64,256]{2,1,0:T(8,128)}, u32[]{:S(2)}) copy-start(f32[4,64,256]{2,1,0:T(8,128)} %refs_0_.1) | copy-start | bytes 786436
  20.0 24.8 %all-to-all-start = ((f32[8,64,256]{2,1,0:T(8,128)}), f32[8,64,256]{2,1,0:T(8,128)S(1)}, u32[]{:S(2)}, u32[]{:S(2)}) async-start(f32[8,64,256]{2,1,0:T(8,128)} %bitcast.1), calls=%async_computation | async-start | bytes 1048576 | tf_op jit(solution)/shard_map/all_to_all | solution.py:422
  23.9 9.2 %collective-permute-start.5 = (f32[4,64,256]{2,1,0:T(8,128)S(1)}, f32[4,64,256]{2,1,0:T(8,128)S(1)}, u32[]{:S(2)}, u32[]{:S(2)}) collective-permute-start(f32[4,64,256]{2,1,0:T(8,128)S(1)} %collective-permute-done.3.refs_4_), channel_id=1, source_target_pairs={{0,16},{1,17},{2,18},{3,19},{4,20},{5,21},{6,22},{7,23},{8,9},{9,8... | collective-permute-start | bytes 786440 | tf_op jit(solution)/shard_map/ppermute | solution.py:397
  24.4 14.6 %collective-permute-start.11 = (f32[4,64,256]{2,1,0:T(8,128)S(1)}, f32[4,64,256]{2,1,0:T(8,128)S(1)}, u32[]{:S(2)}, u32[]{:S(2)}) collective-permute-start(f32[4,64,256]{2,1,0:T(8,128)S(1)} %collective-permute-done.7.refs_8_), channel_id=1, source_target_pairs={{0,2},{1,3},{2,0},{3,1},{4,6},{5,7},{6,4},{7,5},{8,10},{9,11},{10,... | collective-permute-start | bytes 786440 | tf_op jit(solution)/shard_map/ppermute | solution.py:397
  26.5 14.1 %collective-permute-start.4 = (f32[4,64,256]{2,1,0:T(8,128)S(1)}, f32[4,64,256]{2,1,0:T(8,128)S(1)}, u32[]{:S(2)}, u32[]{:S(2)}) collective-permute-start(f32[4,64,256]{2,1,0:T(8,128)S(1)} %collective-permute-done.3.refs_4_), channel_id=1, source_target_pairs={{0,1},{1,0},{2,3},{3,2},{4,5},{5,4},{6,7},{7,6},{8,24},{9,25},{10,... | collective-permute-start | bytes 786440 | tf_op jit(solution)/shard_map/ppermute | solution.py:397
  27.9 16.2 %collective-permute-start.8 = (f32[4,64,256]{2,1,0:T(8,128)S(1)}, f32[4,64,256]{2,1,0:T(8,128)S(1)}, u32[]{:S(2)}, u32[]{:S(2)}) collective-permute-start(f32[4,64,256]{2,1,0:T(8,128)S(1)} %collective-permute-done.7.refs_8_), channel_id=1, source_target_pairs={{0,1},{1,0},{2,3},{3,2},{4,5},{5,4},{6,7},{7,6},{8,24},{9,25},{10,... | collective-permute-start | bytes 786440 | tf_op jit(solution)/shard_map/ppermute | solution.py:397
  28.5 23.0 %collective-permute-start.2 = (f32[4,64,256]{2,1,0:T(8,128)S(1)}, f32[4,64,256]{2,1,0:T(8,128)S(1)}, u32[]{:S(2)}, u32[]{:S(2)}) collective-permute-start(f32[4,64,256]{2,1,0:T(8,128)S(1)} %collective-permute-done.refs_1_), channel_id=1, source_target_pairs={{0,16},{1,17},{2,18},{3,19},{4,20},{5,21},{6,22},{7,23},{8,9},{9,8... | collective-permute-start | bytes 786440 | tf_op jit(solution)/shard_map/ppermute | solution.py:397
  33.1 20.5 %collective-permute-start.9 = (f32[4,64,256]{2,1,0:T(8,128)S(1)}, f32[4,64,256]{2,1,0:T(8,128)}, u32[]{:S(2)}, u32[]{:S(2)}) collective-permute-start(f32[4,64,256]{2,1,0:T(8,128)S(1)} %collective-permute-done.7.refs_8_), channel_id=1, source_target_pairs={{0,16},{1,17},{2,18},{3,19},{4,20},{5,21},{6,22},{7,23},{8,9},{9,8... | collective-permute-start | bytes 786440 | tf_op jit(solution)/shard_map/ppermute | solution.py:397
  39.0 14.4 %collective-permute-start.12 = (f32[4,64,256]{2,1,0:T(8,128)S(1)}, f32[4,64,256]{2,1,0:T(8,128)S(1)}, u32[]{:S(2)}, u32[]{:S(2)}) collective-permute-start(f32[4,64,256]{2,1,0:T(8,128)S(1)} %collective-permute-done.11.refs_0_), channel_id=1, source_target_pairs={{0,1},{1,0},{2,3},{3,2},{4,5},{5,4},{6,7},{7,6},{8,24},{9,25},{10,... | collective-permute-start | bytes 786440 | tf_op jit(solution)/shard_map/ppermute | solution.py:397
  40.5 13.0 %collective-permute-start.6 = (f32[4,64,256]{2,1,0:T(8,128)S(1)}, f32[4,64,256]{2,1,0:T(8,128)}, u32[]{:S(2)}, u32[]{:S(2)}) collective-permute-start(f32[4,64,256]{2,1,0:T(8,128)S(1)} %collective-permute-done.4.refs_5_), channel_id=1, source_target_pairs={{0,16},{1,17},{2,18},{3,19},{4,20},{5,21},{6,22},{7,23},{8,9},{9,8... | collective-permute-start | bytes 786440 | tf_op jit(solution)/shard_map/ppermute | solution.py:397
  44.1 9.5 %collective-permute-start.10 = (f32[4,64,256]{2,1,0:T(8,128)S(1)}, f32[4,64,256]{2,1,0:T(8,128)}, u32[]{:S(2)}, u32[]{:S(2)}) collective-permute-start(f32[4,64,256]{2,1,0:T(8,128)S(1)} %collective-permute-done.8.refs_9_), channel_id=1, source_target_pairs={{0,16},{1,17},{2,18},{3,19},{4,20},{5,21},{6,22},{7,23},{8,9},{9,8... | collective-permute-start | bytes 786440 | tf_op jit(solution)/shard_map/ppermute | solution.py:397
  46.8 22.3 %all-to-all-start.1 = ((f32[16,64,128]{2,1,0:T(8,128)}), f32[16,64,128]{2,1,0:T(8,128)S(1)}, u32[]{:S(2)}, u32[]{:S(2)}) async-start(f32[16,64,128]{2,1,0:T(8,128)} %reorder.1.refs_12_), calls=%async_computation.1 | async-start | bytes 1048576 | tf_op jit(solution)/shard_map/all_to_all | solution.py:425
  51.5 9.1 %collective-permute-start.13 = (f32[4,64,256]{2,1,0:T(8,128)S(1)}, f32[4,64,256]{2,1,0:T(8,128)S(1)}, u32[]{:S(2)}, u32[]{:S(2)}) collective-permute-start(f32[4,64,256]{2,1,0:T(8,128)S(1)} %collective-permute-done.11.refs_0_), channel_id=1, source_target_pairs={{0,16},{1,17},{2,18},{3,19},{4,20},{5,21},{6,22},{7,23},{8,9},{9,8... | collective-permute-start | bytes 786440 | tf_op jit(solution)/shard_map/ppermute | solution.py:397
  53.5 10.6 %collective-permute-start.14 = (f32[4,64,256]{2,1,0:T(8,128)S(1)}, f32[4,64,256]{2,1,0:T(8,128)S(1)}, u32[]{:S(2)}, u32[]{:S(2)}) collective-permute-start(f32[4,64,256]{2,1,0:T(8,128)S(1)} %collective-permute-done.12.refs_1_), channel_id=1, source_target_pairs={{0,16},{1,17},{2,18},{3,19},{4,20},{5,21},{6,22},{7,23},{8,9},{9,8... | collective-permute-start | bytes 786440 | tf_op jit(solution)/shard_map/ppermute | solution.py:397
  68.5 6.7 %collective-permute-start.17 = (f32[6,256,256]{2,1,0:T(8,128)}, f32[6,256,256]{2,1,0:T(8,128)}, u32[]{:S(2)}, u32[]{:S(2)}) collective-permute-start(f32[6,256,256]{2,1,0:T(8,128)} %get-tuple-element.24.corner_own), channel_id=1, source_target_pairs={{0,8},{1,9},{2,10},{3,11},{4,12},{5,13},{6,14},{7,15},{8,0},{9,1},... | collective-permute-start | bytes 4718600 | tf_op jit(solution)/shard_map/ppermute | solution.py:397
  68.6 5.0 %collective-permute-start.16 = (f32[4,256,256]{2,1,0:T(8,128)}, f32[4,256,256]{2,1,0:T(8,128)S(1)}, u32[]{:S(2)}, u32[]{:S(2)}) collective-permute-start(f32[4,256,256]{2,1,0:T(8,128)} %get-tuple-element.23.diag_own), channel_id=1, source_target_pairs={{0,8},{1,9},{2,10},{3,11},{4,12},{5,13},{6,14},{7,15},{8,0},{9,1},... | collective-permute-start | bytes 3145736 | tf_op jit(solution)/shard_map/ppermute | solution.py:397
  69.0 0.8 copy-start.1
  73.2 2.0 %collective-permute-start.15 = (f32[128,1024]{1,0:T(8,128)S(1)}, f32[128,1024]{1,0:T(8,128)S(1)}, u32[]{:S(2)}, u32[]{:S(2)}) collective-permute-start(f32[128,1024]{1,0:T(8,128)S(1)} %project.1.own), channel_id=1, source_target_pairs={{0,8},{1,9},{2,10},{3,11},{4,12},{5,13},{6,14},{7,15},{8,0},{9,1},... | collective-permute-start | bytes 1572872 | tf_op jit(solution)/shard_map/ppermute | solution.py:397
  73.6 1.5 %copy-start.2 = (f32[4,256,256]{2,1,0:T(8,128)}, f32[4,256,256]{2,1,0:T(8,128)S(1)}, u32[]{:S(2)}) copy-start(f32[4,256,256]{2,1,0:T(8,128)S(1)} %collective-permute-done.16.diag_other) | copy-start | bytes 3145732
  81.9 8.4 %collective-permute-start.18 = (f32[8,64,128]{2,1,0:T(8,128)S(1)}, f32[8,64,128]{2,1,0:T(8,128)S(1)}, u32[]{:S(2)}, u32[]{:S(2)}) collective-permute-start(f32[8,64,128]{2,1,0:T(8,128)S(1)} %get-tuple-element.26), channel_id=1, source_target_pairs={{0,16},{1,17},{2,18},{3,19},{4,20},{5,21},{6,22},{7,23},{8,24},{9,... | collective-permute-start | bytes 786440 | tf_op jit(solution)/shard_map/ppermute | solution.py:397

commit v4 on v3

--- a/solution.py
+++ b/solution.py
@@ -106,6 +106,79 @@
     scratch = [pltpu.SMEM(owner_list.shape, jnp.int32), pltpu.SMEM(slot_list.shape, jnp.int32), pltpu.VMEM(spread.shape, F32)]
     return call(
         functools.partial(reorder_kernel, cols), "reorder", outs, (*pinned((owner_list, slot_list)), spread), far=3, copies=3, scratch=scratch
+    )[0]
+
+
+def share_kernel(vectors, *refs):
+    outs, sems = refs[:-1], refs[-1]
+    z = lax.axis_index("col") // 2
+    rows = outs[0].shape[0]
+    pairs = []
+    for at, out in enumerate(outs):
+        start = pl.multiple_of(jnp.bitwise_xor(z, at + 1) * rows, rows)
+        pairs.append((vectors.at[pl.ds(start, rows), :], out))
+    for copy in start_copies(pairs, sems):
+        copy.wait()
+
+
+def halves_of(vectors, received, odd_half):
+    col = lax.axis_index("col")
+    rows = received[0].shape[0] // 2
+    side = jnp.bitwise_xor(col % 2, odd_half) * rows
+    refs = [vectors.at[pl.ds(pl.multiple_of((col // 2) * 2 * rows + side, rows), rows), :]]
+    return refs + [ref.at[pl.ds(pl.multiple_of(side, rows), rows), :] for ref in received]
+
+
+def turn_kernel(vectors, *refs):
+    received, out, sems = refs[:-2], refs[-2], refs[-1]
+    for copy in start_copies([(half, out.at[at]) for at, half in enumerate(halves_of(vectors, received, 1))], sems):
+        copy.wait()
+
+
+def place_blocks(half, owner, slot, held, ordered):
+    def move(block, carry):
+        place = slot[block] * half + owner[block]
+        parity = block % BLK_DEV
+
+        @pl.when(parity == 0)
+        def _():
+            ordered[place] = held[block // BLK_DEV, :, :BW]
+
+        @pl.when(parity == 1)
+        def _():
+            ordered[place] = held[block // BLK_DEV, :, BW:]
+
+        return carry
+
+    lax.fori_loop(0, ordered.shape[0], move, 0)
+
+
+def gather_kernel(half, owner_list, slot_list, vectors, *refs):
+    received, (turned, ordered, owner, slot, held, sems) = refs[:-6], refs[-6:]
+    col = lax.axis_index("col")
+    z, y = col // 2, col % 2
+    pairs = [(owner_list, owner), (slot_list, slot)]
+    for at, part in enumerate(halves_of(vectors, received, 0)):
+        source = jnp.bitwise_xor(z, at) * 2
+        pairs += [(part, held.at[source + y]), (turned.at[at], held.at[source + 1 - y])]
+    for copy in start_copies(pairs, sems):
+        copy.wait()
+    place_blocks(half, owner, slot, held, ordered)
+
+
+def spread_by_steps(vectors, owner_list, slot_list, send, by_z, by_y, cols):
+    rows, width = vectors.shape
+    part, steps = rows // cols, cols // 2
+    sent = call(share_kernel, "share", [shape((2 * part, width))] * (steps - 1), pinned((vectors,)), far=1, copies=steps - 1)
+    received = [send(value, by_z(at + 1)) for at, value in enumerate(sent)]
+    turned = call(
+        turn_kernel, "turn", [shape((steps, part, width))], pinned((vectors, *received)), far=steps, copies=steps
+    )[0]
+    turned = send(turned, by_y)
+    scratch = [pltpu.SMEM(owner_list.shape, jnp.int32), pltpu.SMEM(slot_list.shape, jnp.int32), pltpu.VMEM((cols, part, width), F32)]
+    return call(
+        functools.partial(gather_kernel, cols), "gather", [shape((cols * BLK_DEV, part, BW))],
+        pinned((owner_list, slot_list, vectors, *received, turned)), far=steps + 3, copies=2 + 2 * steps, scratch=scratch,
     )[0]
 
 
@@ -414,13 +487,15 @@
         own = lax.all_gather(own, "col", axis=1, tiled=True, axis_index_groups=groups)
     start = [own, send(own, by_z(1)), send(own, by_z(2))]
     start.append(send(start[2], by_z(1)))
+    if extra == 1:
+        ordered = spread_by_steps(vectors, owner_list, slot_list, send, by_z, lambda r, c: (r, c ^ 1), cols)
+    else:
+        spread = lax.all_to_all(vectors.reshape(cols, local_rows, -1), "col", split_axis=0, concat_axis=0, tiled=True)
+        ordered = reorder(spread, owner_list, slot_list)
     first = [send(piece, by_first) for piece in start]
-    second = [send(piece, by_second) for piece in start]
+    second = [send(piece, by_second) for piece in [after(x, ordered) if k in (1, 2, 3) else x for k, x in enumerate(start)]]
     both = [send(piece, by_second) for piece in first]
 
-    vectors = after(vectors, start[1], start[2], first[0], second[0])
-    spread = lax.all_to_all(vectors.reshape(cols, local_rows, -1), "col", split_axis=0, concat_axis=0, tiled=True)
-    ordered = reorder(spread, owner_list, slot_list)
     groups = [[at(o * inner + i, c) for o in range(2) for c in range(cols)] for i in range(inner)]
     slab = lax.all_to_all(ordered, ("row", "col"), split_axis=0, concat_axis=0, tiled=True, axis_index_groups=groups)
     slab = slab.reshape(2, extra, LOW, local_rows, BW).transpose(0, 2, 1, 3, 4)
@@ -445,7 +520,7 @@
     half_held = [pltpu.VMEM((2 * CHUNKS * half_rows, full), BF16), pltpu.VMEM(slab.shape, F32)]
     away, wide = call(
         functools.partial(solve_kernel, inner, parts), "solve", [block, shape((full, 2 * BW), BF16)],
-        (product, over_inner(product, bits[-1]), *pinned((diag, diag_other, corner, over_inner(corner, bits[-1]))), *pinned((*arrays, slab))),
+        (product, over_inner(product, bits[-1]), *pinned((diag,)), diag_other, *pinned((corner,)), over_inner(corner, bits[-1]), *pinned((*arrays, slab))),
         far=len(arrays) + 5, copies=2 * panels + 2 * CHUNKS + 3,
         scratch=[pltpu.VMEM(diag.shape, F32)] * 2 + [pltpu.VMEM(corner.shape, F32)] * 2 + half_held, flops=8 * 10**9, mib=32,
     )

time: 91.5 us -> 89.7 us (0.980)
  waiting for transfers between devices: 34.4 us -> 25.5 us
  starting transfers between devices: 29.9 us -> 34.3 us
  Pallas kernels: 25.9 us -> 28.1 us
    ppermute x19 -> x23, waiting for transfers between devices: 34.4 us -> 25.5 us  [send(): return lax.ppermute(value, ('row', 'col'), perm)]
    ppermute x19 -> x23, starting transfers between devices: 21.3 us -> 27.4 us  [send(): return lax.ppermute(value, ('row', 'col'), perm)]
    all_to_all x1 -> x0, starting transfers between devices: 3.87 us -> none  [on_device(): lax.all_to_all(vectors.reshape(cols, local_rows, -1), 'col', split_axis=0...]
    all_to_all x1, starting transfers between devices: 4.68 us -> 6.91 us  [on_device(): lax.all_to_all(ordered, ('row', 'col'), split_axis=0, concat_axis=0, tile...]
    pallas_call x7 -> x9, Pallas kernels: 25.9 us -> 28.1 us  [call(): pl.pallas_call(body, out_shape=tuple(outs[:len(outs) - far_outs]) + tuple...]
  transfers between devices with their start and end apart: 21 -> 24, of which waited for: 11 -> 9; matrix products, arithmetic and copies ran while one was open for 0% -> 0% of each run, Pallas kernels for 20% -> 22%
where the time goes in v4:
time: 89.7 us; the launch traced here: 89.3 us
  starting transfers between devices  34.3 us (38%)
  Pallas kernels  28.1 us (31%)
  waiting for transfers between devices  25.5 us (28%)
  local copies, waits for them, and re-layouts  1.3 us (1%)
    pallas_call x9, Pallas kernels, call(): pl.pallas_call(body, out_shape=tuple(outs[:len(outs) - far_outs]) + tuple...  28.1 us
    ppermute x23, starting transfers between devices, send(): return lax.ppermute(value, ('row', 'col'), perm)  27.4 us
    ppermute x23, waiting for transfers between devices, send(): return lax.ppermute(value, ('row', 'col'), perm)  25.5 us
    all_to_all x1, starting transfers between devices, on_device(): lax.all_to_all(ordered, ('row', 'col'), split_axis=0, concat_axis=0, tile...  6.91 us
  transfers between devices with their start and end apart: 24, of which 9 were waited for; matrix products, arithmetic and copies ran while one was open for 0% of the time, Pallas kernels for 22%

profile of v4, /device:TPU:0, one launch (start us, length us, event | category | flops | bytes accessed | tf_op | source)
XLA Modules:
  0.0 89.3 jit_solution(4742968561251876827)
XLA Ops:
  0.0 1.1 %share.1 = (f32[128,256]{1,0:T(8,128)S(1)}, f32[128,256]{1,0:T(8,128)S(1)}, f32[128,256]{1,0:T(8,128)S(1)}) custom-call(f32[512,256]{1,0:T(8,128)} %vectors.5), custom_call_target="tpu_custom_call" | custom-call | bytes 4194304 | tf_op jit(solution)/shard_map/share/pallas_call | solution.py:32
  1.1 3.1 %collective-permute-start.5 = (f32[128,256]{1,0:T(8,128)S(1)}, f32[128,256]{1,0:T(8,128)S(1)}, u32[]{:S(2)}, u32[]{:S(2)}) collective-permute-start(f32[128,256]{1,0:T(8,128)S(1)} %get-tuple-element.21), channel_id=1, source_target_pairs={{0,2},{1,3},{2,0},{3,1},{4,6},{5,7},{6,4},{7,5},{8,10},{9,11},{10,... | collective-permute-start | bytes 393224 | tf_op jit(solution)/shard_map/ppermute | solution.py:470
  4.2 2.6 %collective-permute-start.6 = (f32[128,256]{1,0:T(8,128)S(1)}, f32[128,256]{1,0:T(8,128)S(1)}, u32[]{:S(2)}, u32[]{:S(2)}) collective-permute-start(f32[128,256]{1,0:T(8,128)S(1)} %get-tuple-element.22), channel_id=1, source_target_pairs={{0,4},{1,5},{2,6},{3,7},{4,0},{5,1},{6,2},{7,3},{8,12},{9,13},{10,... | collective-permute-start | bytes 393224 | tf_op jit(solution)/shard_map/ppermute | solution.py:470
  6.8 0.9 %collective-permute-start.3 = (f32[4,64,256]{2,1,0:T(8,128)}, f32[4,64,256]{2,1,0:T(8,128)S(1)}, u32[]{:S(2)}, u32[]{:S(2)}) collective-permute-start(f32[4,64,256]{2,1,0:T(8,128)} %refs_0_.1), channel_id=1, source_target_pairs={{0,2},{1,3},{2,0},{3,1},{4,6},{5,7},{6,4},{7,5},{8,10},{9,11},{10,... | collective-permute-start | bytes 786440 | tf_op jit(solution)/shard_map/ppermute | solution.py:470
  7.7 1.5 %collective-permute-start = (f32[4,64,256]{2,1,0:T(8,128)}, f32[4,64,256]{2,1,0:T(8,128)S(1)}, u32[]{:S(2)}, u32[]{:S(2)}) collective-permute-start(f32[4,64,256]{2,1,0:T(8,128)} %refs_0_.1), channel_id=1, source_target_pairs={{0,1},{1,0},{2,3},{3,2},{4,5},{5,4},{6,7},{7,6},{8,24},{9,25},{10,... | collective-permute-start | bytes 786440 | tf_op jit(solution)/shard_map/ppermute | solution.py:470
  9.5 3.2 %collective-permute-start.11 = (f32[4,64,256]{2,1,0:T(8,128)}, f32[4,64,256]{2,1,0:T(8,128)S(1)}, u32[]{:S(2)}, u32[]{:S(2)}) collective-permute-start(f32[4,64,256]{2,1,0:T(8,128)} %refs_0_.1), channel_id=1, source_target_pairs={{0,4},{1,5},{2,6},{3,7},{4,0},{5,1},{6,2},{7,3},{8,12},{9,13},{10,... | collective-permute-start | bytes 786440 | tf_op jit(solution)/shard_map/ppermute | solution.py:470
  12.7 4.4 %collective-permute-done.6.refs_1_ = f32[128,256]{1,0:T(8,128)S(1)} collective-permute-done((f32[128,256]{1,0:T(8,128)S(1)}, f32[128,256]{1,0:T(8,128)S(1)}, u32[]{:S(2)}, u32[]{:S(2)}) %collective-permute-start.6) | collective-permute-done | bytes 131104 | tf_op jit(solution)/shard_map/ppermute | solution.py:470
  17.8 0.6 copy-done.3
  18.4 1.0 %turn.1 = f32[4,64,256]{2,1,0:T(8,128)S(1)} custom-call(f32[512,256]{1,0:T(8,128)} %vectors.5, f32[128,256]{1,0:T(8,128)} %copy-done.1, f32[128,256]{1,0:T(8,128)} %copy-done.2, f32[128,256]{1,0:T(8,128)} %copy-done.3), custom_call_target="tpu_custom_call" | custom-call | bytes 4194304 | tf_op jit(solution)/shard_map/turn/pallas_call | solution.py:32
  19.4 1.6 %collective-permute-start.8 = (f32[4,64,256]{2,1,0:T(8,128)S(1)}, f32[4,64,256]{2,1,0:T(8,128)S(1)}, u32[]{:S(2)}, u32[]{:S(2)}) collective-permute-start(f32[4,64,256]{2,1,0:T(8,128)S(1)} %turn.1), channel_id=1, source_target_pairs={{0,1},{1,0},{2,3},{3,2},{4,5},{5,4},{6,7},{7,6},{8,9},{9,8},{10,11... | collective-permute-start | bytes 786440 | tf_op jit(solution)/shard_map/ppermute | solution.py:470
  21.0 1.5 %collective-permute-start.1 = (f32[4,64,256]{2,1,0:T(8,128)S(1)}, f32[4,64,256]{2,1,0:T(8,128)S(1)}, u32[]{:S(2)}, u32[]{:S(2)}) collective-permute-start(f32[4,64,256]{2,1,0:T(8,128)S(1)} %copy-done), channel_id=1, source_target_pairs={{0,16},{1,17},{2,18},{3,19},{4,20},{5,21},{6,22},{7,23},{8,9},{9,8... | collective-permute-start | bytes 786440 | tf_op jit(solution)/shard_map/ppermute | solution.py:470
  23.0 6.8 %collective-permute-done.11.refs_8_ = f32[4,64,256]{2,1,0:T(8,128)S(1)} collective-permute-done((f32[4,64,256]{2,1,0:T(8,128)}, f32[4,64,256]{2,1,0:T(8,128)S(1)}, u32[]{:S(2)}, u32[]{:S(2)}) %collective-permute-start.11) | collective-permute-done | bytes 262176 | tf_op jit(solution)/shard_map/ppermute | solution.py:470
  29.8 1.5 %collective-permute-start.2 = (f32[4,64,256]{2,1,0:T(8,128)S(1)}, f32[4,64,256]{2,1,0:T(8,128)S(1)}, u32[]{:S(2)}, u32[]{:S(2)}) collective-permute-start(f32[4,64,256]{2,1,0:T(8,128)S(1)} %collective-permute-done.refs_1_), channel_id=1, source_target_pairs={{0,16},{1,17},{2,18},{3,19},{4,20},{5,21},{6,22},{7,23},{8,9},{9,8... | collective-permute-start | bytes 786440 | tf_op jit(solution)/shard_map/ppermute | solution.py:470
  31.3 1.5 %collective-permute-start.12 = (f32[4,64,256]{2,1,0:T(8,128)S(1)}, f32[4,64,256]{2,1,0:T(8,128)S(1)}, u32[]{:S(2)}, u32[]{:S(2)}) collective-permute-start(f32[4,64,256]{2,1,0:T(8,128)S(1)} %collective-permute-done.11.refs_8_), channel_id=1, source_target_pairs={{0,1},{1,0},{2,3},{3,2},{4,5},{5,4},{6,7},{7,6},{8,24},{9,25},{10,... | collective-permute-start | bytes 786440 | tf_op jit(solution)/shard_map/ppermute | solution.py:470
  32.8 2.3 %gather.1.refs_12_ = f32[16,64,128]{2,1,0:T(8,128)} custom-call(s32[16]{0:T(128)} %owner_list.1, s32[16]{0:T(128)} %slot_list.1, f32[512,256]{1,0:T(8,128)} %vectors.5, f32[128,256]{1,0:T(8,128)} %copy-done.1, f32[128,256]{1,0:T(8,128)} %copy-done.2, f32[128,256]{1,0:T(8,128)} %copy-done.3, f32[4,64,256]{2,1,0:T(8,128)} %copy-done.4), custom_call_target="tpu_custom_call" | custom-call | bytes 4194304 | tf_op jit(solution)/shard_map/gather/pallas_call | solution.py:32
  35.7 1.5 %collective-permute-start.13 = (f32[4,64,256]{2,1,0:T(8,128)S(1)}, f32[4,64,256]{2,1,0:T(8,128)S(1)}, u32[]{:S(2)}, u32[]{:S(2)}) collective-permute-start(f32[4,64,256]{2,1,0:T(8,128)S(1)} %collective-permute-done.11.refs_8_), channel_id=1, source_target_pairs={{0,16},{1,17},{2,18},{3,19},{4,20},{5,21},{6,22},{7,23},{8,9},{9,8... | collective-permute-start | bytes 786440 | tf_op jit(solution)/shard_map/ppermute | solution.py:470
  37.2 1.0 %collective-permute-start.16 = (f32[4,64,256]{2,1,0:T(8,128)S(1)}, f32[4,64,256]{2,1,0:T(8,128)S(1)}, u32[]{:S(2)}, u32[]{:S(2)}) collective-permute-start(f32[4,64,256]{2,1,0:T(8,128)S(1)} %collective-permute-done.15.refs_0_), channel_id=1, source_target_pairs={{0,1},{1,0},{2,3},{3,2},{4,5},{5,4},{6,7},{7,6},{8,24},{9,25},{10,... | collective-permute-start | bytes 786440 | tf_op jit(solution)/shard_map/ppermute | solution.py:470
  38.4 1.8 %collective-permute-start.10 = (f32[4,64,256]{2,1,0:T(8,128)S(1)}, f32[4,64,256]{2,1,0:T(8,128)S(1)}, u32[]{:S(2)}, u32[]{:S(2)}) collective-permute-start(f32[4,64,256]{2,1,0:T(8,128)S(1)} %collective-permute-done.4.refs_5_), channel_id=1, source_target_pairs={{0,16},{1,17},{2,18},{3,19},{4,20},{5,21},{6,22},{7,23},{8,9},{9,8... | collective-permute-start | bytes 786440 | tf_op jit(solution)/shard_map/ppermute | solution.py:470
  40.5 6.9 %all-to-all-start = ((f32[16,64,128]{2,1,0:T(8,128)}), f32[16,64,128]{2,1,0:T(8,128)}, u32[]{:S(2)}, u32[]{:S(2)}) async-start(f32[16,64,128]{2,1,0:T(8,128)} %gather.1.refs_12_), calls=%async_computation | async-start | bytes 1048576 | tf_op jit(solution)/shard_map/all_to_all | solution.py:500
  47.4 1.9 %collective-permute-start.17 = (f32[4,64,256]{2,1,0:T(8,128)S(1)}, f32[4,64,256]{2,1,0:T(8,128)S(1)}, u32[]{:S(2)}, u32[]{:S(2)}) collective-permute-start(f32[4,64,256]{2,1,0:T(8,128)S(1)} %collective-permute-done.15.refs_0_), channel_id=1, source_target_pairs={{0,16},{1,17},{2,18},{3,19},{4,20},{5,21},{6,22},{7,23},{8,9},{9,8... | collective-permute-start | bytes 786440 | tf_op jit(solution)/shard_map/ppermute | solution.py:470
  49.5 2.1 %collective-permute-done.10.refs_7_ = f32[4,64,256]{2,1,0:T(8,128)S(1)} collective-permute-done((f32[4,64,256]{2,1,0:T(8,128)S(1)}, f32[4,64,256]{2,1,0:T(8,128)S(1)}, u32[]{:S(2)}, u32[]{:S(2)}) %collective-permute-start.10) | collective-permute-done | bytes 262176 | tf_op jit(solution)/shard_map/ppermute | solution.py:470
  51.6 4.7 %collective-permute-done.14.refs_11_ = f32[4,64,256]{2,1,0:T(8,128)} collective-permute-done((f32[4,64,256]{2,1,0:T(8,128)S(1)}, f32[4,64,256]{2,1,0:T(8,128)}, u32[]{:S(2)}, u32[]{:S(2)}) %collective-permute-start.14) | collective-permute-done | bytes 262176 | tf_op jit(solution)/shard_map/ppermute | solution.py:470
  56.3 5.5 %gram.2 = (f32[4,256,256]{2,1,0:T(8,128)}, f32[6,256,256]{2,1,0:T(8,128)}, bf16[768,1024]{1,0:T(8,128)(2,1)}, bf16[768,1024]{1,0:T(8,128)(2,1)}) custom-call(f32[4,64,256]{2,1,0:T(8,128)S(1)} %copy-done, f32[4,64,256]{2,1,0:T(8,128)S(1)} %collective-permute-done.refs_1_, f32[4,64,256]{2,1,0:T(8,128)S(1)} %collective-permute-done.1.refs_2_, ...), custom_call_target="tpu_custom_call" | custom-call | flops 3019898880 | bytes 4194304 | tf_op jit(solution)/shard_map/gram/pallas_call | solution.py:32
  61.8 1.4 %collective-permute-done.18.refs_3_ = f32[4,64,256]{2,1,0:T(8,128)S(1)} collective-permute-done((f32[4,64,256]{2,1,0:T(8,128)S(1)}, f32[4,64,256]{2,1,0:T(8,128)S(1)}, u32[]{:S(2)}, u32[]{:S(2)}) %collective-permute-start.18) | collective-permute-done | bytes 262176 | tf_op jit(solution)/shard_map/ppermute | solution.py:470
  63.2 4.4 %gram.3 = (f32[4,256,256]{2,1,0:T(8,128)}, f32[6,256,256]{2,1,0:T(8,128)}, bf16[256,1024]{1,0:T(8,128)(2,1)}, bf16[256,1024]{1,0:T(8,128)(2,1)}) custom-call(f32[4,64,256]{2,1,0:T(8,128)S(1)} %collective-permute-done.15.refs_0_, f32[4,64,256]{2,1,0:T(8,128)S(1)} %collective-permute-done.16.refs_1_, f32[4,64,256]{2,1,0:T(8,128)S(1)} %collective-permute-done.17.refs_2_, ...), custom_call_target="tpu_custom_call" | custom-call | flops 1006632960 | bytes 4194304 | tf_op jit(solution)/shard_map/gram/pallas_call | solution.py:32
  68.2 3.4 %project.1.own = f32[128,1024]{1,0:T(8,128)S(1)} custom-call(bf16[768,1024]{1,0:T(8,128)(2,1)} %get-tuple-element.26.refs_0_, bf16[768,1024]{1,0:T(8,128)(2,1)} %get-tuple-element.27.refs_1_, bf16[256,1024]{1,0:T(8,128)(2,1)} %get-tuple-element.31.refs_2_, bf16[256,1024]{1,0:T(8,128)(2,1)} %get-tuple-element.32.refs_3_, f32[16,64,128]{2,1,0:T(8,128)} %all-to-all-done.refs_4_), custom_call_target="tpu_custom_call" | custom-call | flops 805306368 | bytes 4194304 | tf_op jit(solution)/shard_map/project/pallas_call | solution.py:32
  71.7 1.8 %collective-permute-done.19.other = f32[128,1024]{1,0:T(8,128)S(1)} collective-permute-done((f32[128,1024]{1,0:T(8,128)S(1)}, f32[128,1024]{1,0:T(8,128)S(1)}, u32[]{:S(2)}, u32[]{:S(2)}) %collective-permute-start.19) | collective-permute-done | bytes 524320 | tf_op jit(solution)/shard_map/ppermute | solution.py:470
  73.5 6.6 %solve.1 = (f32[8,64,128]{2,1,0:T(8,128)S(1)}, bf16[1024,256]{1,0:T(8,128)(2,1)S(1)}) custom-call(f32[128,1024]{1,0:T(8,128)S(1)} %project.1.own, f32[128,1024]{1,0:T(8,128)S(1)} %collective-permute-done.19.other, f32[4,256,256]{2,1,0:T(8,128)} %get-tuple-element.33.diag_own, f32[4,256,256]{2,1,0:T(8,128)S(1)} %collective-permute-done.20.diag_other, ...), custom_call_target="tpu_custom_call" | custom-call | flops 8000000000 | bytes 4194304 | tf_op jit(solution)/shard_map/solve/pallas_call | solution.py:32
  80.1 1.6 %collective-permute-start.22 = (f32[8,64,128]{2,1,0:T(8,128)S(1)}, f32[8,64,128]{2,1,0:T(8,128)S(1)}, u32[]{:S(2)}, u32[]{:S(2)}) collective-permute-start(f32[8,64,128]{2,1,0:T(8,128)S(1)} %get-tuple-element.36), channel_id=1, source_target_pairs={{0,16},{1,17},{2,18},{3,19},{4,20},{5,21},{6,22},{7,23},{8,24},{9,... | collective-permute-start | bytes 786440 | tf_op jit(solution)/shard_map/ppermute | solution.py:470
  81.6 3.2 %keep.1.begun = f32[512,256]{1,0:T(8,128)} custom-call(bf16[1024,256]{1,0:T(8,128)(2,1)S(1)} %get-tuple-element.35.wide, bf16[768,1024]{1,0:T(8,128)(2,1)} %get-tuple-element.26.refs_0_, bf16[768,1024]{1,0:T(8,128)(2,1)} %get-tuple-element.27.refs_1_, bf16[256,1024]{1,0:T(8,128)(2,1)} %get-tuple-element.31.refs_2_, ...), custom_call_target="tpu_custom_call" | custom-call | flops 1000000000 | bytes 4194304 | tf_op jit(solution)/shard_map/keep/pallas_call | solution.py:32
  84.9 3.6 %collective-permute-done.22.back = f32[8,64,128]{2,1,0:T(8,128)S(1)} collective-permute-done((f32[8,64,128]{2,1,0:T(8,128)S(1)}, f32[8,64,128]{2,1,0:T(8,128)S(1)}, u32[]{:S(2)}, u32[]{:S(2)}) %collective-permute-start.22) | collective-permute-done | bytes 262176 | tf_op jit(solution)/shard_map/ppermute | solution.py:470
  88.5 0.8 place.1
  (35 shorter events, 3.4 us)
Async XLA Ops:
  0.0 21.0 %copy-start = (f32[4,64,256]{2,1,0:T(8,128)S(1)}, f32[4,64,256]{2,1,0:T(8,128)}, u32[]{:S(2)}) copy-start(f32[4,64,256]{2,1,0:T(8,128)} %refs_0_.1) | copy-start | bytes 786436
  1.1 8.4 %collective-permute-start.5 = (f32[128,256]{1,0:T(8,128)S(1)}, f32[128,256]{1,0:T(8,128)S(1)}, u32[]{:S(2)}, u32[]{:S(2)}) collective-permute-start(f32[128,256]{1,0:T(8,128)S(1)} %get-tuple-element.21), channel_id=1, source_target_pairs={{0,2},{1,3},{2,0},{3,1},{4,6},{5,7},{6,4},{7,5},{8,10},{9,11},{10,... | collective-permute-start | bytes 393224 | tf_op jit(solution)/shard_map/ppermute | solution.py:470
  4.2 12.9 %collective-permute-start.6 = (f32[128,256]{1,0:T(8,128)S(1)}, f32[128,256]{1,0:T(8,128)S(1)}, u32[]{:S(2)}, u32[]{:S(2)}) collective-permute-start(f32[128,256]{1,0:T(8,128)S(1)} %get-tuple-element.22), channel_id=1, source_target_pairs={{0,4},{1,5},{2,6},{3,7},{4,0},{5,1},{6,2},{7,3},{8,12},{9,13},{10,... | collective-permute-start | bytes 393224 | tf_op jit(solution)/shard_map/ppermute | solution.py:470
  6.8 10.4 %collective-permute-start.7 = (f32[128,256]{1,0:T(8,128)S(1)}, f32[128,256]{1,0:T(8,128)S(1)}, u32[]{:S(2)}, u32[]{:S(2)}) collective-permute-start(f32[128,256]{1,0:T(8,128)S(1)} %get-tuple-element.23), channel_id=1, source_target_pairs={{0,6},{1,7},{2,4},{3,5},{4,2},{5,3},{6,0},{7,1},{8,14},{9,15},{10,... | collective-permute-start | bytes 393224 | tf_op jit(solution)/shard_map/ppermute | solution.py:470
  6.8 15.7 %collective-permute-start.3 = (f32[4,64,256]{2,1,0:T(8,128)}, f32[4,64,256]{2,1,0:T(8,128)S(1)}, u32[]{:S(2)}, u32[]{:S(2)}) collective-permute-start(f32[4,64,256]{2,1,0:T(8,128)} %refs_0_.1), channel_id=1, source_target_pairs={{0,2},{1,3},{2,0},{3,1},{4,6},{5,7},{6,4},{7,5},{8,10},{9,11},{10,... | collective-permute-start | bytes 786440 | tf_op jit(solution)/shard_map/ppermute | solution.py:470
  7.7 22.1 %collective-permute-start = (f32[4,64,256]{2,1,0:T(8,128)}, f32[4,64,256]{2,1,0:T(8,128)S(1)}, u32[]{:S(2)}, u32[]{:S(2)}) collective-permute-start(f32[4,64,256]{2,1,0:T(8,128)} %refs_0_.1), channel_id=1, source_target_pairs={{0,1},{1,0},{2,3},{3,2},{4,5},{5,4},{6,7},{7,6},{8,24},{9,25},{10,... | collective-permute-start | bytes 786440 | tf_op jit(solution)/shard_map/ppermute | solution.py:470
  9.5 7.6 %copy-start.1 = (f32[128,256]{1,0:T(8,128)}, f32[128,256]{1,0:T(8,128)S(1)}, u32[]{:S(2)}) copy-start(f32[128,256]{1,0:T(8,128)S(1)} %collective-permute-done.5.refs_0_) | copy-start | bytes 393220
  9.5 20.3 %collective-permute-start.11 = (f32[4,64,256]{2,1,0:T(8,128)}, f32[4,64,256]{2,1,0:T(8,128)S(1)}, u32[]{:S(2)}, u32[]{:S(2)}) collective-permute-start(f32[4,64,256]{2,1,0:T(8,128)} %refs_0_.1), channel_id=1, source_target_pairs={{0,4},{1,5},{2,6},{3,7},{4,0},{5,1},{6,2},{7,3},{8,12},{9,13},{10,... | collective-permute-start | bytes 786440 | tf_op jit(solution)/shard_map/ppermute | solution.py:470
  17.1 0.7 copy-start.2
  17.8 0.6 copy-start.3
  19.4 11.8 %collective-permute-start.8 = (f32[4,64,256]{2,1,0:T(8,128)S(1)}, f32[4,64,256]{2,1,0:T(8,128)S(1)}, u32[]{:S(2)}, u32[]{:S(2)}) collective-permute-start(f32[4,64,256]{2,1,0:T(8,128)S(1)} %turn.1), channel_id=1, source_target_pairs={{0,1},{1,0},{2,3},{3,2},{4,5},{5,4},{6,7},{7,6},{8,9},{9,8},{10,11... | collective-permute-start | bytes 786440 | tf_op jit(solution)/shard_map/ppermute | solution.py:470
  21.0 14.1 %collective-permute-start.1 = (f32[4,64,256]{2,1,0:T(8,128)S(1)}, f32[4,64,256]{2,1,0:T(8,128)S(1)}, u32[]{:S(2)}, u32[]{:S(2)}) collective-permute-start(f32[4,64,256]{2,1,0:T(8,128)S(1)} %copy-done), channel_id=1, source_target_pairs={{0,16},{1,17},{2,18},{3,19},{4,20},{5,21},{6,22},{7,23},{8,9},{9,8... | collective-permute-start | bytes 786440 | tf_op jit(solution)/shard_map/ppermute | solution.py:470
  22.5 13.2 %collective-permute-start.4 = (f32[4,64,256]{2,1,0:T(8,128)S(1)}, f32[4,64,256]{2,1,0:T(8,128)S(1)}, u32[]{:S(2)}, u32[]{:S(2)}) collective-permute-start(f32[4,64,256]{2,1,0:T(8,128)S(1)} %collective-permute-done.3.refs_4_), channel_id=1, source_target_pairs={{0,1},{1,0},{2,3},{3,2},{4,5},{5,4},{6,7},{7,6},{8,24},{9,25},{10,... | collective-permute-start | bytes 786440 | tf_op jit(solution)/shard_map/ppermute | solution.py:470
  29.8 7.4 %collective-permute-start.15 = (f32[4,64,256]{2,1,0:T(8,128)S(1)}, f32[4,64,256]{2,1,0:T(8,128)S(1)}, u32[]{:S(2)}, u32[]{:S(2)}) collective-permute-start(f32[4,64,256]{2,1,0:T(8,128)S(1)} %collective-permute-done.11.refs_8_), channel_id=1, source_target_pairs={{0,2},{1,3},{2,0},{3,1},{4,6},{5,7},{6,4},{7,5},{8,10},{9,11},{10,... | collective-permute-start | bytes 786440 | tf_op jit(solution)/shard_map/ppermute | solution.py:470
  29.8 8.7 %collective-permute-start.2 = (f32[4,64,256]{2,1,0:T(8,128)S(1)}, f32[4,64,256]{2,1,0:T(8,128)S(1)}, u32[]{:S(2)}, u32[]{:S(2)}) collective-permute-start(f32[4,64,256]{2,1,0:T(8,128)S(1)} %collective-permute-done.refs_1_), channel_id=1, source_target_pairs={{0,16},{1,17},{2,18},{3,19},{4,20},{5,21},{6,22},{7,23},{8,9},{9,8... | collective-permute-start | bytes 786440 | tf_op jit(solution)/shard_map/ppermute | solution.py:470
  31.3 1.5 %copy-start.4 = (f32[4,64,256]{2,1,0:T(8,128)}, f32[4,64,256]{2,1,0:T(8,128)S(1)}, u32[]{:S(2)}) copy-start(f32[4,64,256]{2,1,0:T(8,128)S(1)} %collective-permute-done.8.refs_3_) | copy-start | bytes 786436
  31.3 9.0 %collective-permute-start.12 = (f32[4,64,256]{2,1,0:T(8,128)S(1)}, f32[4,64,256]{2,1,0:T(8,128)S(1)}, u32[]{:S(2)}, u32[]{:S(2)}) collective-permute-start(f32[4,64,256]{2,1,0:T(8,128)S(1)} %collective-permute-done.11.refs_8_), channel_id=1, source_target_pairs={{0,1},{1,0},{2,3},{3,2},{4,5},{5,4},{6,7},{7,6},{8,24},{9,25},{10,... | collective-permute-start | bytes 786440 | tf_op jit(solution)/shard_map/ppermute | solution.py:470
  35.1 12.3 %collective-permute-start.9 = (f32[4,64,256]{2,1,0:T(8,128)S(1)}, f32[4,64,256]{2,1,0:T(8,128)S(1)}, u32[]{:S(2)}, u32[]{:S(2)}) collective-permute-start(f32[4,64,256]{2,1,0:T(8,128)S(1)} %collective-permute-done.3.refs_4_), channel_id=1, source_target_pairs={{0,16},{1,17},{2,18},{3,19},{4,20},{5,21},{6,22},{7,23},{8,9},{9,8... | collective-permute-start | bytes 786440 | tf_op jit(solution)/shard_map/ppermute | solution.py:470
  35.7 13.8 %collective-permute-start.13 = (f32[4,64,256]{2,1,0:T(8,128)S(1)}, f32[4,64,256]{2,1,0:T(8,128)S(1)}, u32[]{:S(2)}, u32[]{:S(2)}) collective-permute-start(f32[4,64,256]{2,1,0:T(8,128)S(1)} %collective-permute-done.11.refs_8_), channel_id=1, source_target_pairs={{0,16},{1,17},{2,18},{3,19},{4,20},{5,21},{6,22},{7,23},{8,9},{9,8... | collective-permute-start | bytes 786440 | tf_op jit(solution)/shard_map/ppermute | solution.py:470
  37.2 12.1 %collective-permute-start.16 = (f32[4,64,256]{2,1,0:T(8,128)S(1)}, f32[4,64,256]{2,1,0:T(8,128)S(1)}, u32[]{:S(2)}, u32[]{:S(2)}) collective-permute-start(f32[4,64,256]{2,1,0:T(8,128)S(1)} %collective-permute-done.15.refs_0_), channel_id=1, source_target_pairs={{0,1},{1,0},{2,3},{3,2},{4,5},{5,4},{6,7},{7,6},{8,24},{9,25},{10,... | collective-permute-start | bytes 786440 | tf_op jit(solution)/shard_map/ppermute | solution.py:470
  38.4 13.2 %collective-permute-start.10 = (f32[4,64,256]{2,1,0:T(8,128)S(1)}, f32[4,64,256]{2,1,0:T(8,128)S(1)}, u32[]{:S(2)}, u32[]{:S(2)}) collective-permute-start(f32[4,64,256]{2,1,0:T(8,128)S(1)} %collective-permute-done.4.refs_5_), channel_id=1, source_target_pairs={{0,16},{1,17},{2,18},{3,19},{4,20},{5,21},{6,22},{7,23},{8,9},{9,8... | collective-permute-start | bytes 786440 | tf_op jit(solution)/shard_map/ppermute | solution.py:470
  40.2 16.0 %collective-permute-start.14 = (f32[4,64,256]{2,1,0:T(8,128)S(1)}, f32[4,64,256]{2,1,0:T(8,128)}, u32[]{:S(2)}, u32[]{:S(2)}) collective-permute-start(f32[4,64,256]{2,1,0:T(8,128)S(1)} %collective-permute-done.12.refs_9_), channel_id=1, source_target_pairs={{0,16},{1,17},{2,18},{3,19},{4,20},{5,21},{6,22},{7,23},{8,9},{9,8... | collective-permute-start | bytes 786440 | tf_op jit(solution)/shard_map/ppermute | solution.py:470
  40.5 27.7 %all-to-all-start = ((f32[16,64,128]{2,1,0:T(8,128)}), f32[16,64,128]{2,1,0:T(8,128)}, u32[]{:S(2)}, u32[]{:S(2)}) async-start(f32[16,64,128]{2,1,0:T(8,128)} %gather.1.refs_12_), calls=%async_computation | async-start | bytes 1048576 | tf_op jit(solution)/shard_map/all_to_all | solution.py:500
  47.4 14.4 %collective-permute-start.17 = (f32[4,64,256]{2,1,0:T(8,128)S(1)}, f32[4,64,256]{2,1,0:T(8,128)S(1)}, u32[]{:S(2)}, u32[]{:S(2)}) collective-permute-start(f32[4,64,256]{2,1,0:T(8,128)S(1)} %collective-permute-done.15.refs_0_), channel_id=1, source_target_pairs={{0,16},{1,17},{2,18},{3,19},{4,20},{5,21},{6,22},{7,23},{8,9},{9,8... | collective-permute-start | bytes 786440 | tf_op jit(solution)/shard_map/ppermute | solution.py:470
  49.3 13.9 %collective-permute-start.18 = (f32[4,64,256]{2,1,0:T(8,128)S(1)}, f32[4,64,256]{2,1,0:T(8,128)S(1)}, u32[]{:S(2)}, u32[]{:S(2)}) collective-permute-start(f32[4,64,256]{2,1,0:T(8,128)S(1)} %collective-permute-done.16.refs_1_), channel_id=1, source_target_pairs={{0,16},{1,17},{2,18},{3,19},{4,20},{5,21},{6,22},{7,23},{8,9},{9,8... | collective-permute-start | bytes 786440 | tf_op jit(solution)/shard_map/ppermute | solution.py:470
  67.6 5.9 %collective-permute-start.21 = (f32[6,256,256]{2,1,0:T(8,128)}, f32[6,256,256]{2,1,0:T(8,128)S(1)}, u32[]{:S(2)}, u32[]{:S(2)}) collective-permute-start(f32[6,256,256]{2,1,0:T(8,128)} %get-tuple-element.34.corner_own), channel_id=1, source_target_pairs={{0,8},{1,9},{2,10},{3,11},{4,12},{5,13},{6,14},{7,15},{8,0},{9,1},... | collective-permute-start | bytes 4718600 | tf_op jit(solution)/shard_map/ppermute | solution.py:470
  67.7 5.8 %collective-permute-start.20 = (f32[4,256,256]{2,1,0:T(8,128)}, f32[4,256,256]{2,1,0:T(8,128)S(1)}, u32[]{:S(2)}, u32[]{:S(2)}) collective-permute-start(f32[4,256,256]{2,1,0:T(8,128)} %get-tuple-element.33.diag_own), channel_id=1, source_target_pairs={{0,8},{1,9},{2,10},{3,11},{4,12},{5,13},{6,14},{7,15},{8,0},{9,1},... | collective-permute-start | bytes 3145736 | tf_op jit(solution)/shard_map/ppermute | solution.py:470
  71.5 2.0 %collective-permute-start.19 = (f32[128,1024]{1,0:T(8,128)S(1)}, f32[128,1024]{1,0:T(8,128)S(1)}, u32[]{:S(2)}, u32[]{:S(2)}) collective-permute-start(f32[128,1024]{1,0:T(8,128)S(1)} %project.1.own), channel_id=1, source_target_pairs={{0,8},{1,9},{2,10},{3,11},{4,12},{5,13},{6,14},{7,15},{8,0},{9,1},... | collective-permute-start | bytes 1572872 | tf_op jit(solution)/shard_map/ppermute | solution.py:470
  80.1 8.4 %collective-permute-start.22 = (f32[8,64,128]{2,1,0:T(8,128)S(1)}, f32[8,64,128]{2,1,0:T(8,128)S(1)}, u32[]{:S(2)}, u32[]{:S(2)}) collective-permute-start(f32[8,64,128]{2,1,0:T(8,128)S(1)} %get-tuple-element.36), channel_id=1, source_target_pairs={{0,16},{1,17},{2,18},{3,19},{4,20},{5,21},{6,22},{7,23},{8,24},{9,... | collective-permute-start | bytes 786440 | tf_op jit(solution)/shard_map/ppermute | solution.py:470
